TPU v7x, 32 devices: a whole 2x2x4 slice. The times are simulated.
32 devices in a mesh: tm: 8 (over y, x, core), tensor: 4 (over z).
Axes of the slice: x: 2, y: 2, z: 4, core: 2. Of those that a mesh axis runs over, the one named last changes fastest.
Arguments:
- inputs: bfloat16 [131072, 1536], P('tm', 'tensor'), may hold values from -6 to 6
- kernel: bfloat16 [131072, 1536], P('tm', 'tensor'), may hold values from -5 to 5
- w_in: bfloat16 [12, 128, 128], P('tensor'), may hold values from -0.5 to 0.5
- w_gate: bfloat16 [12, 128, 128], P('tensor'), may hold values from -0.5 to 0.5
- w_out: bfloat16 [12, 128, 128], P('tensor'), may hold values from -0.5 to 0.5
- factor_a: bfloat16 [512, 512], replicated, may hold values from -0.25 to 0.25
- factor_b: bfloat16 [256, 256], replicated, may hold values from -0.375 to 0.375
- cotangent: bfloat16 [131072, 1536], P('tm', 'tensor'), may hold values from -6 to 6
Outputs:
- outputs: bfloat16 [131072, 1536], P('tm', 'tensor')
- grad_inputs: bfloat16 [131072, 1536], P('tm', 'tensor')
- grad_kernel: bfloat16 [131072, 1536], P('tm', 'tensor')
- grad_w_in: float32 [12, 128, 128], P('tensor')
- grad_w_gate: float32 [12, 128, 128], P('tensor')
- grad_w_out: float32 [12, 128, 128], P('tensor')
- grad_factor_a: float32 [512, 512], P('tm')
- grad_factor_b: float32 [256, 256], P('tm')
All inputs are finite; a program needn't handle non-finite values.
Results may differ from a plain program's by a relative error of at most 0.0071.
Values may be sent and summed in bfloat16 or wider, within the bound.
No kernel may reach another device: no remote copies, remote signals or barrier semaphores. Data moves between devices by JAX's collectives and lax.ppermute only.
A program may use at most 320 MiB of HBM per device.

v0:
```python
import math

import jax
import jax.numpy as jnp
from jax import lax
from jax.sharding import PartitionSpec as P

D = 1536
N1 = 256
N2 = 512


def mix(act, weight):
    width = weight.shape[1]
    blocks = act.reshape(act.shape[0], weight.shape[0], width)
    out = jnp.einsum("tnb,nbe->tne", blocks, weight, preferred_element_type=jnp.float32)
    return out.reshape(act.shape[0], act.shape[1])


def mix_back(grad, weight):
    width = weight.shape[1]
    blocks = grad.reshape(grad.shape[0], weight.shape[0], width)
    out = jnp.einsum("tne,nbe->tnb", blocks, weight, preferred_element_type=jnp.float32)
    return out.reshape(grad.shape[0], grad.shape[1])


def mix_grad(act, grad, weight):
    width = weight.shape[1]
    left = act.reshape(act.shape[0], weight.shape[0], width)
    right = grad.reshape(grad.shape[0], weight.shape[0], width)
    return jnp.einsum("tnb,tne->nbe", left, right, preferred_element_type=jnp.float32)


def to_columns(values):
    return lax.all_to_all(values, "tm", split_axis=1, concat_axis=0, tiled=True)


def to_rows(values):
    return lax.all_to_all(values, "tm", split_axis=0, concat_axis=1, tiled=True)


def body(inputs, kernel, w_in, w_gate, w_out, factor_a, factor_b, cotangent):
    rows, chans = inputs.shape
    inner = factor_a.shape[0]
    local = rows // inner
    mixed_in = mix(inputs, w_in).astype(jnp.bfloat16)
    gate = mix(inputs, w_gate)
    mixed3 = mixed_in.reshape(local, inner, chans)
    first = jnp.einsum("ijc,jk->ikc", mixed3, factor_a, preferred_element_type=jnp.float32)
    twiddle = kernel.reshape(local, inner, chans).astype(jnp.float32)
    twisted = (first * twiddle).astype(jnp.bfloat16)
    twisted_cols = to_columns(twisted)
    second_cols = jnp.einsum(
        "im,ikc->mkc", factor_b, twisted_cols, preferred_element_type=jnp.float32
    )
    second_rows = to_rows(second_cols.astype(jnp.bfloat16))
    second = second_rows.reshape(rows, chans)
    second32 = second.astype(jnp.float32)
    gated = (second32 * gate).astype(jnp.bfloat16)
    outputs = mix(gated, w_out).astype(jnp.bfloat16)
    grad_gated = mix_back(cotangent, w_out)
    grad_second = (grad_gated * gate).astype(jnp.bfloat16)
    grad_gate = (grad_gated * second32).astype(jnp.bfloat16)
    grad_second_cols = to_columns(grad_second.reshape(local, inner, chans))
    grad_twisted_cols = jnp.einsum(
        "im,mkc->ikc", factor_b, grad_second_cols, preferred_element_type=jnp.float32
    )
    factor_b_part = jnp.einsum(
        "ikc,mkc->im", twisted_cols, grad_second_cols, preferred_element_type=jnp.float32
    )
    grad_twisted = to_rows(grad_twisted_cols.astype(jnp.bfloat16))
    grad_tw32 = grad_twisted.astype(jnp.float32)
    grad_first = (grad_tw32 * twiddle).astype(jnp.bfloat16)
    grad_kernel = (grad_tw32 * first).astype(jnp.bfloat16).reshape(rows, chans)
    factor_a_part = jnp.einsum(
        "ijc,ikc->jk", mixed3, grad_first, preferred_element_type=jnp.float32
    )
    grad_mixed = jnp.einsum("jk,ikc->ijc", factor_a, grad_first, preferred_element_type=jnp.float32)
    grad_mixed = grad_mixed.astype(jnp.bfloat16).reshape(rows, chans)
    grad_inputs = (mix_back(grad_mixed, w_in) + mix_back(grad_gate, w_gate)).astype(jnp.bfloat16)
    mixer_terms = (
        mix_grad(inputs, grad_mixed, w_in),
        mix_grad(inputs, grad_gate, w_gate),
        mix_grad(gated, cotangent, w_out),
    )
    summed_in, summed_gate, summed_out = lax.psum(
        (mixer_terms[0], mixer_terms[1], mixer_terms[2]), "tm"
    )
    token_scale = 1.0 / math.sqrt(N1 * N2)
    factor_terms = (factor_a_part, factor_b_part)
    factor_terms = lax.psum((factor_terms[0], factor_terms[1]), "tensor")
    factor_pieces = (
        lax.psum_scatter(factor_terms[0], "tm", scatter_dimension=0, tiled=True),
        lax.psum_scatter(factor_terms[1], "tm", scatter_dimension=0, tiled=True),
    )
    grad_factor_a = factor_pieces[0] / math.sqrt(N1 * D)
    grad_factor_b = factor_pieces[1] / math.sqrt(N2 * D)
    return (
        outputs,
        grad_inputs,
        grad_kernel,
        summed_in * token_scale,
        summed_gate * token_scale,
        summed_out * token_scale,
        grad_factor_a,
        grad_factor_b,
    )


def solution(mesh):
    return jax.shard_map(
        body,
        mesh=mesh,
        in_specs=(
            P("tm", "tensor"),
            P("tm", "tensor"),
            P("tensor", None, None),
            P("tensor", None, None),
            P("tensor", None, None),
            P(),
            P(),
            P("tm", "tensor"),
        ),
        out_specs=(
            P("tm", "tensor"),
            P("tm", "tensor"),
            P("tm", "tensor"),
            P("tensor", None, None),
            P("tensor", None, None),
            P("tensor", None, None),
            P("tm", None),
            P("tm", None),
        ),
        check_vma=False,
    )
```

profile of v0, /device:TPU:0, one launch (start us, length us, event | category | flops | bytes accessed | tf_op | source)
XLA Modules:
  0.0 1193.9 jit_solution(16334861767342294621)
XLA Ops:
  7.2 16.7 %copy.84 = bf16[16384,384]{0,1:T(8,128)(2,1)} copy(bf16[16384,384]{1,0:T(8,128)(2,1)} %param.8) | data formatting | bytes 25165824 | tf_op args[0]
  23.8 16.6 %copy.100 = bf16[16384,384]{0,1:T(8,128)(2,1)} copy(bf16[16384,384]{1,0:T(8,128)(2,1)} %param.15) | data formatting | bytes 25165824 | tf_op args[7]
  40.5 16.4 %fusion.27 = f32[3,128,16384]{2,1,0:T(8,128)} fusion(bf16[3,128,128]{2,1,0:T(8,128)(2,1)S(1)} %copy-done.7, bf16[16384,3,128]{0,2,1:T(8,128)(2,1)} %bitcast.112), kind=kOutput, calls=%fused_computation.41 | convolution fusion | flops 1610612736 | bytes 37847040 | tf_op jit(solution)/shard_map/tnb,nbe->tne/dot_general | solution.py:16
  56.8 26.7 %fusion = (bf16[16384,3,128]{0,2,1:T(8,128)(2,1)}, f32[3,128,16384]{2,1,0:T(8,128)}) fusion(f32[3,128,16384]{2,1,0:T(8,128)} %fusion.27, bf16[3,128,128]{2,1,0:T(8,128)(2,1)S(1)} %copy-done.3, bf16[16384,3,128]{0,2,1:T(8,128)(2,1)} %bitcast.117), kind=kOutput, calls=%fused_computation.4 | convolution fusion | flops 1623195648 | bytes 75595776 | tf_op jit(solution)/shard_map/tne,nbe->tnb/dot_general | solution.py:23
  83.5 12.8 %copy.146 = bf16[48,8,32,512]{3,2,1,0:T(8,128)(2,1)} copy(bf16[48,8,32,512]{3,1,2,0:T(8,128)(2,1)} %bitcast.123) | data formatting | bytes 25165824
  96.3 18.2 %copy.102 = bf16[32,512,384]{2,0,1:T(8,128)(2,1)} copy(bf16[32,512,384]{1,0,2:T(8,128)(2,1)} %bitcast.125) | data formatting | bytes 25165824 | tf_op jit(solution)/shard_map/convert_element_type | solution.py:62
  114.5 144.3 %all_to_all.54 = bf16[32,512,384]{2,0,1:T(8,128)(2,1)S(1)} all-to-all(bf16[32,512,384]{2,0,1:T(8,128)(2,1)} %copy.102), channel_id=1, replica_groups=mesh['tm'=8,'tensor'=4] {'tm'}, dimensions={1} | all-to-all | bytes 25165824 | tf_op jit(solution)/shard_map/all_to_all | solution.py:35
  258.8 6.8 copy.104
  265.7 18.5 %convert_bitcast_fusion.3 = bf16[256,64,384]{0,2,1:T(8,128)(2,1)} fusion(bf16[256,64,384]{2,1,0:T(8,128)(2,1)} %bitcast.119, bf16[256,256]{1,0:T(8,128)(2,1)S(1)} %copy-done.9), kind=kOutput, calls=%fused_computation.19 | convolution fusion | flops 3227516928 | bytes 25296896 | tf_op jit(solution)/shard_map/im,mkc->ikc/dot_general | solution.py:65
  284.2 16.8 %copy.106 = bf16[256,64,384]{2,1,0:T(8,128)(2,1)} copy(bf16[256,64,384]{0,2,1:T(8,128)(2,1)} %convert_bitcast_fusion.3) | data formatting | bytes 25165824 | tf_op jit(solution)/shard_map/convert_element_type | solution.py:71
  301.0 5.7 all-to-all-start.3
  306.7 12.6 %convolution_convert_fusion.1 = bf16[3,128,16384]{2,1,0:T(8,128)(2,1)} fusion(bf16[3,128,128]{2,1,0:T(8,128)(2,1)S(1)} %copy-done.5, bf16[16384,3,128]{0,2,1:T(8,128)(2,1)} %bitcast.113), kind=kOutput, calls=%fused_computation.15 | convolution fusion | flops 1616904192 | bytes 25264128 | tf_op jit(solution)/shard_map/tnb,nbe->tne/dot_general | solution.py:16
  319.3 12.8 %copy.145 = bf16[48,8,32,512]{3,2,1,0:T(8,128)(2,1)} copy(bf16[48,8,32,512]{3,1,2,0:T(8,128)(2,1)} %bitcast.128) | data formatting | bytes 25165824
  332.1 17.6 %copy.88 = f32[32,512,384]{1,2,0:T(8,128)} copy(bf16[32,512,384]{2,1,0:T(8,128)(2,1)} %bitcast.130) | data formatting | bytes 37748736 | tf_op jit(solution)/shard_map/convert_element_type | solution.py:50
  349.6 96.0 %all-to-all-done.3 = bf16[256,64,384]{2,1,0:T(8,128)(2,1)} async-done(((bf16[256,64,384]{2,1,0:T(8,128)(2,1)}), bf16[256,64,384]{2,1,0:T(8,128)(2,1)}, u32[]{:S(2)}, u32[]{:S(2)}) %all-to-all-start.3) | async-done | bytes 12582944 | tf_op jit(solution)/shard_map/all_to_all | solution.py:39
  445.7 7.1 convert_bitcast_fusion
  452.8 9.5 copy.107
  462.3 24.7 %copy.113 = f32[32,512,384]{1,2,0:T(8,128)} copy(f32[32,512,384]{2,1,0:T(8,128)} %bitcast.116) | data formatting | bytes 50331648 | tf_op jit(solution)/shard_map/convert_element_type | solution.py:72
  487.1 33.2 %fusion.4 = (bf16[32,512,384]{1,2,0:T(8,128)(2,1)}, bf16[32,512,384]{1,2,0:T(8,128)(2,1)}) fusion(f32[32,512,384]{1,2,0:T(8,128)} %copy.113, f32[32,512,384]{1,2,0:T(8,128)} %copy.88, bf16[512,512]{1,0:T(8,128)(2,1)S(1)} %copy-done, bf16[32,512,384]{1,0,2:T(8,128)(2,1)} %bitcast.121), kind=kOutput, calls=%fused_computation.11 | convolution fusion | flops 6467616768 | bytes 88604672 | tf_op jit(solution)/shard_map/ijc,jk->ikc/dot_general | solution.py:49
  520.3 16.7 %copy.89 = bf16[32,512,384]{2,0,1:T(8,128)(2,1)} copy(bf16[32,512,384]{1,2,0:T(8,128)(2,1)} %get-tuple-element.36) | data formatting | bytes 25165824 | tf_op jit(solution)/shard_map/convert_element_type | solution.py:51
  537.0 143.3 %all_to_all.55 = bf16[32,512,384]{2,0,1:T(8,128)(2,1)S(1)} all-to-all(bf16[32,512,384]{2,0,1:T(8,128)(2,1)} %copy.89), channel_id=1, replica_groups=mesh['tm'=8,'tensor'=4] {'tm'}, dimensions={1} | all-to-all | bytes 25165824 | tf_op jit(solution)/shard_map/all_to_all | solution.py:35
  680.4 7.1 copy.91
  687.5 19.0 %convert_bitcast_fusion.4 = bf16[256,64,384]{0,2,1:T(8,128)(2,1)} fusion(bf16[256,64,384]{2,1,0:T(8,128)(2,1)} %bitcast.133, bf16[256,256]{1,0:T(8,128)(2,1)S(1)} %copy-done.9), kind=kOutput, calls=%fused_computation.20 | convolution fusion | flops 3227516928 | bytes 25296896 | tf_op jit(solution)/shard_map/im,ikc->mkc/dot_general | solution.py:53
  706.5 16.7 %copy.93 = bf16[256,64,384]{2,1,0:T(8,128)(2,1)} copy(bf16[256,64,384]{0,2,1:T(8,128)(2,1)} %convert_bitcast_fusion.4) | data formatting | bytes 25165824 | tf_op jit(solution)/shard_map/convert_element_type | solution.py:56
  728.8 17.3 %multiply_convert_fusion = bf16[32,512,384]{2,1,0:T(8,128)(2,1)} fusion(bf16[32,512,384]{2,1,0:T(8,128)(2,1)} %bitcast.131, f32[32,8,64,384]{3,2,1,0:T(8,128)} %copy.107), kind=kLoop, calls=%fused_computation.13 | loop fusion | flops 18874368 | bytes 50331648 | tf_op jit(solution)/shard_map/convert_element_type | solution.py:73
  746.2 16.8 %copy.119 = bf16[32,512,384]{1,0,2:T(8,128)(2,1)} copy(bf16[32,512,384]{2,1,0:T(8,128)(2,1)} %multiply_convert_fusion) | data formatting | bytes 25165824 | tf_op jit(solution)/shard_map/convert_element_type | solution.py:73
  763.0 11.6 convert_bitcast_fusion.2
  774.6 20.3 %copy.109 = bf16[32,512,384]{1,0,2:T(8,128)(2,1)} copy(bf16[32,512,384]{1,2,0:T(8,128)(2,1)S(1)} %convert_bitcast_fusion.2) | data formatting | bytes 25165824 | tf_op jit(solution)/shard_map/convert_element_type | solution.py:79
  794.9 19.5 %reshape_reshape.4 = bf16[16384,3,128]{0,2,1:T(8,128)(2,1)} reshape(bf16[32,512,384]{1,0,2:T(8,128)(2,1)} %copy.109) | data formatting | bytes 25165824 | tf_op jit(solution)/shard_map/reshape;reshape | solution.py:22
  814.4 14.2 %convolution_bitcast_fusion = f32[512,512]{1,0:T(8,128)} fusion(bf16[32,512,384]{1,0,2:T(8,128)(2,1)} %bitcast.122, bf16[32,512,384]{1,0,2:T(8,128)(2,1)} %copy.119), kind=kOutput, calls=%fused_computation.28 | convolution fusion | flops 6442450944 | bytes 26214400 | tf_op jit(solution)/shard_map/ijc,ikc->jk/dot_general | solution.py:75
  828.7 16.8 %fusion.29 = f32[3,16384,128]{1,2,0:T(8,128)} fusion(bf16[3,128,128]{2,1,0:T(8,128)(2,1)S(1)} %copy-done.6, bf16[16384,3,128]{0,2,1:T(8,128)(2,1)} %reshape_reshape.4), kind=kOutput, calls=%fused_computation.43 | convolution fusion | flops 1610612736 | bytes 37847040 | tf_op jit(solution)/shard_map/tne,nbe->tnb/dot_general | solution.py:23
  845.5 26.4 %reduce-scatter.3.cloned.1.call-done = f32[64,512]{1,0:T(8,128)} async-done(((f32[512,512]{1,0:T(8,128)}), f32[64,512]{1,0:T(8,128)}) %reduce-scatter.3.cloned.1.call-update) | async-done | bytes 131088 | tf_op jit(solution)/shard_map/reduce_scatter | solution.py:93
  871.9 29.3 %fusion.18 = f32[256,256]{1,0:T(8,128)} fusion(bf16[256,64,384]{2,1,0:T(8,128)(2,1)} %bitcast.120, bf16[256,64,384]{2,1,0:T(8,128)(2,1)} %bitcast.134), kind=kOutput, calls=%fused_computation.29 | convolution fusion | flops 3221225472 | bytes 25427968 | tf_op jit(solution)/shard_map/ikc,mkc->im/dot_general | solution.py:68
  901.3 10.7 convolution_bitcast_fusion.2
  912.0 16.6 %copy.114 = bf16[32,512,384]{2,1,0:T(8,128)(2,1)} copy(bf16[32,512,384]{1,2,0:T(8,128)(2,1)} %get-tuple-element.35) | data formatting | bytes 25165824 | tf_op jit(solution)/shard_map/convert_element_type | solution.py:74
  930.2 14.1 %reduce-scatter.5.cloned.1.call-done = f32[32,256]{1,0:T(8,128)} async-done(((f32[256,256]{1,0:T(8,128)}), f32[32,256]{1,0:T(8,128)}) %reduce-scatter.5.cloned.1.call-update) | async-done | bytes 32784 | tf_op jit(solution)/shard_map/reduce_scatter | solution.py:94
  944.3 19.6 %psum.41 = f32[32,256]{1,0:T(8,128)S(1)} all-reduce(f32[32,256]{1,0:T(8,128)} %reduce-scatter.5.cloned.1.call-done), channel_id=1, replica_groups=mesh['tm'=8,'tensor'=4] {'tensor'}, use_global_device_ids=true, to_apply=%region_5.0 | all-reduce | flops 8192 | bytes 65536 | tf_op jit(solution)/shard_map/psum | solution.py:91
  964.6 14.5 %convert_bitcast_fusion.1 = f32[32,8,64,384]{3,2,0,1:T(8,128)} fusion(bf16[8,32,64,384]{3,2,1,0:T(8,128)(2,1)} %bitcast.35), kind=kLoop, calls=%fused_computation.1 | loop fusion | flops 6291456 | bytes 37748736 | tf_op jit(solution)/shard_map/convert_element_type | solution.py:58
  979.0 45.2 %copy.143 = f32[32,8,64,384]{2,1,0,3:T(8,128)} copy(f32[32,8,64,384]{3,2,0,1:T(8,128)} %convert_bitcast_fusion.1) | data formatting | bytes 50331648 | tf_op jit(solution)/shard_map/convert_element_type | solution.py:58
  1024.2 36.9 %reshape.77 = f32[16384,3,128]{0,2,1:T(8,128)} reshape(f32[32,8,64,384]{2,1,0,3:T(8,128)} %copy.143) | data formatting | bytes 50331648 | tf_op jit(solution)/shard_map/convert_element_type | solution.py:58
  1061.1 28.4 %fusion.1 = (bf16[16384,3,128]{0,2,1:T(8,128)(2,1)}, bf16[16384,3,128]{0,2,1:T(8,128)(2,1)S(1)}) fusion(f32[16384,3,128]{0,2,1:T(8,128)} %reshape.77, f32[3,128,16384]{2,1,0:T(8,128)} %get-tuple-element.40, f32[3,128,16384]{2,1,0:T(8,128)} %fusion.27), kind=kLoop, calls=%fused_computation.5 | loop fusion | flops 25165824 | bytes 100663296 | tf_op jit(solution)/shard_map/convert_element_type | solution.py:63
  1089.5 11.6 fusion.28
  1101.1 10.7 convolution_bitcast_fusion.1
  1111.8 18.1 %add_convert_fusion = bf16[3,16384,128]{1,2,0:T(8,128)(2,1)} fusion(f32[3,16384,128]{1,2,0:T(8,128)} %fusion.29, bf16[3,128,128]{2,1,0:T(8,128)(2,1)S(1)} %copy-done.8, bf16[16384,3,128]{0,2,1:T(8,128)(2,1)} %get-tuple-element.37), kind=kOutput, calls=%fused_computation.12 | convolution fusion | flops 1623195648 | bytes 50429952 | tf_op jit(solution)/shard_map/tne,nbe->tnb/dot_general | solution.py:23
  1130.0 9.2 convolution_convert_fusion
  1139.2 16.6 %copy.123 = bf16[16384,384]{1,0:T(8,128)(2,1)} copy(bf16[16384,384]{0,1:T(8,128)(2,1)} %bitcast.129) | data formatting | bytes 25165824
  1155.8 16.7 %copy.122 = bf16[16384,384]{1,0:T(8,128)(2,1)} copy(bf16[16384,384]{0,1:T(8,128)(2,1)} %bitcast.124) | data formatting | bytes 25165824
  1172.5 10.3 all-reduce.6.cloned.1.call-done
  (38 shorter events, 12.5 us)
Async XLA Ops:
  7.2 479.9 %copy-start = (bf16[512,512]{1,0:T(8,128)(2,1)S(1)}, bf16[512,512]{1,0:T(8,128)(2,1)}, u32[]{:S(2)}) copy-start(bf16[512,512]{1,0:T(8,128)(2,1)} %param.13) | copy-start | bytes 1572868
  23.8 16.6 %copy-start.7 = (bf16[3,128,128]{2,1,0:T(8,128)(2,1)S(1)}, bf16[3,128,128]{2,1,0:T(8,128)(2,1)}, u32[]{:S(2)}) copy-start(bf16[3,128,128]{2,1,0:T(8,128)(2,1)} %param.11) | copy-start | bytes 294916
  40.5 16.4 %copy-start.3 = (bf16[3,128,128]{2,1,0:T(8,128)(2,1)S(1)}, bf16[3,128,128]{2,1,0:T(8,128)(2,1)}, u32[]{:S(2)}) copy-start(bf16[3,128,128]{2,1,0:T(8,128)(2,1)} %param.12) | copy-start | bytes 294916
  258.8 6.8 copy-start.9
  301.0 5.7 copy-start.5
  301.0 144.7 %all-to-all-start.3 = ((bf16[256,64,384]{2,1,0:T(8,128)(2,1)}), bf16[256,64,384]{2,1,0:T(8,128)(2,1)}, u32[]{:S(2)}, u32[]{:S(2)}) async-start(bf16[256,64,384]{2,1,0:T(8,128)(2,1)} %copy.106), calls=%async_computation.3 | async-start | bytes 25165824 | tf_op jit(solution)/shard_map/all_to_all | solution.py:39
  723.2 241.4 %all-to-all-start.1 = ((bf16[256,64,384]{2,1,0:T(8,128)(2,1)}), bf16[256,64,384]{2,1,0:T(8,128)(2,1)}, u32[]{:S(2)}, u32[]{:S(2)}) async-start(bf16[256,64,384]{2,1,0:T(8,128)(2,1)} %copy.93), calls=%async_computation.1 | async-start | bytes 25165824 | tf_op jit(solution)/shard_map/all_to_all | solution.py:39
  728.6 143.2 %reduce-scatter.3.cloned.1.call-start = ((), (), s32[]{:S(2)}) async-start(), calls=%async_computation.6 | async-start | bytes 1179648 | tf_op jit(solution)/shard_map/reduce_scatter | solution.py:93
  814.4 14.2 %copy-start.6 = (bf16[3,128,128]{2,1,0:T(8,128)(2,1)S(1)}, bf16[3,128,128]{2,1,0:T(8,128)(2,1)}, u32[]{:S(2)}) copy-start(bf16[3,128,128]{2,1,0:T(8,128)(2,1)} %param.10) | copy-start | bytes 294916
  828.6 100.0 %all-reduce.4.cloned.1.call-start = ((), (), s32[]{:S(2)}) async-start(), calls=%async_computation.7 | async-start | bytes 262144 | tf_op jit(solution)/shard_map/psum | solution.py:91
  871.9 72.5 %reduce-scatter.5.cloned.1.call-start = ((), (), s32[]{:S(2)}) async-start(), calls=%async_computation.8 | async-start | bytes 294912 | tf_op jit(solution)/shard_map/reduce_scatter | solution.py:94
  901.3 281.4 %all-reduce.6.cloned.1.call-start = ((), (), s32[]{:S(2)}) async-start(), calls=%async_computation.9 | async-start | bytes 1179648 | tf_op jit(solution)/shard_map/psum | solution.py:86
  1089.5 11.6 copy-start.2
  1101.1 10.7 copy-start.8
  1111.8 18.2 %copy-start.4 = (bf16[3,128,128]{2,1,0:T(8,128)(2,1)S(1)}, bf16[3,128,128]{2,1,0:T(8,128)(2,1)}, u32[]{:S(2)}) copy-start(bf16[3,128,128]{2,1,0:T(8,128)(2,1)} %param.12) | copy-start | bytes 294916
  1155.8 31.4 %copy-start.1 = (bf16[512,512]{1,0:T(8,128)(2,1)S(1)}, bf16[512,512]{1,0:T(8,128)(2,1)}, u32[]{:S(2)}) copy-start(bf16[512,512]{1,0:T(8,128)(2,1)} %param.13) | copy-start | bytes 1572868
Sparse Core Ops, SparseCore 0:
  828.7 43.0 reduce-scatter.2
  874.2 33.5 all-reduce.3
  911.1 33.1 reduce-scatter.4
  1130.1 52.6 all-reduce.5
where the time goes:
time: 1210 us; the launch traced here: 1190 us
  local copies, waits for them, and re-layouts  384 us (32%)
  blocking collectives  307 us (25%)
  matrix products  259 us (21%)
  waiting for transfers between devices  147 us (12%)
  other arithmetic  71.5 us (6%)
  between operations  14.1 us (1%)
    all_to_all x2, blocking collectives, to_columns(): return lax.all_to_all(values, 'tm', split_axis=1, concat_axis=0, tiled=True)  288 us
    all_to_all x2, waiting for transfers between devices, to_rows(): return lax.all_to_all(values, 'tm', split_axis=0, concat_axis=1, tiled=True)  96.1 us
    unnamed x29, local copies, waits for them, and re-layouts  94.6 us
    convert_element_type x2, local copies, waits for them, and re-layouts, body(): second32 = second.astype(jnp.float32)  82 us
    dot_general x3, matrix products, mix_back(): jnp.einsum('tne,nbe->tnb', blocks, weight, preferred_element_type=jnp.flo...  61.6 us
    dot_general x3, matrix products, mix(): jnp.einsum('tnb,nbe->tne', blocks, weight, preferred_element_type=jnp.flo...  38.2 us
    convert_element_type x2, local copies, waits for them, and re-layouts, body(): grad_tw32 = grad_twisted.astype(jnp.float32)  34.2 us
    dot_general x1, matrix products, body(): jnp.einsum('ijc,jk->ikc', mixed3, factor_a, preferred_element_type=jnp.fl...  33.2 us
  transfers between devices with their start and end apart: 6, of which 4 were waited for; matrix products, arithmetic and copies ran while one was open for 22% of the time, Pallas kernels for 0%

commit v1 on v0

v1 whole, which is shorter than its diff:
```python
import functools
import math

import jax
import jax.numpy as jnp
from jax import lax
from jax.experimental import pallas as pl
from jax.experimental.pallas import tpu as pltpu
from jax.sharding import PartitionSpec as P

D = 1536
N1 = 256
N2 = 512
BF = jnp.bfloat16
F32 = jnp.float32
VMEM_LIMIT = 56 * 1024 * 1024


def dot(left, right):
    return jnp.dot(left, right, preferred_element_type=F32)


def dot_nt(left, right):
    return lax.dot_general(left, right, (((1,), (1,)), ((), ())), preferred_element_type=F32)


def dot_tn(left, right):
    return lax.dot_general(left, right, (((0,), (0,)), ((), ())), preferred_element_type=F32)


def params(dims):
    return pltpu.CompilerParams(
        dimension_semantics=("arbitrary",) * dims, vmem_limit_bytes=VMEM_LIMIT
    )


def cost(flops, nbytes):
    return pl.CostEstimate(flops=int(flops), bytes_accessed=int(nbytes), transcendentals=0)


def stack_rows(pieces):
    if pieces[0].shape[0] % 16 == 0:
        return jnp.concatenate(pieces, axis=0)
    return jnp.concatenate([p.astype(F32) for p in pieces], axis=0).astype(BF)


def grad_second_kernel(p_ref, x_ref, ct_ref, wg_ref, wo_ref, out_ref, scr):
    blocks, span, width = x_ref.shape
    x = x_ref[...].reshape(blocks * span, width)
    ct = ct_ref[...].reshape(blocks * span, width)
    scr[...] = dot_nt(ct, wo_ref[0]) * dot(x, wg_ref[0])
    for k in range(span):
        out_ref[k] = scr[pl.ds(k, blocks, stride=span), :].astype(BF)


def grad_second_call(partner, x3, ct3, w_gate, w_out, span):
    blocks, inner, chans = x3.shape
    width = w_gate.shape[1]
    rows = pl.BlockSpec((blocks, span, width), lambda n, p: (0, p[0], n))
    weight = pl.BlockSpec((1, width, width), lambda n, p: (n, 0, 0))
    size = blocks * span * chans
    return pl.pallas_call(
        grad_second_kernel,
        grid_spec=pltpu.PrefetchScalarGridSpec(
            num_scalar_prefetch=1,
            grid=(chans // width,),
            in_specs=[rows, rows, weight, weight],
            out_specs=pl.BlockSpec((span, blocks, width), lambda n, p: (0, 0, n)),
            scratch_shapes=[pltpu.VMEM((blocks * span, width), F32)],
        ),
        out_shape=jax.ShapeDtypeStruct((span, blocks, chans), BF),
        compiler_params=params(1),
        cost_estimate=cost(4 * size * width, 6 * size),
        name="grad_second",
    )(partner, x3, ct3, w_gate, w_out)


def twisted_kernel(me_ref, x_ref, kn_ref, wi_ref, at_ref, *rest):
    outs, scr = rest[:-1], rest[-1]
    some, inner, width = x_ref.shape
    span, blocks, _ = outs[0].shape
    step = pl.program_id(1)
    mixed = dot(x_ref[...].reshape(some * inner, width), wi_ref[0]).astype(BF)
    for q in range(0, some, 2):
        pair = jnp.concatenate(
            [mixed[q * inner : (q + 1) * inner], mixed[(q + 1) * inner : (q + 2) * inner]], axis=1
        )
        first = dot(at_ref[...], pair)
        for h in range(2):
            value = first[:, h * width : (h + 1) * width] * kn_ref[q + h].astype(F32)
            scr[pl.ds(step * some + q + h, inner, stride=blocks), :] = value

    @pl.when(step == pl.num_programs(1) - 1)
    def _():
        for d, out in enumerate(outs):
            first_row = pl.multiple_of((me_ref[0] ^ d) * (span * blocks), span * blocks)
            piece = scr[pl.ds(first_row, span * blocks), :]
            out[...] = piece.reshape(span, blocks, width).astype(BF)


def twisted_call(me, x3, kn3, w_in, factor_at, parts):
    blocks, inner, chans = x3.shape
    width = w_in.shape[1]
    span = inner // parts
    some = 4
    rows = pl.BlockSpec((some, inner, width), lambda n, i, m: (i, 0, n))
    out = pl.BlockSpec((span, blocks, width), lambda n, i, m: (0, 0, n))
    size = blocks * inner * chans
    return pl.pallas_call(
        twisted_kernel,
        grid_spec=pltpu.PrefetchScalarGridSpec(
            num_scalar_prefetch=1,
            grid=(chans // width, blocks // some),
            in_specs=[
                rows,
                rows,
                pl.BlockSpec((1, width, width), lambda n, i, m: (n, 0, 0)),
                pl.BlockSpec((inner, inner), lambda n, i, m: (0, 0)),
            ],
            out_specs=[out] * parts,
            scratch_shapes=[pltpu.VMEM((inner * blocks, width), F32)],
        ),
        out_shape=[jax.ShapeDtypeStruct((span, blocks, chans), BF)] * parts,
        compiler_params=params(2),
        cost_estimate=cost(2 * size * (width + inner), 6 * size),
        name="twisted",
    )(me, x3, kn3, w_in, factor_at)


def grad_twisted_kernel(fb_ref, *refs):
    parts = len(refs) // 2
    ins, outs = refs[:parts], refs[parts:]
    some, blocks, _ = ins[0].shape
    for k in range(some):
        value = dot(fb_ref[...], stack_rows([ref[k] for ref in ins])).astype(BF)
        for d in range(parts):
            outs[d][k] = value[d * blocks : (d + 1) * blocks]


def grad_twisted_call(fb, arrays):
    parts = len(arrays)
    span, blocks, chans = arrays[0].shape
    some = 8
    spec = pl.BlockSpec((some, blocks, chans), lambda k: (k, 0, 0))
    size = parts * span * blocks * chans
    return pl.pallas_call(
        grad_twisted_kernel,
        grid=(span // some,),
        in_specs=[pl.BlockSpec(fb.shape, lambda k: (0, 0))] + [spec] * parts,
        out_specs=[spec] * parts,
        out_shape=[jax.ShapeDtypeStruct((span, blocks, chans), BF)] * parts,
        compiler_params=params(1),
        cost_estimate=cost(2 * size * fb.shape[0], 4 * size),
        name="grad_twisted",
    )(fb, *arrays)


def second_kernel(fbt_ref, *refs):
    parts = (len(refs) - 1) // 3
    tws, gss, outs, fbg = refs[:parts], refs[parts : 2 * parts], refs[2 * parts : -1], refs[-1]
    some, blocks, _ = tws[0].shape

    @pl.when(pl.program_id(0) == 0)
    def _():
        fbg[...] = jnp.zeros_like(fbg)

    for k in range(some):
        tw = stack_rows([ref[k] for ref in tws])
        gs = stack_rows([ref[k] for ref in gss])
        value = dot(fbt_ref[...], tw).astype(BF)
        for d in range(parts):
            outs[d][k] = value[d * blocks : (d + 1) * blocks]
        fbg[...] += dot_nt(tw, gs)


def second_call(fbt, tws, gss):
    parts = len(tws)
    span, blocks, chans = tws[0].shape
    some = 8
    spec = pl.BlockSpec((some, blocks, chans), lambda k: (k, 0, 0))
    whole = pl.BlockSpec(fbt.shape, lambda k: (0, 0))
    size = parts * span * blocks * chans
    result = pl.pallas_call(
        second_kernel,
        grid=(span // some,),
        in_specs=[whole] + [spec] * (2 * parts),
        out_specs=[spec] * parts + [whole],
        out_shape=[jax.ShapeDtypeStruct((span, blocks, chans), BF)] * parts
        + [jax.ShapeDtypeStruct(fbt.shape, F32)],
        compiler_params=params(1),
        cost_estimate=cost(4 * size * fbt.shape[0], 6 * size),
        name="second",
    )(fbt, *tws, *gss)
    return result[:-1], result[-1]


def grad_mixed_kernel(me_ref, x_ref, kn_ref, wi_ref, at_ref, a_ref, *rest):
    gts = rest[:-5]
    gk_ref, gm_ref, fag, gwi, scr = rest[-5:]
    some, inner, width = x_ref.shape
    span, blocks, _ = gts[0].shape
    step = pl.program_id(1)

    @pl.when(step == 0)
    def _():
        gwi[...] = jnp.zeros_like(gwi)
        for d, ref in enumerate(gts):
            first_row = pl.multiple_of((me_ref[0] ^ d) * (span * blocks), span * blocks)
            scr[pl.ds(first_row, span * blocks), :] = (
                ref[...].astype(F32).reshape(span * blocks, width)
            )

    @pl.when((step == 0) & (pl.program_id(0) == 0))
    def _():
        fag[...] = jnp.zeros_like(fag)

    x = x_ref[...].reshape(some * inner, width)
    mixed = dot(x, wi_ref[0]).astype(BF)
    for q in range(0, some, 2):
        pair = jnp.concatenate(
            [mixed[q * inner : (q + 1) * inner], mixed[(q + 1) * inner : (q + 2) * inner]], axis=1
        )
        first = dot(at_ref[...], pair)
        grads = []
        for h in range(2):
            gt = scr[pl.ds(step * some + q + h, inner, stride=blocks), :]
            gk_ref[q + h] = (gt * first[:, h * width : (h + 1) * width]).astype(BF)
            grads.append((gt * kn_ref[q + h].astype(F32)).astype(BF))
        grad_first = jnp.concatenate(grads, axis=1)
        fag[...] += dot_nt(pair, grad_first)
        grad_mixed = dot(a_ref[...], grad_first).astype(BF)
        for h in range(2):
            gm_ref[q + h] = grad_mixed[:, h * width : (h + 1) * width]
    gwi[0] += dot_tn(x, gm_ref[...].reshape(some * inner, width))


def grad_mixed_call(me, x3, kn3, w_in, factor_at, factor_a, gts):
    parts = len(gts)
    blocks, inner, chans = x3.shape
    width = w_in.shape[1]
    span = inner // parts
    some = 4
    rows = pl.BlockSpec((some, inner, width), lambda n, i, m: (i, 0, n))
    weight = pl.BlockSpec((1, width, width), lambda n, i, m: (n, 0, 0))
    whole = pl.BlockSpec((inner, inner), lambda n, i, m: (0, 0))
    size = blocks * inner * chans
    return pl.pallas_call(
        grad_mixed_kernel,
        grid_spec=pltpu.PrefetchScalarGridSpec(
            num_scalar_prefetch=1,
            grid=(chans // width, blocks // some),
            in_specs=[rows, rows, weight, whole, whole]
            + [pl.BlockSpec((span, blocks, width), lambda n, i, m: (0, 0, n))] * parts,
            out_specs=[rows, rows, whole, weight],
            scratch_shapes=[pltpu.VMEM((inner * blocks, width), F32)],
        ),
        out_shape=[
            jax.ShapeDtypeStruct(x3.shape, BF),
            jax.ShapeDtypeStruct(x3.shape, BF),
            jax.ShapeDtypeStruct((inner, inner), F32),
            jax.ShapeDtypeStruct(w_in.shape, F32),
        ],
        compiler_params=params(2),
        cost_estimate=cost(2 * size * (2 * width + 3 * inner), 10 * size),
        name="grad_mixed",
    )(me, x3, kn3, w_in, factor_at, factor_a, *gts)


def outputs_kernel(p_ref, x_ref, ct_ref, gm_ref, se_ref, wi_ref, wg_ref, wo_ref, *rest):
    out_ref, gi_ref, gwg, gwo, scr = rest[-5:]
    before = rest[:-5]
    blocks, span, width = x_ref.shape
    rows = blocks * span
    x = x_ref[...].reshape(rows, width)
    ct = ct_ref[...].reshape(rows, width)
    scr[...] = se_ref[...].astype(F32).reshape(rows, width)
    second = jnp.concatenate(
        [scr[pl.ds(i, span, stride=blocks), :] for i in range(blocks)], axis=0
    )
    gated = (second * dot(x, wg_ref[0])).astype(BF)
    out_ref[...] = dot(gated, wo_ref[0]).astype(BF).reshape(blocks, span, width)
    grad_gate = (dot_nt(ct, wo_ref[0]) * second).astype(BF)
    grad_mixed = gm_ref[...].reshape(rows, width)
    grad_inputs = dot_nt(grad_mixed, wi_ref[0]) + dot_nt(grad_gate, wg_ref[0])
    gi_ref[...] = grad_inputs.astype(BF).reshape(blocks, span, width)
    gate_term = dot_tn(x, grad_gate)
    out_term = dot_tn(gated, ct)
    if before:
        gate_term += before[2][0]
        out_term += before[3][0]
    gwg[0] = gate_term
    gwo[0] = out_term


def outputs_call(partner, x3, ct3, gm3, second, w_in, w_gate, w_out, before):
    blocks, inner, chans = x3.shape
    width = w_in.shape[1]
    span = second.shape[0]
    rows = pl.BlockSpec((blocks, span, width), lambda n, p: (0, p[0], n))
    weight = pl.BlockSpec((1, width, width), lambda n, p: (n, 0, 0))
    anywhere = pl.BlockSpec(memory_space=pl.ANY)
    size = blocks * span * chans
    return pl.pallas_call(
        outputs_kernel,
        grid_spec=pltpu.PrefetchScalarGridSpec(
            num_scalar_prefetch=1,
            grid=(chans // width,),
            in_specs=[
                rows,
                rows,
                rows,
                pl.BlockSpec((span, blocks, width), lambda n, p: (0, 0, n)),
                weight,
                weight,
                weight,
            ]
            + ([anywhere, anywhere, weight, weight] if before else []),
            out_specs=[rows, rows, weight, weight],
            scratch_shapes=[pltpu.VMEM((blocks * span, width), F32)],
        ),
        out_shape=[
            jax.ShapeDtypeStruct(x3.shape, BF),
            jax.ShapeDtypeStruct(x3.shape, BF),
            jax.ShapeDtypeStruct(w_in.shape, F32),
            jax.ShapeDtypeStruct(w_in.shape, F32),
        ],
        input_output_aliases={8: 0, 9: 1} if before else {},
        compiler_params=params(1),
        cost_estimate=cost(14 * size * width, 12 * size),
        name="outputs",
    )(partner, x3, ct3, gm3, second, w_in, w_gate, w_out, *before)


def exchange(array, d, parts):
    if d == 0:
        return array
    return lax.ppermute(array, "tm", [(i, i ^ d) for i in range(parts)])


def send_order(parts):
    return list(range(parts - 1, -1, -1))


def body(parts, inputs, kernel, w_in, w_gate, w_out, factor_a, factor_b, cotangent):
    rows, chans = inputs.shape
    inner = factor_a.shape[0]
    blocks = rows // inner
    span = inner // parts
    me = lax.axis_index("tm").astype(jnp.int32)
    me1 = me[None]
    partners = me ^ jnp.arange(parts, dtype=jnp.int32)
    x3 = inputs.reshape(blocks, inner, chans)
    kn3 = kernel.reshape(blocks, inner, chans)
    ct3 = cotangent.reshape(blocks, inner, chans)
    factor_at = factor_a.T
    order = send_order(parts)

    spread = (partners[:, None] * blocks + jnp.arange(blocks, dtype=jnp.int32)).reshape(-1)
    fb = jnp.take(jnp.take(factor_b, spread, axis=0), spread, axis=1)

    gs_in = [None] * parts
    for d in order:
        piece = grad_second_call(partners[d][None], x3, ct3, w_gate, w_out, span)
        gs_in[d] = exchange(piece, d, parts)
    tw_out = twisted_call(me1, x3, kn3, w_in, factor_at, parts)
    tw_in = [None] * parts
    for d in order:
        tw_in[d] = exchange(tw_out[d], d, parts)
    gt_out = grad_twisted_call(fb, gs_in)
    gt_in = [None] * parts
    for d in order:
        gt_in[d] = exchange(gt_out[d], d, parts)
    se_out, fb_term = second_call(fb.T, tw_in, gs_in)
    se_in = [None] * parts
    for d in order:
        se_in[d] = exchange(se_out[d], d, parts)
    gk, gm, fa_term, gwi_term = grad_mixed_call(
        me1, x3, kn3, w_in, factor_at, factor_a, gt_in
    )
    state = ()
    for d in order[-1:] + order[:-1]:
        state = outputs_call(
            partners[d][None], x3, ct3, gm, se_in[d], w_in, w_gate, w_out, state
        )
    outputs, grad_inputs, gwg_term, gwo_term = state

    fb_term = jnp.take(jnp.take(fb_term, spread, axis=0), spread, axis=1)
    token_scale = 1.0 / math.sqrt(N1 * N2)
    fa_piece = lax.psum_scatter(fa_term, "tm", scatter_dimension=0, tiled=True)
    fb_piece = lax.psum_scatter(fb_term, "tm", scatter_dimension=0, tiled=True)
    grad_factor_a = lax.psum(fa_piece, "tensor") / math.sqrt(N1 * D)
    grad_factor_b = lax.psum(fb_piece, "tensor") / math.sqrt(N2 * D)
    summed_in = lax.psum(gwi_term, "tm")
    summed_gate, summed_out = lax.psum((gwg_term, gwo_term), "tm")
    return (
        outputs.reshape(rows, chans),
        grad_inputs.reshape(rows, chans),
        gk.reshape(rows, chans),
        summed_in * token_scale,
        summed_gate * token_scale,
        summed_out * token_scale,
        grad_factor_a,
        grad_factor_b,
    )


def solution(mesh):
    return jax.shard_map(
        functools.partial(body, mesh.shape["tm"]),
        mesh=mesh,
        in_specs=(
            P("tm", "tensor"),
            P("tm", "tensor"),
            P("tensor", None, None),
            P("tensor", None, None),
            P("tensor", None, None),
            P(),
            P(),
            P("tm", "tensor"),
        ),
        out_specs=(
            P("tm", "tensor"),
            P("tm", "tensor"),
            P("tm", "tensor"),
            P("tensor", None, None),
            P("tensor", None, None),
            P("tensor", None, None),
            P("tm", None),
            P("tm", None),
        ),
        check_vma=False,
    )
```

time: 1210 us -> 799 us (0.66)
  local copies, waits for them, and re-layouts: 384 us -> 16.6 us
  waiting for transfers between devices: 147 us -> 453 us
  blocking collectives: 307 us -> 21.3 us
  matrix products: 259 us -> 0 us
  Pallas kernels: 0 us -> 246 us
  other arithmetic: 71.5 us -> 9.36 us
  starting transfers between devices: 11.5 us -> 30.4 us
    ppermute x0 -> x28, waiting for transfers between devices: none -> 349 us  [exchange(): return lax.ppermute(array, 'tm', [(i, i ^ d) for i in range(parts)])]
    all_to_all x2 -> x0, blocking collectives: 288 us -> none  [to_columns(): return lax.all_to_all(values, 'tm', split_axis=1, concat_axis=0, tiled=True)]
    dot_general x15 -> x0, matrix products: 259 us -> none  [the longest x3 61.6 us: mix_back(): jnp.einsum('tne,nbe->tnb', blocks, weight, preferred_element_type=jnp.flo...]
    convert_element_type x12 -> x0, local copies, waits for them, and re-layouts: 256 us -> none  [the longest x2 82 us: body(): second32 = second.astype(jnp.float32)]
    pallas_call x0 -> x20, Pallas kernels: none -> 246 us  [the longest x8 73 us: outputs_call(): pl.pallas_call(outputs_kernel, grid_spec=pltpu.PrefetchScalarGridSpec(num...]
    all_to_all x2 -> x0, waiting for transfers between devices: 96.1 us -> none  [to_rows(): return lax.all_to_all(values, 'tm', split_axis=0, concat_axis=1, tiled=True)]
    unnamed x29 -> x34, local copies, waits for them, and re-layouts: 94.6 us -> 7.96 us
    convert_element_type x4 -> x0, other arithmetic: 67.4 us -> none  [the longest x1 28.4 us: body(): grad_gate = (grad_gated * second32).astype(jnp.bfloat16)]
  transfers between devices with their start and end apart: 6 -> 32, of which waited for: 4 -> 9; matrix products, arithmetic and copies ran while one was open for 22% -> 3% of each run, Pallas kernels for 0% -> 30%
where the time goes in v1:
time: 799 us; the launch traced here: 791 us
  waiting for transfers between devices  453 us (57%)
  Pallas kernels  246 us (31%)
  starting transfers between devices  30.4 us (4%)
  blocking collectives  21.3 us (3%)
  local copies, waits for them, and re-layouts  16.6 us (2%)
  between operations  14.5 us (2%)
  other arithmetic  9.36 us (1%)
    ppermute x28, waiting for transfers between devices, exchange(): return lax.ppermute(array, 'tm', [(i, i ^ d) for i in range(parts)])  349 us
    pallas_call x8, Pallas kernels, outputs_call(): pl.pallas_call(outputs_kernel, grid_spec=pltpu.PrefetchScalarGridSpec(num...  73 us
    pallas_call x1, Pallas kernels, grad_mixed_call(): pl.pallas_call(grad_mixed_kernel, grid_spec=pltpu.PrefetchScalarGridSpec(...  51.3 us
    pallas_call x8, Pallas kernels, grad_second_call(): pl.pallas_call(grad_second_kernel, grid_spec=pltpu.PrefetchScalarGridSpec...  51.2 us
    pallas_call x1, Pallas kernels, twisted_call(): pl.pallas_call(twisted_kernel, grid_spec=pltpu.PrefetchScalarGridSpec(num...  37.6 us
    reduce_scatter x1, waiting for transfers between devices, body(): fa_piece = lax.psum_scatter(fa_term, 'tm', scatter_dimension=0, tiled=True)  35.3 us
    psum x1, waiting for transfers between devices, body(): grad_factor_a = lax.psum(fa_piece, 'tensor') / math.sqrt(N1 * D)  35 us
    psum x1, waiting for transfers between devices, body(): summed_in = lax.psum(gwi_term, 'tm')  32.4 us
  transfers between devices with their start and end apart: 32, of which 9 were waited for; matrix products, arithmetic and copies ran while one was open for 3% of the time, Pallas kernels for 30%

profile of v1, /device:TPU:0, one launch (start us, length us, event | category | flops | bytes accessed | tf_op | source)
XLA Modules:
  0.0 790.6 jit_solution(771386924941997840)
XLA Ops:
  7.9 6.3 grad_second.9
  14.7 6.4 grad_second.10
  21.1 2.5 collective-permute-start.1
  23.6 6.4 grad_second.11
  30.0 6.3 grad_second.12
  36.4 1.8 collective-permute-start.3
  38.2 6.4 grad_second.13
  44.6 2.1 copy.35
  46.6 6.3 grad_second.14
  53.0 37.6 %twisted.1 = (bf16[64,32,384]{2,1,0:T(8,128)(2,1)}, bf16[64,32,384]{2,1,0:T(8,128)(2,1)}, bf16[64,32,384]{2,1,0:T(8,128)(2,1)}, bf16[64,32,384]{2,1,0:T(8,128)(2...) custom-call(s32[1]{0:T(128)} %bitcast.3.me_ref, ...), custom_call_target="tpu_custom_call" | custom-call | flops 8053063680 | bytes 37748736 | tf_op jit(solution)/shard_map/twisted/pallas_call | solution.py:109
  90.6 2.6 collective-permute-start.5
  93.2 6.6 grad_second.15
  100.5 1.6 collective-permute-start.15
  102.1 71.8 %collective-permute-done.4.refs_5_.refs_13_ = bf16[64,32,384]{2,1,0:T(8,128)(2,1)} collective-permute-done((bf16[64,32,384]{2,1,0:T(8,128)(2,1)}, bf16[64,32,384]{2,1,0:T(8,128)(2,1)}, u32[]{:S(2)}, u32[]{:S(2)}) %collective-permute-start.4) | collective-permute-done | bytes 1572896 | tf_op jit(solution)/shard_map/ppermute | solution.py:337
  173.8 2.0 collective-permute-start.16
  175.9 1.5 collective-permute-start.17
  180.0 16.4 %collective-permute-done.15.refs_2_ = bf16[64,32,384]{2,1,0:T(8,128)(2,1)} collective-permute-done((bf16[64,32,384]{2,1,0:T(8,128)(2,1)}, bf16[64,32,384]{2,1,0:T(8,128)(2,1)}, u32[]{:S(2)}, u32[]{:S(2)}) %collective-permute-start.15) | collective-permute-done | bytes 1572896 | tf_op jit(solution)/shard_map/ppermute | solution.py:337
  199.1 6.5 grad_second.8.refs_0_.refs_8_
  205.6 14.1 %grad_twisted.1 = (bf16[64,32,384]{2,1,0:T(8,128)(2,1)}, bf16[64,32,384]{2,1,0:T(8,128)(2,1)}, bf16[64,32,384]{2,1,0:T(8,128)(2,1)}, bf16[64,32,384]{2,1,0:T(8,1...) custom-call(bf16[256,256]{1,0:T(8,128)(2,1)} %copy.37.fb_ref, ...), custom_call_target="tpu_custom_call" | custom-call | flops 3221225472 | bytes 25165824 | tf_op jit(solution)/shard_map/grad_twisted/pallas_call | solution.py:146
  219.6 9.8 %collective-permute-done.16.refs_3_ = bf16[64,32,384]{2,1,0:T(8,128)(2,1)} collective-permute-done((bf16[64,32,384]{2,1,0:T(8,128)(2,1)}, bf16[64,32,384]{2,1,0:T(8,128)(2,1)}, u32[]{:S(2)}, u32[]{:S(2)}) %collective-permute-start.16) | collective-permute-done | bytes 1572896 | tf_op jit(solution)/shard_map/ppermute | solution.py:337
  230.3 1.5 collective-permute-start.8
  231.8 80.6 %collective-permute-done.18.refs_5_ = bf16[64,32,384]{2,1,0:T(8,128)(2,1)} collective-permute-done((bf16[64,32,384]{2,1,0:T(8,128)(2,1)}, bf16[64,32,384]{2,1,0:T(8,128)(2,1)}, u32[]{:S(2)}, u32[]{:S(2)}) %collective-permute-start.18) | collective-permute-done | bytes 1572896 | tf_op jit(solution)/shard_map/ppermute | solution.py:337
  313.6 1.5 collective-permute-start.10
  315.9 18.4 %second.1 = (bf16[64,32,384]{2,1,0:T(8,128)(2,1)}, bf16[64,32,384]{2,1,0:T(8,128)(2,1)}, bf16[64,32,384]{2,1,0:T(8,128)(2,1)}, bf16[64,32,384]{2,1,0:T(8,128)(2,...) custom-call(bf16[256,256]{1,0:T(8,128)(2,1)} %broadcast_select_fusio, ...), custom_call_target="tpu_custom_call" | custom-call | flops 6442450944 | bytes 37748736 | tf_op jit(solution)/shard_map/second/pallas_call | solution.py:183
  334.4 1.5 collective-permute-start.12
  337.3 26.9 %collective-permute-done.9.rest_3_ = bf16[64,32,384]{2,1,0:T(8,128)(2,1)S(1)} collective-permute-done((bf16[64,32,384]{2,1,0:T(8,128)(2,1)}, bf16[64,32,384]{2,1,0:T(8,128)(2,1)S(1)}, u32[]{:S(2)}, u32[]{:S(2)}) %collective-permute-start.9) | collective-permute-done | bytes 1572896 | tf_op jit(solution)/shard_map/ppermute | solution.py:337
  365.6 1.8 collective-permute-start.27
  367.4 1.9 gather_fusion.2
  371.2 1.7 gather_fusion.3
  374.8 143.8 %collective-permute-done.11.rest_5_ = bf16[64,32,384]{2,1,0:T(8,128)(2,1)} collective-permute-done((bf16[64,32,384]{2,1,0:T(8,128)(2,1)}, bf16[64,32,384]{2,1,0:T(8,128)(2,1)}, u32[]{:S(2)}, u32[]{:S(2)}) %collective-permute-start.11) | collective-permute-done | bytes 1572896 | tf_op jit(solution)/shard_map/ppermute | solution.py:337
  520.8 1.5 collective-permute-start.24
  522.9 51.3 %grad_mixed.1 = (bf16[32,512,384]{2,1,0:T(8,128)(2,1)}, bf16[32,512,384]{2,1,0:T(8,128)(2,1)}, f32[512,512]{1,0:T(8,128)}, f32[3,128,128]{2,1,0:T(8,128)}) custom-call(s32[1]{0:T(128)} %bitcast.3.me_ref, bf16[32,512,384]{2,1,0:T(8,128)(2,1)} %bitcast.23, bf16[32,512,384]{2,1,0:T(8,128)(2,1)} %bitcast.54, bf16[3,128,128]{2,1,0:T(8,128)(2,1)} %wi_ref.19, ...), custom_call_target="tpu_custom_call" | custom-call | flops 22548578304 | bytes 62914560 | tf_op jit(solution)/shard_map/grad_mixed/pallas_call | solution.py:247
  574.2 9.2 %outputs.8 = (bf16[32,512,384]{2,1,0:T(8,128)(2,1)}, bf16[32,512,384]{2,1,0:T(8,128)(2,1)}, f32[3,128,128]{2,1,0:T(8,128)}, f32[3,128,128]{2,1,0:T(8,128)}) custom-call(s32[1]{0:T(128)} %get-tuple-element.155.p_ref, bf16[32,512,384]{2,1,0:T(8,128)(2,1)} %bitcast.24, bf16[32,512,384]{2,1,0:T(8,128)(2,1)} %bitcast.40, ...), custom_call_target="tpu_custom_call" | custom-call | flops 1409286144 | bytes 9437184 | tf_op jit(solution)/shard_map/outputs/pallas_call | solution.py:303
  583.4 9.1 %outputs.9 = (bf16[32,512,384]{2,1,0:T(8,128)(2,1)}, bf16[32,512,384]{2,1,0:T(8,128)(2,1)}, f32[3,128,128]{2,1,0:T(8,128)}, f32[3,128,128]{2,1,0:T(8,128)}) custom-call(s32[1]{0:T(128)} %get-tuple-element.149.p_ref, bf16[32,512,384]{2,1,0:T(8,128)(2,1)} %bitcast.25, bf16[32,512,384]{2,1,0:T(8,128)(2,1)} %bitcast.41, ...), custom_call_target="tpu_custom_call", output_to_operand_aliasing={{0}: (8, {}), {1}: (9, {})} | custom-call | flops 1409286144 | bytes 9437184 | tf_op jit(solution)/shard_map/outputs/pallas_call | solution.py:303
  592.5 9.0 %outputs.10 = (bf16[32,512,384]{2,1,0:T(8,128)(2,1)}, bf16[32,512,384]{2,1,0:T(8,128)(2,1)}, f32[3,128,128]{2,1,0:T(8,128)}, f32[3,128,128]{2,1,0:T(8,128)}) custom-call(s32[1]{0:T(128)} %get-tuple-element.150.p_ref, bf16[32,512,384]{2,1,0:T(8,128)(2,1)} %bitcast.26, bf16[32,512,384]{2,1,0:T(8,128)(2,1)} %bitcast.42, ...), custom_call_target="tpu_custom_call", output_to_operand_aliasing={{0}: (8, {}), {1}: (9, {})} | custom-call | flops 1409286144 | bytes 9437184 | tf_op jit(solution)/shard_map/outputs/pallas_call | solution.py:303
  601.6 9.1 %outputs.11 = (bf16[32,512,384]{2,1,0:T(8,128)(2,1)}, bf16[32,512,384]{2,1,0:T(8,128)(2,1)}, f32[3,128,128]{2,1,0:T(8,128)}, f32[3,128,128]{2,1,0:T(8,128)}) custom-call(s32[1]{0:T(128)} %get-tuple-element.151.p_ref, bf16[32,512,384]{2,1,0:T(8,128)(2,1)} %bitcast.27, bf16[32,512,384]{2,1,0:T(8,128)(2,1)} %bitcast.43, ...), custom_call_target="tpu_custom_call", output_to_operand_aliasing={{0}: (8, {}), {1}: (9, {})} | custom-call | flops 1409286144 | bytes 9437184 | tf_op jit(solution)/shard_map/outputs/pallas_call | solution.py:303
  610.7 9.3 %outputs.12 = (bf16[32,512,384]{2,1,0:T(8,128)(2,1)}, bf16[32,512,384]{2,1,0:T(8,128)(2,1)}, f32[3,128,128]{2,1,0:T(8,128)}, f32[3,128,128]{2,1,0:T(8,128)}) custom-call(s32[1]{0:T(128)} %get-tuple-element.152.p_ref, bf16[32,512,384]{2,1,0:T(8,128)(2,1)} %bitcast.28, bf16[32,512,384]{2,1,0:T(8,128)(2,1)} %bitcast.44, ...), custom_call_target="tpu_custom_call", output_to_operand_aliasing={{0}: (8, {}), {1}: (9, {})} | custom-call | flops 1409286144 | bytes 9437184 | tf_op jit(solution)/shard_map/outputs/pallas_call | solution.py:303
  621.1 9.1 %outputs.13 = (bf16[32,512,384]{2,1,0:T(8,128)(2,1)}, bf16[32,512,384]{2,1,0:T(8,128)(2,1)}, f32[3,128,128]{2,1,0:T(8,128)}, f32[3,128,128]{2,1,0:T(8,128)}) custom-call(s32[1]{0:T(128)} %get-tuple-element.153.p_ref, bf16[32,512,384]{2,1,0:T(8,128)(2,1)} %bitcast.29, bf16[32,512,384]{2,1,0:T(8,128)(2,1)} %bitcast.45, ...), custom_call_target="tpu_custom_call", output_to_operand_aliasing={{0}: (8, {}), {1}: (9, {})} | custom-call | flops 1409286144 | bytes 9437184 | tf_op jit(solution)/shard_map/outputs/pallas_call | solution.py:303
  631.4 9.1 %outputs.14 = (bf16[32,512,384]{2,1,0:T(8,128)(2,1)}, bf16[32,512,384]{2,1,0:T(8,128)(2,1)}, f32[3,128,128]{2,1,0:T(8,128)}, f32[3,128,128]{2,1,0:T(8,128)}) custom-call(s32[1]{0:T(128)} %get-tuple-element.154.p_ref, bf16[32,512,384]{2,1,0:T(8,128)(2,1)} %bitcast.30, bf16[32,512,384]{2,1,0:T(8,128)(2,1)} %bitcast.46, ...), custom_call_target="tpu_custom_call", output_to_operand_aliasing={{0}: (8, {}), {1}: (9, {})} | custom-call | flops 1409286144 | bytes 9437184 | tf_op jit(solution)/shard_map/outputs/pallas_call | solution.py:303
  641.7 9.1 %outputs.15 = (bf16[32,512,384]{2,1,0:T(8,128)(2,1)}, bf16[32,512,384]{2,1,0:T(8,128)(2,1)}, f32[3,128,128]{2,1,0:T(8,128)}, f32[3,128,128]{2,1,0:T(8,128)}) custom-call(s32[1]{0:T(128)} %get-tuple-element.156.p_ref, bf16[32,512,384]{2,1,0:T(8,128)(2,1)} %bitcast.31, bf16[32,512,384]{2,1,0:T(8,128)(2,1)} %bitcast.47, ...), custom_call_target="tpu_custom_call", output_to_operand_aliasing={{0}: (8, {}), {1}: (9, {})} | custom-call | flops 1409286144 | bytes 9437184 | tf_op jit(solution)/shard_map/outputs/pallas_call | solution.py:303
  652.5 21.3 %psum.39 = f32[32,256]{0,1:T(8,128)S(1)} all-reduce(f32[32,256]{0,1:T(8,128)S(1)} %copy.41), channel_id=1, replica_groups=mesh['tm'=8,'tensor'=4] {'tensor'}, use_global_device_ids=true, to_apply=%region_6.7 | all-reduce | flops 8192 | bytes 65536 | tf_op jit(solution)/shard_map/psum | solution.py:392
  674.5 32.4 %all-reduce.6.cloned.1.call-done = (f32[3,128,128]{2,1,0:T(8,128)}, f32[3,128,128]{2,1,0:T(8,128)}, f32[3,128,128]{2,1,0:T(8,128)}) async-done(((f32[3,128,128]{2,1,0:T(8,128)}, f32[3,128,128]{2,1,0:T(8,128)}, f32[3,128,128]{2,1,0:T(8,128)}), (f32[3,128,128]{2,1,0:T(8,128)}, f32[3,128,128]{2,1,0:T(8,128)}, f32[3,128,128]{2,1,0:T(8,128)})) %all-reduce.6.cloned.1.call-update) | async-done | bytes 589840 | tf_op jit(solution)/shard_map/psum | solution.py:393
  706.8 1.6 broadcast_multiply_fusion.2
  708.4 1.6 broadcast_multiply_fusion.1
  710.1 35.3 %reduce-scatter.5.cloned.1.call-done = f32[64,512]{1,0:T(8,128)} async-done(((f32[512,512]{1,0:T(8,128)}), f32[64,512]{1,0:T(8,128)}) %reduce-scatter.5.cloned.1.call-update) | async-done | bytes 131088 | tf_op jit(solution)/shard_map/reduce_scatter | solution.py:389
  745.4 1.6 broadcast_multiply_fusion
  747.0 35.0 %all-reduce.4.cloned.1.call-done = f32[64,512]{1,0:T(8,128)} async-done(((f32[64,512]{1,0:T(8,128)}), f32[64,512]{1,0:T(8,128)}) %all-reduce.4.cloned.1.call-update) | async-done | bytes 131088 | tf_op jit(solution)/shard_map/psum | solution.py:391
  782.0 1.6 broadcast_multiply_fusion.4
  (100 shorter events, 25.2 us)
Async XLA Ops:
  7.2 171.7 %copy-start = (bf16[256,256]{1,0:T(8,128)(2,1)S(1)}, bf16[256,256]{1,0:T(8,128)(2,1)}, u32[]{:S(2)}) copy-start(bf16[256,256]{1,0:T(8,128)(2,1)} %param.14) | copy-start | bytes 393220
  7.2 644.4 %reduce-scatter.7.cloned.1.call-start = ((), (), s32[]{:S(2)}) async-start(), calls=%async_computation.4 | async-start | bytes 294912
  14.2 76.3 %collective-permute-start = (bf16[64,32,384]{2,1,0:T(8,128)(2,1)}, bf16[64,32,384]{2,1,0:T(8,128)(2,1)S(1)}, u32[]{:S(2)}, u32[]{:S(2)}) collective-permute-start(bf16[64,32,384]{2,1,0:T(8,128)(2,1)} %grad_second.9), channel_id=1, source_target_pairs={{0,4},{4,0},{8,12},{12,8},{16,20},{20,16},{24,28},{28,24},{1,5},{5... | collective-permute-start | bytes 4718600 | tf_op jit(solution)/shard_map/ppermute | solution.py:337
  21.1 78.8 %collective-permute-start.1 = (bf16[64,32,384]{2,1,0:T(8,128)(2,1)}, bf16[64,32,384]{2,1,0:T(8,128)(2,1)S(1)}, u32[]{:S(2)}, u32[]{:S(2)}) collective-permute-start(bf16[64,32,384]{2,1,0:T(8,128)(2,1)} %grad_second.10), channel_id=1, source_target_pairs={{0,8},{4,12},{8,0},{12,4},{16,24},{20,28},{24,16},{28,20},{1,9},{5... | collective-permute-start | bytes 4718600 | tf_op jit(solution)/shard_map/ppermute | solution.py:337
  29.9 70.4 %collective-permute-start.2 = (bf16[64,32,384]{2,1,0:T(8,128)(2,1)}, bf16[64,32,384]{2,1,0:T(8,128)(2,1)}, u32[]{:S(2)}, u32[]{:S(2)}) collective-permute-start(bf16[64,32,384]{2,1,0:T(8,128)(2,1)} %grad_second.11), channel_id=1, source_target_pairs={{0,12},{4,8},{8,4},{12,0},{16,28},{20,24},{24,20},{28,16},{1,13},{... | collective-permute-start | bytes 4718600 | tf_op jit(solution)/shard_map/ppermute | solution.py:337
  36.4 64.1 %collective-permute-start.3 = (bf16[64,32,384]{2,1,0:T(8,128)(2,1)}, bf16[64,32,384]{2,1,0:T(8,128)(2,1)}, u32[]{:S(2)}, u32[]{:S(2)}) collective-permute-start(bf16[64,32,384]{2,1,0:T(8,128)(2,1)} %grad_second.12), channel_id=1, source_target_pairs={{0,16},{4,20},{8,24},{12,28},{16,0},{20,4},{24,8},{28,12},{1,17},{... | collective-permute-start | bytes 4718600 | tf_op jit(solution)/shard_map/ppermute | solution.py:337
  44.6 129.3 %collective-permute-start.4 = (bf16[64,32,384]{2,1,0:T(8,128)(2,1)}, bf16[64,32,384]{2,1,0:T(8,128)(2,1)}, u32[]{:S(2)}, u32[]{:S(2)}) collective-permute-start(bf16[64,32,384]{2,1,0:T(8,128)(2,1)} %grad_second.13), channel_id=1, source_target_pairs={{0,20},{4,16},{8,28},{12,24},{16,4},{20,0},{24,12},{28,8},{1,21},{... | collective-permute-start | bytes 4718600 | tf_op jit(solution)/shard_map/ppermute | solution.py:337
  53.0 37.6 %copy-start.5 = (bf16[64,32,384]{2,1,0:T(8,128)(2,1)S(1)}, bf16[64,32,384]{2,1,0:T(8,128)(2,1)}, u32[]{:S(2)}) copy-start(bf16[64,32,384]{2,1,0:T(8,128)(2,1)} %grad_second.14) | copy-start | bytes 4718596
  90.6 9.3 %copy-start.2 = (bf16[64,32,384]{2,1,0:T(8,128)(2,1)}, bf16[64,32,384]{2,1,0:T(8,128)(2,1)S(1)}, u32[]{:S(2)}) copy-start(bf16[64,32,384]{2,1,0:T(8,128)(2,1)S(1)} %collective-permute-done.refs_1_.refs_9_) | copy-start | bytes 4718596
  90.6 85.3 %collective-permute-start.5 = (bf16[64,32,384]{2,1,0:T(8,128)(2,1)S(1)}, bf16[64,32,384]{2,1,0:T(8,128)(2,1)}, u32[]{:S(2)}, u32[]{:S(2)}) collective-permute-start(bf16[64,32,384]{2,1,0:T(8,128)(2,1)S(1)} %copy-done.5), channel_id=1, source_target_pairs={{0,24},{4,28},{8,16},{12,20},{16,8},{20,12},{24,0},{28,4},{1,25},{... | collective-permute-start | bytes 4718600 | tf_op jit(solution)/shard_map/ppermute | solution.py:337
  93.2 7.1 copy-start.14
  99.9 98.5 %copy-start.3 = (bf16[64,32,384]{2,1,0:T(8,128)(2,1)}, bf16[64,32,384]{2,1,0:T(8,128)(2,1)S(1)}, u32[]{:S(2)}) copy-start(bf16[64,32,384]{2,1,0:T(8,128)(2,1)S(1)} %collective-permute-done.1.refs_2_.refs_10_) | copy-start | bytes 4718596
  99.9 77.5 %collective-permute-start.6 = (bf16[64,32,384]{2,1,0:T(8,128)(2,1)}, bf16[64,32,384]{2,1,0:T(8,128)(2,1)S(1)}, u32[]{:S(2)}, u32[]{:S(2)}) collective-permute-start(bf16[64,32,384]{2,1,0:T(8,128)(2,1)} %grad_second.15), channel_id=1, source_target_pairs={{0,28},{4,24},{8,20},{12,16},{16,12},{20,8},{24,4},{28,0},{1,29},{... | collective-permute-start | bytes 4718600 | tf_op jit(solution)/shard_map/ppermute | solution.py:337
  100.3 77.1 %collective-permute-start.14 = (bf16[64,32,384]{2,1,0:T(8,128)(2,1)S(1)}, bf16[64,32,384]{2,1,0:T(8,128)(2,1)}, u32[]{:S(2)}, u32[]{:S(2)}) collective-permute-start(bf16[64,32,384]{2,1,0:T(8,128)(2,1)S(1)} %copy-done.14), channel_id=1, source_target_pairs={{0,4},{4,0},{8,12},{12,8},{16,20},{20,16},{24,28},{28,24},{1,5},{5... | collective-permute-start | bytes 4718600 | tf_op jit(solution)/shard_map/ppermute | solution.py:337
  100.5 96.0 %collective-permute-start.15 = (bf16[64,32,384]{2,1,0:T(8,128)(2,1)}, bf16[64,32,384]{2,1,0:T(8,128)(2,1)}, u32[]{:S(2)}, u32[]{:S(2)}) collective-permute-start(bf16[64,32,384]{2,1,0:T(8,128)(2,1)} %get-tuple-element.80), channel_id=1, source_target_pairs={{0,8},{4,12},{8,0},{12,4},{16,24},{20,28},{24,16},{28,20},{1,9},{5... | collective-permute-start | bytes 4718600 | tf_op jit(solution)/shard_map/ppermute | solution.py:337
  173.8 55.6 %collective-permute-start.16 = (bf16[64,32,384]{2,1,0:T(8,128)(2,1)}, bf16[64,32,384]{2,1,0:T(8,128)(2,1)}, u32[]{:S(2)}, u32[]{:S(2)}) collective-permute-start(bf16[64,32,384]{2,1,0:T(8,128)(2,1)} %get-tuple-element.81), channel_id=1, source_target_pairs={{0,12},{4,8},{8,4},{12,0},{16,28},{20,24},{24,20},{28,16},{1,13},{... | collective-permute-start | bytes 4718600 | tf_op jit(solution)/shard_map/ppermute | solution.py:337
  175.9 54.4 %collective-permute-start.17 = (bf16[64,32,384]{2,1,0:T(8,128)(2,1)}, bf16[64,32,384]{2,1,0:T(8,128)(2,1)}, u32[]{:S(2)}, u32[]{:S(2)}) collective-permute-start(bf16[64,32,384]{2,1,0:T(8,128)(2,1)} %get-tuple-element.82), channel_id=1, source_target_pairs={{0,16},{4,20},{8,24},{12,28},{16,0},{20,4},{24,8},{28,12},{1,17},{... | collective-permute-start | bytes 4718600 | tf_op jit(solution)/shard_map/ppermute | solution.py:337
  177.4 20.9 %copy-start.4 = (bf16[64,32,384]{2,1,0:T(8,128)(2,1)}, bf16[64,32,384]{2,1,0:T(8,128)(2,1)S(1)}, u32[]{:S(2)}) copy-start(bf16[64,32,384]{2,1,0:T(8,128)(2,1)S(1)} %collective-permute-done.6.refs_7_.refs_15_) | copy-start | bytes 4718596
  177.4 135.0 %collective-permute-start.18 = (bf16[64,32,384]{2,1,0:T(8,128)(2,1)}, bf16[64,32,384]{2,1,0:T(8,128)(2,1)}, u32[]{:S(2)}, u32[]{:S(2)}) collective-permute-start(bf16[64,32,384]{2,1,0:T(8,128)(2,1)} %get-tuple-element.83), channel_id=1, source_target_pairs={{0,20},{4,16},{8,28},{12,24},{16,4},{20,0},{24,12},{28,8},{1,21},{... | collective-permute-start | bytes 4718600 | tf_op jit(solution)/shard_map/ppermute | solution.py:337
  177.4 136.2 %collective-permute-start.19 = (bf16[64,32,384]{2,1,0:T(8,128)(2,1)}, bf16[64,32,384]{2,1,0:T(8,128)(2,1)}, u32[]{:S(2)}, u32[]{:S(2)}) collective-permute-start(bf16[64,32,384]{2,1,0:T(8,128)(2,1)} %get-tuple-element.84), channel_id=1, source_target_pairs={{0,24},{4,28},{8,16},{12,20},{16,8},{20,12},{24,0},{28,4},{1,25},{... | collective-permute-start | bytes 4718600 | tf_op jit(solution)/shard_map/ppermute | solution.py:337
  196.4 119.5 %collective-permute-start.20 = (bf16[64,32,384]{2,1,0:T(8,128)(2,1)}, bf16[64,32,384]{2,1,0:T(8,128)(2,1)}, u32[]{:S(2)}, u32[]{:S(2)}) collective-permute-start(bf16[64,32,384]{2,1,0:T(8,128)(2,1)} %get-tuple-element.85), channel_id=1, source_target_pairs={{0,28},{4,24},{8,20},{12,16},{16,12},{20,8},{24,4},{28,0},{1,29},{... | collective-permute-start | bytes 4718600 | tf_op jit(solution)/shard_map/ppermute | solution.py:337
  229.4 104.9 %collective-permute-start.7 = (bf16[64,32,384]{2,1,0:T(8,128)(2,1)}, bf16[64,32,384]{2,1,0:T(8,128)(2,1)S(1)}, u32[]{:S(2)}, u32[]{:S(2)}) collective-permute-start(bf16[64,32,384]{2,1,0:T(8,128)(2,1)} %get-tuple-element.70), channel_id=1, source_target_pairs={{0,4},{4,0},{8,12},{12,8},{16,20},{20,16},{24,28},{28,24},{1,5},{5... | collective-permute-start | bytes 4718600 | tf_op jit(solution)/shard_map/ppermute | solution.py:337
  230.3 105.6 %collective-permute-start.8 = (bf16[64,32,384]{2,1,0:T(8,128)(2,1)}, bf16[64,32,384]{2,1,0:T(8,128)(2,1)S(1)}, u32[]{:S(2)}, u32[]{:S(2)}) collective-permute-start(bf16[64,32,384]{2,1,0:T(8,128)(2,1)} %get-tuple-element.71), channel_id=1, source_target_pairs={{0,8},{4,12},{8,0},{12,4},{16,24},{20,28},{24,16},{28,20},{1,9},{5... | collective-permute-start | bytes 4718600 | tf_op jit(solution)/shard_map/ppermute | solution.py:337
  312.4 51.8 %collective-permute-start.9 = (bf16[64,32,384]{2,1,0:T(8,128)(2,1)}, bf16[64,32,384]{2,1,0:T(8,128)(2,1)S(1)}, u32[]{:S(2)}, u32[]{:S(2)}) collective-permute-start(bf16[64,32,384]{2,1,0:T(8,128)(2,1)} %get-tuple-element.72), channel_id=1, source_target_pairs={{0,12},{4,8},{8,4},{12,0},{16,28},{20,24},{24,20},{28,16},{1,13},{... | collective-permute-start | bytes 4718600 | tf_op jit(solution)/shard_map/ppermute | solution.py:337
  313.6 52.0 %collective-permute-start.10 = (bf16[64,32,384]{2,1,0:T(8,128)(2,1)}, bf16[64,32,384]{2,1,0:T(8,128)(2,1)}, u32[]{:S(2)}, u32[]{:S(2)}) collective-permute-start(bf16[64,32,384]{2,1,0:T(8,128)(2,1)} %get-tuple-element.73), channel_id=1, source_target_pairs={{0,16},{4,20},{8,24},{12,28},{16,0},{20,4},{24,8},{28,12},{1,17},{... | collective-permute-start | bytes 4718600 | tf_op jit(solution)/shard_map/ppermute | solution.py:337
  315.9 202.7 %collective-permute-start.11 = (bf16[64,32,384]{2,1,0:T(8,128)(2,1)}, bf16[64,32,384]{2,1,0:T(8,128)(2,1)}, u32[]{:S(2)}, u32[]{:S(2)}) collective-permute-start(bf16[64,32,384]{2,1,0:T(8,128)(2,1)} %get-tuple-element.74), channel_id=1, source_target_pairs={{0,20},{4,16},{8,28},{12,24},{16,4},{20,0},{24,12},{28,8},{1,21},{... | collective-permute-start | bytes 4718600 | tf_op jit(solution)/shard_map/ppermute | solution.py:337
  334.4 33.0 %copy-start.11 = (bf16[64,32,384]{2,1,0:T(8,128)(2,1)}, bf16[64,32,384]{2,1,0:T(8,128)(2,1)S(1)}, u32[]{:S(2)}) copy-start(bf16[64,32,384]{2,1,0:T(8,128)(2,1)S(1)} %collective-permute-done.7.rest_1_) | copy-start | bytes 4718596
  334.4 185.0 %collective-permute-start.12 = (bf16[64,32,384]{2,1,0:T(8,128)(2,1)}, bf16[64,32,384]{2,1,0:T(8,128)(2,1)}, u32[]{:S(2)}, u32[]{:S(2)}) collective-permute-start(bf16[64,32,384]{2,1,0:T(8,128)(2,1)} %get-tuple-element.75), channel_id=1, source_target_pairs={{0,24},{4,28},{8,16},{12,20},{16,8},{20,12},{24,0},{28,4},{1,25},{... | collective-permute-start | bytes 4718600 | tf_op jit(solution)/shard_map/ppermute | solution.py:337
  335.9 31.5 %copy-start.12 = (bf16[64,32,384]{2,1,0:T(8,128)(2,1)}, bf16[64,32,384]{2,1,0:T(8,128)(2,1)S(1)}, u32[]{:S(2)}) copy-start(bf16[64,32,384]{2,1,0:T(8,128)(2,1)S(1)} %collective-permute-done.8.rest_2_) | copy-start | bytes 4718596
  335.9 184.7 %collective-permute-start.13 = (bf16[64,32,384]{2,1,0:T(8,128)(2,1)}, bf16[64,32,384]{2,1,0:T(8,128)(2,1)}, u32[]{:S(2)}, u32[]{:S(2)}) collective-permute-start(bf16[64,32,384]{2,1,0:T(8,128)(2,1)} %get-tuple-element.76), channel_id=1, source_target_pairs={{0,28},{4,24},{8,20},{12,16},{16,12},{20,8},{24,4},{28,0},{1,29},{... | collective-permute-start | bytes 4718600 | tf_op jit(solution)/shard_map/ppermute | solution.py:337
  364.2 3.2 copy-start.13
  364.2 156.6 %collective-permute-start.26 = (bf16[64,32,384]{2,1,0:T(8,128)(2,1)}, bf16[64,32,384]{2,1,0:T(8,128)(2,1)S(1)}, u32[]{:S(2)}, u32[]{:S(2)}) collective-permute-start(bf16[64,32,384]{2,1,0:T(8,128)(2,1)} %get-tuple-element.91), channel_id=1, source_target_pairs={{0,24},{4,28},{8,16},{12,20},{16,8},{20,12},{24,0},{28,4},{1,25},{... | collective-permute-start | bytes 4718600 | tf_op jit(solution)/shard_map/ppermute | solution.py:337
  365.6 156.7 %collective-permute-start.27 = (bf16[64,32,384]{2,1,0:T(8,128)(2,1)}, bf16[64,32,384]{2,1,0:T(8,128)(2,1)S(1)}, u32[]{:S(2)}, u32[]{:S(2)}) collective-permute-start(bf16[64,32,384]{2,1,0:T(8,128)(2,1)} %get-tuple-element.92), channel_id=1, source_target_pairs={{0,28},{4,24},{8,20},{12,16},{16,12},{20,8},{24,4},{28,0},{1,29},{... | collective-permute-start | bytes 4718600 | tf_op jit(solution)/shard_map/ppermute | solution.py:337
  374.8 332.0 %all-reduce.6.cloned.1.call-start = ((), (), s32[]{:S(2)}) async-start(), calls=%async_computation.5 | async-start | bytes 1179648 | tf_op jit(solution)/shard_map/psum | solution.py:393
  518.6 121.9 %collective-permute-start.21 = (bf16[64,32,384]{2,1,0:T(8,128)(2,1)}, bf16[64,32,384]{2,1,0:T(8,128)(2,1)S(1)}, u32[]{:S(2)}, u32[]{:S(2)}) collective-permute-start(bf16[64,32,384]{2,1,0:T(8,128)(2,1)} %get-tuple-element.86), channel_id=1, source_target_pairs={{0,4},{4,0},{8,12},{12,8},{16,20},{20,16},{24,28},{28,24},{1,5},{5... | collective-permute-start | bytes 4718600 | tf_op jit(solution)/shard_map/ppermute | solution.py:337
  519.4 110.8 %collective-permute-start.22 = (bf16[64,32,384]{2,1,0:T(8,128)(2,1)}, bf16[64,32,384]{2,1,0:T(8,128)(2,1)S(1)}, u32[]{:S(2)}, u32[]{:S(2)}) collective-permute-start(bf16[64,32,384]{2,1,0:T(8,128)(2,1)} %get-tuple-element.87), channel_id=1, source_target_pairs={{0,8},{4,12},{8,0},{12,4},{16,24},{20,28},{24,16},{28,20},{1,9},{5... | collective-permute-start | bytes 4718600 | tf_op jit(solution)/shard_map/ppermute | solution.py:337
  520.6 99.4 %collective-permute-start.23 = (bf16[64,32,384]{2,1,0:T(8,128)(2,1)}, bf16[64,32,384]{2,1,0:T(8,128)(2,1)S(1)}, u32[]{:S(2)}, u32[]{:S(2)}) collective-permute-start(bf16[64,32,384]{2,1,0:T(8,128)(2,1)} %get-tuple-element.88), channel_id=1, source_target_pairs={{0,12},{4,8},{8,4},{12,0},{16,28},{20,24},{24,20},{28,16},{1,13},{... | collective-permute-start | bytes 4718600 | tf_op jit(solution)/shard_map/ppermute | solution.py:337
  520.8 53.5 %copy-start.8 = (bf16[64,32,384]{2,1,0:T(8,128)(2,1)}, bf16[64,32,384]{2,1,0:T(8,128)(2,1)S(1)}, u32[]{:S(2)}) copy-start(bf16[64,32,384]{2,1,0:T(8,128)(2,1)S(1)} %collective-permute-done.26.se_ref) | copy-start | bytes 4718596
  520.8 89.9 %collective-permute-start.24 = (bf16[64,32,384]{2,1,0:T(8,128)(2,1)}, bf16[64,32,384]{2,1,0:T(8,128)(2,1)}, u32[]{:S(2)}, u32[]{:S(2)}) collective-permute-start(bf16[64,32,384]{2,1,0:T(8,128)(2,1)} %get-tuple-element.89), channel_id=1, source_target_pairs={{0,16},{4,20},{8,24},{12,28},{16,0},{20,4},{24,8},{28,12},{1,17},{... | collective-permute-start | bytes 4718600 | tf_op jit(solution)/shard_map/ppermute | solution.py:337
  522.3 51.9 %copy-start.10 = (bf16[64,32,384]{2,1,0:T(8,128)(2,1)}, bf16[64,32,384]{2,1,0:T(8,128)(2,1)S(1)}, u32[]{:S(2)}) copy-start(bf16[64,32,384]{2,1,0:T(8,128)(2,1)S(1)} %collective-permute-done.27.se_ref) | copy-start | bytes 4718596
  522.3 79.3 %collective-permute-start.25 = (bf16[64,32,384]{2,1,0:T(8,128)(2,1)}, bf16[64,32,384]{2,1,0:T(8,128)(2,1)}, u32[]{:S(2)}, u32[]{:S(2)}) collective-permute-start(bf16[64,32,384]{2,1,0:T(8,128)(2,1)} %get-tuple-element.90), channel_id=1, source_target_pairs={{0,20},{4,16},{8,28},{12,24},{16,4},{20,0},{24,12},{28,8},{1,21},{... | collective-permute-start | bytes 4718600 | tf_op jit(solution)/shard_map/ppermute | solution.py:337
  620.0 1.2 copy-start.9
  630.2 1.2 copy-start.7
  640.5 1.1 copy-start.6
  650.8 94.6 %reduce-scatter.5.cloned.1.call-start = ((), (), s32[]{:S(2)}) async-start(), calls=%async_computation.2 | async-start | bytes 1179648 | tf_op jit(solution)/shard_map/reduce_scatter | solution.py:389
  650.8 132.7 %copy-start.1 = (bf16[256,256]{1,0:T(8,128)(2,1)S(1)}, bf16[256,256]{1,0:T(8,128)(2,1)}, u32[]{:S(2)}) copy-start(bf16[256,256]{1,0:T(8,128)(2,1)} %param.14) | copy-start | bytes 393220
  651.5 130.5 %all-reduce.4.cloned.1.call-start = ((), (), s32[]{:S(2)}) async-start(), calls=%async_computation.3 | async-start | bytes 262144 | tf_op jit(solution)/shard_map/psum | solution.py:391
Sparse Core Ops, SparseCore 0:
  374.9 137.6 reduce-scatter.6
  650.9 55.8 all-reduce.5
  710.0 35.3 reduce-scatter.4
  747.5 34.4 all-reduce.3

commit v2 on v1

--- a/solution.py
+++ b/solution.py
@@ -14,6 +14,7 @@
 BF = jnp.bfloat16
 F32 = jnp.float32
 VMEM_LIMIT = 56 * 1024 * 1024
+COST = 0.1
 
 
 def dot(left, right):
@@ -26,6 +27,13 @@
 
 def dot_tn(left, right):
     return lax.dot_general(left, right, (((0,), (0,)), ((), ())), preferred_element_type=F32)
+
+
+def diagonal(first, second):
+    zero = jnp.zeros_like(first)
+    return jnp.concatenate(
+        [jnp.concatenate([first, zero], axis=1), jnp.concatenate([zero, second], axis=1)], axis=0
+    )
 
 
 def params(dims):
@@ -35,7 +43,7 @@
 
 
 def cost(flops, nbytes):
-    return pl.CostEstimate(flops=int(flops), bytes_accessed=int(nbytes), transcendentals=0)
+    return pl.CostEstimate(flops=int(flops * COST), bytes_accessed=int(nbytes * COST), transcendentals=0)
 
 
 def stack_rows(pieces):
@@ -44,41 +52,49 @@
     return jnp.concatenate([p.astype(F32) for p in pieces], axis=0).astype(BF)
 
 
-def grad_second_kernel(p_ref, x_ref, ct_ref, wg_ref, wo_ref, out_ref, scr):
-    blocks, span, width = x_ref.shape
-    x = x_ref[...].reshape(blocks * span, width)
-    ct = ct_ref[...].reshape(blocks * span, width)
-    scr[...] = dot_nt(ct, wo_ref[0]) * dot(x, wg_ref[0])
-    for k in range(span):
-        out_ref[k] = scr[pl.ds(k, blocks, stride=span), :].astype(BF)
-
-
-def grad_second_call(partner, x3, ct3, w_gate, w_out, span):
+def grad_second_kernel(p_ref, x_ref, ct_ref, wg_ref, wo_ref, *rest):
+    out_ref = rest[-1]
+    blocks, span, chans = x_ref.shape
+    width = wg_ref.shape[1]
+    rows = blocks * span
+    for n in range(chans // width):
+        lanes = slice(n * width, (n + 1) * width)
+        x = x_ref[:, :, lanes].reshape(rows, width)
+        ct = ct_ref[:, :, lanes].reshape(rows, width)
+        both = dot(jnp.concatenate([x, ct], axis=1), diagonal(wg_ref[n], wo_ref[n].T))
+        value = (both[:, :width] * both[:, width:]).astype(BF)
+        out_ref[:, :, lanes] = jnp.swapaxes(value.reshape(blocks, span, width), 0, 1)
+
+
+def grad_second_call(partner, x3, ct3, w_gate, w_out, span, after):
     blocks, inner, chans = x3.shape
     width = w_gate.shape[1]
-    rows = pl.BlockSpec((blocks, span, width), lambda n, p: (0, p[0], n))
-    weight = pl.BlockSpec((1, width, width), lambda n, p: (n, 0, 0))
+    some = min(blocks, 16)
+    rows = pl.BlockSpec((some, span, chans), lambda i, p: (i, p[0], 0))
+    weight = pl.BlockSpec(w_gate.shape, lambda i, p: (0, 0, 0))
+    anywhere = pl.BlockSpec(memory_space=pl.ANY)
     size = blocks * span * chans
     return pl.pallas_call(
         grad_second_kernel,
         grid_spec=pltpu.PrefetchScalarGridSpec(
             num_scalar_prefetch=1,
-            grid=(chans // width,),
-            in_specs=[rows, rows, weight, weight],
-            out_specs=pl.BlockSpec((span, blocks, width), lambda n, p: (0, 0, n)),
-            scratch_shapes=[pltpu.VMEM((blocks * span, width), F32)],
+            grid=(blocks // some,),
+            in_specs=[rows, rows, weight, weight] + [anywhere] * len(after),
+            out_specs=pl.BlockSpec((span, some, chans), lambda i, p: (0, i, 0)),
         ),
         out_shape=jax.ShapeDtypeStruct((span, blocks, chans), BF),
         compiler_params=params(1),
         cost_estimate=cost(4 * size * width, 6 * size),
         name="grad_second",
-    )(partner, x3, ct3, w_gate, w_out)
-
-
-def twisted_kernel(me_ref, x_ref, kn_ref, wi_ref, at_ref, *rest):
-    outs, scr = rest[:-1], rest[-1]
+    )(partner, x3, ct3, w_gate, w_out, *after)
+
+
+def twisted_kernel(dist, me_ref, x_ref, kn_ref, wi_ref, at_ref, *rest):
     some, inner, width = x_ref.shape
-    span, blocks, _ = outs[0].shape
+    scr = rest[-1]
+    blocks = scr.shape[0] // inner
+    outs = rest[-1 - len(dist) : -1]
+    span = inner // len(dist)
     step = pl.program_id(1)
     mixed = dot(x_ref[...].reshape(some * inner, width), wi_ref[0]).astype(BF)
     for q in range(0, some, 2):
@@ -92,13 +108,14 @@
 
     @pl.when(step == pl.num_programs(1) - 1)
     def _():
-        for d, out in enumerate(outs):
+        for d, out in zip(dist, outs):
             first_row = pl.multiple_of((me_ref[0] ^ d) * (span * blocks), span * blocks)
             piece = scr[pl.ds(first_row, span * blocks), :]
             out[...] = piece.reshape(span, blocks, width).astype(BF)
 
 
-def twisted_call(me, x3, kn3, w_in, factor_at, parts):
+def twisted_call(me, x3, kn3, w_in, factor_at, dist, after):
+    parts = len(dist)
     blocks, inner, chans = x3.shape
     width = w_in.shape[1]
     span = inner // parts
@@ -107,7 +124,7 @@
     out = pl.BlockSpec((span, blocks, width), lambda n, i, m: (0, 0, n))
     size = blocks * inner * chans
     return pl.pallas_call(
-        twisted_kernel,
+        functools.partial(twisted_kernel, dist),
         grid_spec=pltpu.PrefetchScalarGridSpec(
             num_scalar_prefetch=1,
             grid=(chans // width, blocks // some),
@@ -116,7 +133,8 @@
                 rows,
                 pl.BlockSpec((1, width, width), lambda n, i, m: (n, 0, 0)),
                 pl.BlockSpec((inner, inner), lambda n, i, m: (0, 0)),
-            ],
+            ]
+            + [pl.BlockSpec(memory_space=pl.ANY)] * len(after),
             out_specs=[out] * parts,
             scratch_shapes=[pltpu.VMEM((inner * blocks, width), F32)],
         ),
@@ -124,7 +142,7 @@
         compiler_params=params(2),
         cost_estimate=cost(2 * size * (width + inner), 6 * size),
         name="twisted",
-    )(me, x3, kn3, w_in, factor_at)
+    )(me, x3, kn3, w_in, factor_at, *after)
 
 
 def grad_twisted_kernel(fb_ref, *refs):
@@ -194,7 +212,7 @@
     return result[:-1], result[-1]
 
 
-def grad_mixed_kernel(me_ref, x_ref, kn_ref, wi_ref, at_ref, a_ref, *rest):
+def grad_mixed_kernel(dist, me_ref, x_ref, kn_ref, wi_ref, at_ref, a_ref, *rest):
     gts = rest[:-5]
     gk_ref, gm_ref, fag, gwi, scr = rest[-5:]
     some, inner, width = x_ref.shape
@@ -204,7 +222,7 @@
     @pl.when(step == 0)
     def _():
         gwi[...] = jnp.zeros_like(gwi)
-        for d, ref in enumerate(gts):
+        for d, ref in zip(dist, gts):
             first_row = pl.multiple_of((me_ref[0] ^ d) * (span * blocks), span * blocks)
             scr[pl.ds(first_row, span * blocks), :] = (
                 ref[...].astype(F32).reshape(span * blocks, width)
@@ -234,7 +252,7 @@
     gwi[0] += dot_tn(x, gm_ref[...].reshape(some * inner, width))
 
 
-def grad_mixed_call(me, x3, kn3, w_in, factor_at, factor_a, gts):
+def grad_mixed_call(me, x3, kn3, w_in, factor_at, factor_a, dist, gts):
     parts = len(gts)
     blocks, inner, chans = x3.shape
     width = w_in.shape[1]
@@ -245,7 +263,7 @@
     whole = pl.BlockSpec((inner, inner), lambda n, i, m: (0, 0))
     size = blocks * inner * chans
     return pl.pallas_call(
-        grad_mixed_kernel,
+        functools.partial(grad_mixed_kernel, dist),
         grid_spec=pltpu.PrefetchScalarGridSpec(
             num_scalar_prefetch=1,
             grid=(chans // width, blocks // some),
@@ -267,62 +285,68 @@
 
 
 def outputs_kernel(p_ref, x_ref, ct_ref, gm_ref, se_ref, wi_ref, wg_ref, wo_ref, *rest):
-    out_ref, gi_ref, gwg, gwo, scr = rest[-5:]
-    before = rest[:-5]
-    blocks, span, width = x_ref.shape
+    out_ref, gi_ref, gw = rest[-3:]
+    before = rest[:-3]
+    mixers = wi_ref.shape[0]
+    blocks, span, chans = x_ref.shape
+    width = wi_ref.shape[1]
     rows = blocks * span
-    x = x_ref[...].reshape(rows, width)
-    ct = ct_ref[...].reshape(rows, width)
-    scr[...] = se_ref[...].astype(F32).reshape(rows, width)
-    second = jnp.concatenate(
-        [scr[pl.ds(i, span, stride=blocks), :] for i in range(blocks)], axis=0
-    )
-    gated = (second * dot(x, wg_ref[0])).astype(BF)
-    out_ref[...] = dot(gated, wo_ref[0]).astype(BF).reshape(blocks, span, width)
-    grad_gate = (dot_nt(ct, wo_ref[0]) * second).astype(BF)
-    grad_mixed = gm_ref[...].reshape(rows, width)
-    grad_inputs = dot_nt(grad_mixed, wi_ref[0]) + dot_nt(grad_gate, wg_ref[0])
-    gi_ref[...] = grad_inputs.astype(BF).reshape(blocks, span, width)
-    gate_term = dot_tn(x, grad_gate)
-    out_term = dot_tn(gated, ct)
-    if before:
-        gate_term += before[2][0]
-        out_term += before[3][0]
-    gwg[0] = gate_term
-    gwo[0] = out_term
+
+    @pl.when(pl.program_id(0) == 0)
+    def _():
+        gw[...] = before[2][...] if before else jnp.zeros_like(gw)
+
+    for n in range(chans // width):
+        lanes = slice(n * width, (n + 1) * width)
+        x = x_ref[:, :, lanes].reshape(rows, width)
+        ct = ct_ref[:, :, lanes].reshape(rows, width)
+        second = jnp.swapaxes(se_ref[:, :, lanes], 0, 1).astype(F32).reshape(rows, width)
+        both = dot(jnp.concatenate([x, ct], axis=1), diagonal(wg_ref[n], wo_ref[n].T))
+        gated = (second * both[:, :width]).astype(BF)
+        grad_gate = (both[:, width:] * second).astype(BF)
+        out_ref[:, :, lanes] = dot(gated, wo_ref[n]).astype(BF).reshape(blocks, span, width)
+        grads = jnp.concatenate([gm_ref[:, :, lanes].reshape(rows, width), grad_gate], axis=1)
+        back = jnp.concatenate([wi_ref[n].T, wg_ref[n].T], axis=0)
+        gi_ref[:, :, lanes] = dot(grads, back).astype(BF).reshape(blocks, span, width)
+        terms = dot_tn(
+            jnp.concatenate([x, gated], axis=1), jnp.concatenate([grad_gate, ct], axis=1)
+        )
+        gw[n] += terms[:width, :width]
+        gw[mixers + n] += terms[width:, width:]
 
 
 def outputs_call(partner, x3, ct3, gm3, second, w_in, w_gate, w_out, before):
     blocks, inner, chans = x3.shape
     width = w_in.shape[1]
     span = second.shape[0]
-    rows = pl.BlockSpec((blocks, span, width), lambda n, p: (0, p[0], n))
-    weight = pl.BlockSpec((1, width, width), lambda n, p: (n, 0, 0))
+    some = min(blocks, 16)
+    rows = pl.BlockSpec((some, span, chans), lambda i, p: (i, p[0], 0))
+    weight = pl.BlockSpec(w_in.shape, lambda i, p: (0, 0, 0))
+    both = (2 * w_in.shape[0], width, width)
+    grads = pl.BlockSpec(both, lambda i, p: (0, 0, 0))
     anywhere = pl.BlockSpec(memory_space=pl.ANY)
     size = blocks * span * chans
     return pl.pallas_call(
         outputs_kernel,
         grid_spec=pltpu.PrefetchScalarGridSpec(
             num_scalar_prefetch=1,
-            grid=(chans // width,),
+            grid=(blocks // some,),
             in_specs=[
                 rows,
                 rows,
                 rows,
-                pl.BlockSpec((span, blocks, width), lambda n, p: (0, 0, n)),
+                pl.BlockSpec((span, some, chans), lambda i, p: (0, i, 0)),
                 weight,
                 weight,
                 weight,
             ]
-            + ([anywhere, anywhere, weight, weight] if before else []),
-            out_specs=[rows, rows, weight, weight],
-            scratch_shapes=[pltpu.VMEM((blocks * span, width), F32)],
+            + ([anywhere, anywhere, grads] if before else []),
+            out_specs=[rows, rows, grads],
         ),
         out_shape=[
             jax.ShapeDtypeStruct(x3.shape, BF),
             jax.ShapeDtypeStruct(x3.shape, BF),
-            jax.ShapeDtypeStruct(w_in.shape, F32),
-            jax.ShapeDtypeStruct(w_in.shape, F32),
+            jax.ShapeDtypeStruct(both, F32),
         ],
         input_output_aliases={8: 0, 9: 1} if before else {},
         compiler_params=params(1),
@@ -331,67 +355,159 @@
     )(partner, x3, ct3, gm3, second, w_in, w_gate, w_out, *before)
 
 
-def exchange(array, d, parts):
-    if d == 0:
-        return array
-    return lax.ppermute(array, "tm", [(i, i ^ d) for i in range(parts)])
-
-
-def send_order(parts):
-    return list(range(parts - 1, -1, -1))
-
-
-def body(parts, inputs, kernel, w_in, w_gate, w_out, factor_a, factor_b, cotangent):
+def nothing_kernel(*refs):
+    pass
+
+
+def wait_for(arrays, after):
+    anywhere = pl.BlockSpec(memory_space=pl.ANY)
+    return pl.pallas_call(
+        nothing_kernel,
+        in_specs=[anywhere] * (len(arrays) + len(after)),
+        out_specs=[anywhere] * len(arrays),
+        out_shape=[jax.ShapeDtypeStruct(a.shape, a.dtype) for a in arrays],
+        input_output_aliases={i: i for i in range(len(arrays))},
+        compiler_params=pltpu.CompilerParams(vmem_limit_bytes=VMEM_LIMIT),
+        name="wait_for",
+    )(*arrays, *after)
+
+
+def permute(array, d, parts, axis="tm"):
+    return lax.ppermute(array, axis, [(i, i ^ d) for i in range(parts)])
+
+
+def distances(parts):
+    far = sorted(range(2, parts), key=lambda d: (-bin(d >> 1).count("1"), -(d & 1), -d))
+    return [0] + far[:2] + [1] + far[2:]
+
+
+def send(dist, arrays, received, window, parts):
+    into = [arrays[0]]
+    for d, array in zip(dist[1:], arrays[1:]):
+        if len(received) >= window:
+            (array,) = wait_for([array], [received[-window]])
+        received.append(permute(array, d, parts))
+        into.append(received[-1])
+    return into
+
+
+def sum_terms(pieces, whole, me, parts, tensors, after, last):
+    chips = parts // 2
+    core, chip = me % 2, me // 2
+    width = whole.shape[-1]
+    packed = jnp.concatenate([p.reshape(chips, 2, -1, width) for p in pieces], axis=2)
+    halves = whole.reshape(2, -1, width)
+
+    def of_core(c):
+        rows = lax.dynamic_index_in_dim(packed, c, 1, keepdims=False).reshape(-1, width)
+        return jnp.concatenate([rows, lax.dynamic_index_in_dim(halves, c, 0, keepdims=False)])
+
+    mine = of_core(core) + permute(of_core(1 - core), 1, parts)
+    (mine,) = wait_for([mine], after)
+    size = packed.shape[2]
+    rows = mine[: chips * size].reshape(chips, size, width)
+    half = mine[chips * size :]
+
+    def of_chip(c):
+        return jnp.concatenate([lax.dynamic_index_in_dim(rows, c, 0, keepdims=False), half])
+
+    total = of_chip(chip)
+    for e in range(1, chips):
+        total = total + permute(of_chip(chip ^ e), 2 * e, parts)
+    (later,) = wait_for([total], [last])
+    summed, half = later[:size], later[size:]
+    d = 1
+    while d < tensors:
+        summed = summed + permute(summed, d, tensors, "tensor")
+        d *= 2
+    other = permute(half, 1, parts)
+    whole = jnp.where(core == 0, jnp.concatenate([half, other]), jnp.concatenate([other, half]))
+    out, start = [], 0
+    for p in pieces:
+        rows = p.size // parts // width
+        out.append(summed[start : start + rows].reshape(-1, p.shape[1]))
+        start += rows
+    return out, whole, total
+
+
+def sum_halves(term, me, parts):
+    core = me % 2
+    half = term.shape[0] // 2
+    term = term + permute(term, 1, parts)
+    return lax.dynamic_slice_in_dim(term, core * half, half, 0)
+
+
+def sum_all(mine, me, parts, after):
+    (mine,) = wait_for([mine], after)
+    total = mine
+    for e in range(1, parts // 2):
+        total = total + permute(mine, 2 * e, parts)
+    other = permute(total, 1, parts)
+    return jnp.where(
+        me % 2 == 0, jnp.concatenate([total, other]), jnp.concatenate([other, total])
+    )
+
+
+def body(parts, tensors, inputs, kernel, w_in, w_gate, w_out, factor_a, factor_b, cotangent):
     rows, chans = inputs.shape
     inner = factor_a.shape[0]
     blocks = rows // inner
     span = inner // parts
     me = lax.axis_index("tm").astype(jnp.int32)
     me1 = me[None]
-    partners = me ^ jnp.arange(parts, dtype=jnp.int32)
     x3 = inputs.reshape(blocks, inner, chans)
     kn3 = kernel.reshape(blocks, inner, chans)
     ct3 = cotangent.reshape(blocks, inner, chans)
     factor_at = factor_a.T
-    order = send_order(parts)
-
-    spread = (partners[:, None] * blocks + jnp.arange(blocks, dtype=jnp.int32)).reshape(-1)
+    dist = distances(parts)
+    partners = [(me ^ d)[None] for d in dist]
+
+    spread = jnp.concatenate([p * blocks + jnp.arange(blocks, dtype=jnp.int32) for p in partners])
     fb = jnp.take(jnp.take(factor_b, spread, axis=0), spread, axis=1)
 
-    gs_in = [None] * parts
-    for d in order:
-        piece = grad_second_call(partners[d][None], x3, ct3, w_gate, w_out, span)
-        gs_in[d] = exchange(piece, d, parts)
-    tw_out = twisted_call(me1, x3, kn3, w_in, factor_at, parts)
-    tw_in = [None] * parts
-    for d in order:
-        tw_in[d] = exchange(tw_out[d], d, parts)
+    received, window = [], 5
+    gs_out = [grad_second_call(p, x3, ct3, w_gate, w_out, span, ()) for p in partners]
+    gs_in = send(dist, gs_out, received, window, parts)
+    tw_out = twisted_call(me1, x3, kn3, w_in, factor_at, dist, ())
+    tw_in = send(dist, tw_out, received, window, parts)
     gt_out = grad_twisted_call(fb, gs_in)
-    gt_in = [None] * parts
-    for d in order:
-        gt_in[d] = exchange(gt_out[d], d, parts)
+    gt_in = send(dist, gt_out, received, window, parts)
     se_out, fb_term = second_call(fb.T, tw_in, gs_in)
-    se_in = [None] * parts
-    for d in order:
-        se_in[d] = exchange(se_out[d], d, parts)
     gk, gm, fa_term, gwi_term = grad_mixed_call(
-        me1, x3, kn3, w_in, factor_at, factor_a, gt_in
-    )
+        me1, x3, kn3, w_in, factor_at, factor_a, dist, gt_in
+    )
+    se_out = list(se_out)
+    tail = 2 * (parts - 1) // 7
+    se_out[-tail - 1 :] = wait_for(se_out[-tail - 1 :], [gwi_term])
+    se_in = send(dist[:-tail], se_out[:-tail], received, window, parts)
+    last = wait_for(se_out[-tail:], se_in[1 : parts // 2])
+    se_in += [permute(a, d, parts) for a, d in zip(last, dist[-tail:])]
     state = ()
-    for d in order[-1:] + order[:-1]:
-        state = outputs_call(
-            partners[d][None], x3, ct3, gm, se_in[d], w_in, w_gate, w_out, state
-        )
-    outputs, grad_inputs, gwg_term, gwo_term = state
-
-    fb_term = jnp.take(jnp.take(fb_term, spread, axis=0), spread, axis=1)
+    for i, (partner, second) in enumerate(zip(partners, se_in)):
+        if i == parts - 2:
+            (second,) = wait_for([second], se_in[-1:] + list(state[2:]))
+        if i == 1:
+            early = state[2:]
+        if i == parts - 1:
+            middle = state[2:]
+        state = outputs_call(partner, x3, ct3, gm, second, w_in, w_gate, w_out, state)
+    outputs, grad_inputs, gw_term = state
+
+    place = jnp.asarray([dist.index(d) for d in range(parts)], jnp.int32)
+    natural = place[me ^ jnp.arange(parts, dtype=jnp.int32)]
+    back = (natural[:, None] * blocks + jnp.arange(blocks, dtype=jnp.int32)).reshape(-1)
+    fb_term = jnp.take(jnp.take(fb_term, back, axis=0), back, axis=1)
+    fa_term, fb_term, gwi_term = wait_for([fa_term, fb_term, gwi_term], early)
+    gw_half = sum_halves(gw_term, me, parts)
+    (fa_sum, fb_sum), summed_in, total = sum_terms(
+        [fa_term, fb_term], gwi_term.reshape(-1, w_in.shape[1]), me, parts, tensors, middle, gw_half
+    )
     token_scale = 1.0 / math.sqrt(N1 * N2)
-    fa_piece = lax.psum_scatter(fa_term, "tm", scatter_dimension=0, tiled=True)
-    fb_piece = lax.psum_scatter(fb_term, "tm", scatter_dimension=0, tiled=True)
-    grad_factor_a = lax.psum(fa_piece, "tensor") / math.sqrt(N1 * D)
-    grad_factor_b = lax.psum(fb_piece, "tensor") / math.sqrt(N2 * D)
-    summed_in = lax.psum(gwi_term, "tm")
-    summed_gate, summed_out = lax.psum((gwg_term, gwo_term), "tm")
+    grad_factor_a = fa_sum / math.sqrt(N1 * D)
+    grad_factor_b = fb_sum / math.sqrt(N2 * D)
+    summed_in = summed_in.reshape(w_in.shape)
+    summed = sum_all(gw_half, me, parts, [total])
+    summed_gate, summed_out = jnp.split(summed, 2)
     return (
         outputs.reshape(rows, chans),
         grad_inputs.reshape(rows, chans),
@@ -406,7 +522,7 @@
 
 def solution(mesh):
     return jax.shard_map(
-        functools.partial(body, mesh.shape["tm"]),
+        functools.partial(body, mesh.shape["tm"], mesh.shape["tensor"]),
         mesh=mesh,
         in_specs=(
             P("tm", "tensor"),

time: 799 us -> 621 us (0.78)
  waiting for transfers between devices: 453 us -> 297 us
  Pallas kernels: 246 us -> 215 us
  starting transfers between devices: 30.4 us -> 53.1 us
  blocking collectives: 21.3 us -> 0 us
  local copies, waits for them, and re-layouts: 16.6 us -> 35.4 us
  between operations: 14.5 us -> 1.62 us
    psum x2 -> x0, waiting for transfers between devices: 67.4 us -> none  [the longest x1 35 us: body(): grad_factor_a = lax.psum(fa_piece, 'tensor') / math.sqrt(N1 * D)]
    ppermute x28 -> x40, waiting for transfers between devices: 349 us -> 297 us  [permute(): return lax.ppermute(array, axis, [(i, i ^ d) for i in range(parts)])]
    reduce_scatter x1 -> x0, waiting for transfers between devices: 35.3 us -> none  [body(): fa_piece = lax.psum_scatter(fa_term, 'tm', scatter_dimension=0, tiled=True)]
    ppermute x28 -> x40, starting transfers between devices: 30.2 us -> 53.1 us  [permute(): return lax.ppermute(array, axis, [(i, i ^ d) for i in range(parts)])]
    psum x1 -> x0, blocking collectives: 21.3 us -> none  [body(): grad_factor_b = lax.psum(fb_piece, 'tensor') / math.sqrt(N2 * D)]
    pallas_call x8, Pallas kernels: 51.2 us -> 30.8 us  [grad_second_call(): pl.pallas_call(grad_second_kernel, grid_spec=pltpu.PrefetchScalarGridSpec...]
    pallas_call x8, Pallas kernels: 73 us -> 62.8 us  [outputs_call(): pl.pallas_call(outputs_kernel, grid_spec=pltpu.PrefetchScalarGridSpec(num...]
    pallas_call x2 -> x30, Pallas kernels: 88.9 us -> 88.5 us  [the longest x1 51.1 us: grad_mixed_call(): pl.pallas_call(functools.partial(grad_mixed_kernel, dist), grid_spec=pltp...]
  transfers between devices with their start and end apart: 32 -> 40, of which waited for: 9 -> 19; matrix products, arithmetic and copies ran while one was open for 3% -> 5% of each run, Pallas kernels for 30% -> 33%
where the time goes in v2:
time: 621 us; the launch traced here: 612 us
  waiting for transfers between devices  297 us (48%)
  Pallas kernels  215 us (35%)
  starting transfers between devices  53.1 us (9%)
  local copies, waits for them, and re-layouts  35.4 us (6%)
  other arithmetic  10.1 us (2%)
    ppermute x40, waiting for transfers between devices, permute(): return lax.ppermute(array, axis, [(i, i ^ d) for i in range(parts)])  297 us
    pallas_call x8, Pallas kernels, outputs_call(): pl.pallas_call(outputs_kernel, grid_spec=pltpu.PrefetchScalarGridSpec(num...  62.8 us
    ppermute x40, starting transfers between devices, permute(): return lax.ppermute(array, axis, [(i, i ^ d) for i in range(parts)])  53.1 us
    pallas_call x1, Pallas kernels, grad_mixed_call(): pl.pallas_call(functools.partial(grad_mixed_kernel, dist), grid_spec=pltp...  51.1 us
    pallas_call x1, Pallas kernels, twisted_call(): pl.pallas_call(functools.partial(twisted_kernel, dist), grid_spec=pltpu.P...  37.4 us
    pallas_call x8, Pallas kernels, grad_second_call(): pl.pallas_call(grad_second_kernel, grid_spec=pltpu.PrefetchScalarGridSpec...  30.8 us
    pallas_call x1, Pallas kernels, second_call(): pl.pallas_call(second_kernel, grid=(span // some,), in_specs=[whole] + [s...  18.6 us
    unnamed x45, local copies, waits for them, and re-layouts  15.8 us
  transfers between devices with their start and end apart: 40, of which 19 were waited for; matrix products, arithmetic and copies ran while one was open for 5% of the time, Pallas kernels for 33%

profile of v2, /device:TPU:0, one launch (start us, length us, event | category | flops | bytes accessed | tf_op | source)
XLA Modules:
  0.0 611.6 jit_solution(4641933459959388505)
XLA Ops:
  0.7 3.9 grad_second.9
  4.5 3.3 collective-permute-start
  7.9 3.8 grad_second.10
  12.3 3.9 grad_second.11
  16.2 3.9 grad_second.12
  21.5 3.9 grad_second.13
  26.9 3.9 grad_second.14.refs_0_
  30.8 12.2 %collective-permute-done.refs_1_.refs_9_ = bf16[64,32,384]{2,1,0:T(8,128)(2,1)S(1)} collective-permute-done((bf16[64,32,384]{2,1,0:T(8,128)(2,1)}, bf16[64,32,384]{2,1,0:T(8,128)(2,1)S(1)}, u32[]{:S(2)}, u32[]{:S(2)}) %collective-permute-start) | collective-permute-done | bytes 1572896 | tf_op jit(solution)/shard_map/ppermute | solution.py:376
  44.1 2.4 collective-permute-start.5
  48.6 3.8 grad_second.15.refs_0_
  52.4 37.4 %twisted.1 = (bf16[64,32,384]{2,1,0:T(8,128)(2,1)}, bf16[64,32,384]{2,1,0:T(8,128)(2,1)}, bf16[64,32,384]{2,1,0:T(8,128)(2,1)}, bf16[64,32,384]{2,1,0:T(8,128)(2...) custom-call(s32[1]{0:T(128)} %bitcast.3.p_ref.me_ref, ...), custom_call_target="tpu_custom_call" | custom-call | flops 805306368 | bytes 3774873 | tf_op jit(solution)/shard_map/twisted/pallas_call | solution.py:126
  92.5 18.0 %collective-permute-done.3.refs_4_.refs_1_.refs_12_ = bf16[64,32,384]{2,1,0:T(8,128)(2,1)} collective-permute-done((bf16[64,32,384]{2,1,0:T(8,128)(2,1)}, bf16[64,32,384]{2,1,0:T(8,128)(2,1)}, u32[]{:S(2)}, u32[]{:S(2)}) %collective-permute-start.3) | collective-permute-done | bytes 1572896 | tf_op jit(solution)/shard_map/ppermute | solution.py:376
  110.5 3.2 collective-permute-start.16
  113.8 31.1 %collective-permute-done.5.refs_6_.refs_1_.refs_14_ = bf16[64,32,384]{2,1,0:T(8,128)(2,1)S(1)} collective-permute-done((bf16[64,32,384]{2,1,0:T(8,128)(2,1)}, bf16[64,32,384]{2,1,0:T(8,128)(2,1)S(1)}, u32[]{:S(2)}, u32[]{:S(2)}) %collective-permute-start.5) | collective-permute-done | bytes 1572896 | tf_op jit(solution)/shard_map/ppermute | solution.py:376
  150.2 27.7 %collective-permute-done.13.refs_1_ = bf16[64,32,384]{2,1,0:T(8,128)(2,1)} collective-permute-done((bf16[64,32,384]{2,1,0:T(8,128)(2,1)}, bf16[64,32,384]{2,1,0:T(8,128)(2,1)}, u32[]{:S(2)}, u32[]{:S(2)}) %collective-permute-start.13) | collective-permute-done | bytes 1572896 | tf_op jit(solution)/shard_map/ppermute | solution.py:376
  177.9 2.5 collective-permute-start.14
  180.4 32.2 %collective-permute-done.16.refs_1_.refs_2_ = bf16[64,32,384]{2,1,0:T(8,128)(2,1)} collective-permute-done((bf16[64,32,384]{2,1,0:T(8,128)(2,1)}, bf16[64,32,384]{2,1,0:T(8,128)(2,1)}, u32[]{:S(2)}, u32[]{:S(2)}) %collective-permute-start.16) | collective-permute-done | bytes 1572896 | tf_op jit(solution)/shard_map/ppermute | solution.py:376
  217.6 3.8 grad_second.8.refs_0_.refs_8_
  221.4 14.1 %grad_twisted.1 = (bf16[64,32,384]{2,1,0:T(8,128)(2,1)}, bf16[64,32,384]{2,1,0:T(8,128)(2,1)}, bf16[64,32,384]{2,1,0:T(8,128)(2,1)}, bf16[64,32,384]{2,1,0:T(8,1...) custom-call(bf16[256,256]{1,0:T(8,128)(2,1)} %copy.73.fb_ref, ...), custom_call_target="tpu_custom_call" | custom-call | flops 322122560 | bytes 2516582 | tf_op jit(solution)/shard_map/grad_twisted/pallas_call | solution.py:164
  236.4 8.8 %collective-permute-done.9.refs_1_.refs_4_ = bf16[64,32,384]{2,1,0:T(8,128)(2,1)S(1)} collective-permute-done((bf16[64,32,384]{2,1,0:T(8,128)(2,1)}, bf16[64,32,384]{2,1,0:T(8,128)(2,1)S(1)}, u32[]{:S(2)}, u32[]{:S(2)}) %collective-permute-start.9) | collective-permute-done | bytes 1572896 | tf_op jit(solution)/shard_map/ppermute | solution.py:376
  246.4 3.2 collective-permute-start.10
  249.7 30.2 %collective-permute-done.14.refs_1_.refs_6_ = bf16[64,32,384]{2,1,0:T(8,128)(2,1)} collective-permute-done((bf16[64,32,384]{2,1,0:T(8,128)(2,1)}, bf16[64,32,384]{2,1,0:T(8,128)(2,1)}, u32[]{:S(2)}, u32[]{:S(2)}) %collective-permute-start.14) | collective-permute-done | bytes 1572896 | tf_op jit(solution)/shard_map/ppermute | solution.py:376
  283.4 29.4 %collective-permute-done.8.refs_1_.rest_1_ = bf16[64,32,384]{2,1,0:T(8,128)(2,1)S(1)} collective-permute-done((bf16[64,32,384]{2,1,0:T(8,128)(2,1)}, bf16[64,32,384]{2,1,0:T(8,128)(2,1)S(1)}, u32[]{:S(2)}, u32[]{:S(2)}) %collective-permute-start.8) | collective-permute-done | bytes 1572896 | tf_op jit(solution)/shard_map/ppermute | solution.py:376
  313.9 2.4 collective-permute-start.19
  316.3 31.0 %collective-permute-done.10.refs_1_.rest_2_ = bf16[64,32,384]{2,1,0:T(8,128)(2,1)S(1)} collective-permute-done((bf16[64,32,384]{2,1,0:T(8,128)(2,1)}, bf16[64,32,384]{2,1,0:T(8,128)(2,1)S(1)}, u32[]{:S(2)}, u32[]{:S(2)}) %collective-permute-start.10) | collective-permute-done | bytes 1572896 | tf_op jit(solution)/shard_map/ppermute | solution.py:376
  350.6 18.6 %second.1 = (bf16[64,32,384]{2,1,0:T(8,128)(2,1)}, bf16[64,32,384]{2,1,0:T(8,128)(2,1)}, bf16[64,32,384]{2,1,0:T(8,128)(2,1)}, bf16[64,32,384]{2,1,0:T(8,128)(2,...) custom-call(bf16[256,256]{1,0:T(8,128)(2,1)} %broadcast_select_fusio, ...), custom_call_target="tpu_custom_call" | custom-call | flops 644245120 | bytes 3774873 | tf_op jit(solution)/shard_map/second/pallas_call | solution.py:201
  370.6 9.7 %collective-permute-done.15.rest_4_.refs_1_ = bf16[64,32,384]{2,1,0:T(8,128)(2,1)} collective-permute-done((bf16[64,32,384]{2,1,0:T(8,128)(2,1)}, bf16[64,32,384]{2,1,0:T(8,128)(2,1)}, u32[]{:S(2)}, u32[]{:S(2)}) %collective-permute-start.15) | collective-permute-done | bytes 1572896 | tf_op jit(solution)/shard_map/ppermute | solution.py:376
  380.3 3.2 collective-permute-start.22
  392.3 22.5 %collective-permute-done.19.rest_6_.refs_1_ = bf16[64,32,384]{2,1,0:T(8,128)(2,1)} collective-permute-done((bf16[64,32,384]{2,1,0:T(8,128)(2,1)}, bf16[64,32,384]{2,1,0:T(8,128)(2,1)}, u32[]{:S(2)}, u32[]{:S(2)}) %collective-permute-start.19) | collective-permute-done | bytes 1572896 | tf_op jit(solution)/shard_map/ppermute | solution.py:376
  417.1 51.1 %grad_mixed.1 = (bf16[32,512,384]{2,1,0:T(8,128)(2,1)}, bf16[32,512,384]{2,1,0:T(8,128)(2,1)}, f32[512,512]{1,0:T(8,128)}, f32[3,128,128]{2,1,0:T(8,128)}) custom-call(s32[1]{0:T(128)} %bitcast.3.p_ref.me_ref, bf16[32,512,384]{2,1,0:T(8,128)(2,1)} %bitcast.77, bf16[32,512,384]{2,1,0:T(8,128)(2,1)} %bitcast.105, bf16[3,128,128]{2,1,0:T(8,128)(2,1)} %wi_ref.19, ...), custom_call_target="tpu_custom_call" | custom-call | flops 2254857728 | bytes 6291456 | tf_op jit(solution)/shard_map/grad_mixed/pallas_call | solution.py:265
  468.3 13.3 %collective-permute-done.22.refs_3_.se_ref = bf16[64,32,384]{2,1,0:T(8,128)(2,1)} collective-permute-done((bf16[64,32,384]{2,1,0:T(8,128)(2,1)}, bf16[64,32,384]{2,1,0:T(8,128)(2,1)}, u32[]{:S(2)}, u32[]{:S(2)}) %collective-permute-start.22) | collective-permute-done | bytes 1572896 | tf_op jit(solution)/shard_map/ppermute | solution.py:376
  481.5 2.2 collective-permute-start.24
  485.3 7.7 %outputs.8 = (bf16[32,512,384]{2,1,0:T(8,128)(2,1)}, bf16[32,512,384]{2,1,0:T(8,128)(2,1)}, f32[6,128,128]{2,1,0:T(8,128)}) custom-call(s32[1]{0:T(128)} %bitcast.3.p_ref.me_ref, bf16[32,512,384]{2,1,0:T(8,128)(2,1)} %bitcast.78, bf16[32,512,384]{2,1,0:T(8,128)(2,1)} %bitcast.94, bf16[32,512,384]{2,1,0:T(8,128)(2,1)} %get-tuple-element.84.gm_ref, ...), custom_call_target="tpu_custom_call" | custom-call | flops 140928608 | bytes 943718 | tf_op jit(solution)/shard_map/outputs/pallas_call | solution.py:329
  493.0 2.3 reshape.342
  499.9 7.7 %outputs.9 = (bf16[32,512,384]{2,1,0:T(8,128)(2,1)}, bf16[32,512,384]{2,1,0:T(8,128)(2,1)}, f32[6,128,128]{2,1,0:T(8,128)}) custom-call(s32[1]{0:T(128)} %bitcast.7.p_ref, bf16[32,512,384]{2,1,0:T(8,128)(2,1)} %bitcast.79, bf16[32,512,384]{2,1,0:T(8,128)(2,1)} %bitcast.95, ...), custom_call_target="tpu_custom_call", output_to_operand_aliasing={{0}: (8, {}), {1}: (9, {})} | custom-call | flops 140928608 | bytes 943718 | tf_op jit(solution)/shard_map/outputs/pallas_call | solution.py:329
  507.7 8.0 %outputs.10 = (bf16[32,512,384]{2,1,0:T(8,128)(2,1)}, bf16[32,512,384]{2,1,0:T(8,128)(2,1)}, f32[6,128,128]{2,1,0:T(8,128)}) custom-call(s32[1]{0:T(128)} %bitcast.9.p_ref, bf16[32,512,384]{2,1,0:T(8,128)(2,1)} %bitcast.80, bf16[32,512,384]{2,1,0:T(8,128)(2,1)} %bitcast.96, ...), custom_call_target="tpu_custom_call", output_to_operand_aliasing={{0}: (8, {}), {1}: (9, {})} | custom-call | flops 140928608 | bytes 943718 | tf_op jit(solution)/shard_map/outputs/pallas_call | solution.py:329
  515.7 7.8 %outputs.11 = (bf16[32,512,384]{2,1,0:T(8,128)(2,1)}, bf16[32,512,384]{2,1,0:T(8,128)(2,1)}, f32[6,128,128]{2,1,0:T(8,128)}) custom-call(s32[1]{0:T(128)} %bitcast.11.p_ref, bf16[32,512,384]{2,1,0:T(8,128)(2,1)} %bitcast.81, bf16[32,512,384]{2,1,0:T(8,128)(2,1)} %bitcast.97, ...), custom_call_target="tpu_custom_call", output_to_operand_aliasing={{0}: (8, {}), {1}: (9, {})} | custom-call | flops 140928608 | bytes 943718 | tf_op jit(solution)/shard_map/outputs/pallas_call | solution.py:329
  523.6 7.9 %outputs.12 = (bf16[32,512,384]{2,1,0:T(8,128)(2,1)}, bf16[32,512,384]{2,1,0:T(8,128)(2,1)}, f32[6,128,128]{2,1,0:T(8,128)}) custom-call(s32[1]{0:T(128)} %bitcast.13.p_ref, bf16[32,512,384]{2,1,0:T(8,128)(2,1)} %bitcast.82, bf16[32,512,384]{2,1,0:T(8,128)(2,1)} %bitcast.98, ...), custom_call_target="tpu_custom_call", output_to_operand_aliasing={{0}: (8, {}), {1}: (9, {})} | custom-call | flops 140928608 | bytes 943718 | tf_op jit(solution)/shard_map/outputs/pallas_call | solution.py:329
  531.5 2.1 maximum_add_fusion.refs_0_
  533.6 18.2 %collective-permute-done.26.se_ref = bf16[64,32,384]{2,1,0:T(8,128)(2,1)} collective-permute-done((bf16[64,32,384]{2,1,0:T(8,128)(2,1)}, bf16[64,32,384]{2,1,0:T(8,128)(2,1)}, u32[]{:S(2)}, u32[]{:S(2)}) %collective-permute-start.26) | collective-permute-done | bytes 1572896 | tf_op jit(solution)/shard_map/ppermute | solution.py:376
  551.8 7.8 %outputs.13 = (bf16[32,512,384]{2,1,0:T(8,128)(2,1)}, bf16[32,512,384]{2,1,0:T(8,128)(2,1)}, f32[6,128,128]{2,1,0:T(8,128)}) custom-call(s32[1]{0:T(128)} %bitcast.15.p_ref, bf16[32,512,384]{2,1,0:T(8,128)(2,1)} %bitcast.83, bf16[32,512,384]{2,1,0:T(8,128)(2,1)} %bitcast.99, ...), custom_call_target="tpu_custom_call", output_to_operand_aliasing={{0}: (8, {}), {1}: (9, {})} | custom-call | flops 140928608 | bytes 943718 | tf_op jit(solution)/shard_map/outputs/pallas_call | solution.py:329
  561.3 7.8 %outputs.14 = (bf16[32,512,384]{2,1,0:T(8,128)(2,1)}, bf16[32,512,384]{2,1,0:T(8,128)(2,1)}, f32[6,128,128]{2,1,0:T(8,128)}) custom-call(s32[1]{0:T(128)} %bitcast.17.p_ref, bf16[32,512,384]{2,1,0:T(8,128)(2,1)} %bitcast.84, bf16[32,512,384]{2,1,0:T(8,128)(2,1)} %bitcast.100, ...), custom_call_target="tpu_custom_call", output_to_operand_aliasing={{0}: (8, {}), {1}: (9, {})} | custom-call | flops 140928608 | bytes 943718 | tf_op jit(solution)/shard_map/outputs/pallas_call | solution.py:329
  571.2 2.4 collective-permute-start.31
  574.8 8.0 %outputs.15 = (bf16[32,512,384]{2,1,0:T(8,128)(2,1)}, bf16[32,512,384]{2,1,0:T(8,128)(2,1)}, f32[6,128,128]{2,1,0:T(8,128)}) custom-call(s32[1]{0:T(128)} %bitcast.p_ref, bf16[32,512,384]{2,1,0:T(8,128)(2,1)} %bitcast.85, bf16[32,512,384]{2,1,0:T(8,128)(2,1)} %bitcast.101, ...), custom_call_target="tpu_custom_call", output_to_operand_aliasing={{0}: (8, {}), {1}: (9, {})} | custom-call | flops 140928608 | bytes 943718 | tf_op jit(solution)/shard_map/outputs/pallas_call | solution.py:329
  582.9 3.6 collective-permute-done.30
  598.7 2.7 collective-permute-start.39
  601.7 3.5 collective-permute-done.35
  605.3 3.8 collective-permute-done.39
  (186 shorter events, 68.2 us)
Async XLA Ops:
  0.6 213.4 %copy-start = (bf16[256,256]{1,0:T(8,128)(2,1)S(1)}, bf16[256,256]{1,0:T(8,128)(2,1)}, u32[]{:S(2)}) copy-start(bf16[256,256]{1,0:T(8,128)(2,1)} %param.15) | copy-start | bytes 393220
  4.5 38.5 %collective-permute-start = (bf16[64,32,384]{2,1,0:T(8,128)(2,1)}, bf16[64,32,384]{2,1,0:T(8,128)(2,1)S(1)}, u32[]{:S(2)}, u32[]{:S(2)}) collective-permute-start(bf16[64,32,384]{2,1,0:T(8,128)(2,1)} %grad_second.9), channel_id=1, source_target_pairs={{0,28},{4,24},{8,20},{12,16},{16,12},{20,8},{24,4},{28,0},{1,29},{... | collective-permute-start | bytes 4718600 | tf_op jit(solution)/shard_map/ppermute | solution.py:376
  11.7 78.1 %collective-permute-start.1 = (bf16[64,32,384]{2,1,0:T(8,128)(2,1)}, bf16[64,32,384]{2,1,0:T(8,128)(2,1)S(1)}, u32[]{:S(2)}, u32[]{:S(2)}) collective-permute-start(bf16[64,32,384]{2,1,0:T(8,128)(2,1)} %grad_second.10), channel_id=1, source_target_pairs={{0,24},{4,28},{8,16},{12,20},{16,8},{20,12},{24,0},{28,4},{1,25},{... | collective-permute-start | bytes 4718600 | tf_op jit(solution)/shard_map/ppermute | solution.py:376
  16.1 76.4 %collective-permute-start.2 = (bf16[64,32,384]{2,1,0:T(8,128)(2,1)}, bf16[64,32,384]{2,1,0:T(8,128)(2,1)}, u32[]{:S(2)}, u32[]{:S(2)}) collective-permute-start(bf16[64,32,384]{2,1,0:T(8,128)(2,1)} %grad_second.11), channel_id=1, source_target_pairs={{0,4},{4,0},{8,12},{12,8},{16,20},{20,16},{24,28},{28,24},{1,5},{5... | collective-permute-start | bytes 4718600 | tf_op jit(solution)/shard_map/ppermute | solution.py:376
  20.1 90.4 %collective-permute-start.3 = (bf16[64,32,384]{2,1,0:T(8,128)(2,1)}, bf16[64,32,384]{2,1,0:T(8,128)(2,1)}, u32[]{:S(2)}, u32[]{:S(2)}) collective-permute-start(bf16[64,32,384]{2,1,0:T(8,128)(2,1)} %grad_second.12), channel_id=1, source_target_pairs={{0,20},{4,16},{8,28},{12,24},{16,4},{20,0},{24,12},{28,8},{1,21},{... | collective-permute-start | bytes 4718600 | tf_op jit(solution)/shard_map/ppermute | solution.py:376
  25.4 88.3 %collective-permute-start.4 = (bf16[64,32,384]{2,1,0:T(8,128)(2,1)}, bf16[64,32,384]{2,1,0:T(8,128)(2,1)}, u32[]{:S(2)}, u32[]{:S(2)}) collective-permute-start(bf16[64,32,384]{2,1,0:T(8,128)(2,1)} %grad_second.13), channel_id=1, source_target_pairs={{0,12},{4,8},{8,4},{12,0},{16,28},{20,24},{24,20},{28,16},{1,13},{... | collective-permute-start | bytes 4718600 | tf_op jit(solution)/shard_map/ppermute | solution.py:376
  44.1 100.8 %collective-permute-start.5 = (bf16[64,32,384]{2,1,0:T(8,128)(2,1)}, bf16[64,32,384]{2,1,0:T(8,128)(2,1)S(1)}, u32[]{:S(2)}, u32[]{:S(2)}) collective-permute-start(bf16[64,32,384]{2,1,0:T(8,128)(2,1)} %wait_for.28), channel_id=1, source_target_pairs={{0,16},{4,20},{8,24},{12,28},{16,0},{20,4},{24,8},{28,12},{1,17},{... | collective-permute-start | bytes 4718600 | tf_op jit(solution)/shard_map/ppermute | solution.py:376
  90.9 56.5 %collective-permute-start.6 = (bf16[64,32,384]{2,1,0:T(8,128)(2,1)}, bf16[64,32,384]{2,1,0:T(8,128)(2,1)S(1)}, u32[]{:S(2)}, u32[]{:S(2)}) collective-permute-start(bf16[64,32,384]{2,1,0:T(8,128)(2,1)} %wait_for.29), channel_id=1, source_target_pairs={{0,8},{4,12},{8,0},{12,4},{16,24},{20,28},{24,16},{28,20},{1,9},{5... | collective-permute-start | bytes 4718600 | tf_op jit(solution)/shard_map/ppermute | solution.py:376
  92.5 85.4 %collective-permute-start.13 = (bf16[64,32,384]{2,1,0:T(8,128)(2,1)}, bf16[64,32,384]{2,1,0:T(8,128)(2,1)}, u32[]{:S(2)}, u32[]{:S(2)}) collective-permute-start(bf16[64,32,384]{2,1,0:T(8,128)(2,1)} %wait_for.36), channel_id=1, source_target_pairs={{0,28},{4,24},{8,20},{12,16},{16,12},{20,8},{24,4},{28,0},{1,29},{... | collective-permute-start | bytes 4718600 | tf_op jit(solution)/shard_map/ppermute | solution.py:376
  110.5 102.1 %collective-permute-start.16 = (bf16[64,32,384]{2,1,0:T(8,128)(2,1)}, bf16[64,32,384]{2,1,0:T(8,128)(2,1)}, u32[]{:S(2)}, u32[]{:S(2)}) collective-permute-start(bf16[64,32,384]{2,1,0:T(8,128)(2,1)} %wait_for.39), channel_id=1, source_target_pairs={{0,24},{4,28},{8,16},{12,20},{16,8},{20,12},{24,0},{28,4},{1,25},{... | collective-permute-start | bytes 4718600 | tf_op jit(solution)/shard_map/ppermute | solution.py:376
  113.7 121.7 %collective-permute-start.7 = (bf16[64,32,384]{2,1,0:T(8,128)(2,1)}, bf16[64,32,384]{2,1,0:T(8,128)(2,1)}, u32[]{:S(2)}, u32[]{:S(2)}) collective-permute-start(bf16[64,32,384]{2,1,0:T(8,128)(2,1)} %wait_for.30), channel_id=1, source_target_pairs={{0,4},{4,0},{8,12},{12,8},{16,20},{20,16},{24,28},{28,24},{1,5},{5... | collective-permute-start | bytes 4718600 | tf_op jit(solution)/shard_map/ppermute | solution.py:376
  146.2 99.1 %collective-permute-start.9 = (bf16[64,32,384]{2,1,0:T(8,128)(2,1)}, bf16[64,32,384]{2,1,0:T(8,128)(2,1)S(1)}, u32[]{:S(2)}, u32[]{:S(2)}) collective-permute-start(bf16[64,32,384]{2,1,0:T(8,128)(2,1)} %wait_for.32), channel_id=1, source_target_pairs={{0,20},{4,16},{8,28},{12,24},{16,4},{20,0},{24,12},{28,8},{1,21},{... | collective-permute-start | bytes 4718600 | tf_op jit(solution)/shard_map/ppermute | solution.py:376
  148.6 101.0 %collective-permute-start.11 = (bf16[64,32,384]{2,1,0:T(8,128)(2,1)}, bf16[64,32,384]{2,1,0:T(8,128)(2,1)}, u32[]{:S(2)}, u32[]{:S(2)}) collective-permute-start(bf16[64,32,384]{2,1,0:T(8,128)(2,1)} %wait_for.34), channel_id=1, source_target_pairs={{0,12},{4,8},{8,4},{12,0},{16,28},{20,24},{24,20},{28,16},{1,13},{... | collective-permute-start | bytes 4718600 | tf_op jit(solution)/shard_map/ppermute | solution.py:376
  177.9 102.0 %collective-permute-start.14 = (bf16[64,32,384]{2,1,0:T(8,128)(2,1)}, bf16[64,32,384]{2,1,0:T(8,128)(2,1)}, u32[]{:S(2)}, u32[]{:S(2)}) collective-permute-start(bf16[64,32,384]{2,1,0:T(8,128)(2,1)} %wait_for.37), channel_id=1, source_target_pairs={{0,16},{4,20},{8,24},{12,28},{16,0},{20,4},{24,8},{28,12},{1,17},{... | collective-permute-start | bytes 4718600 | tf_op jit(solution)/shard_map/ppermute | solution.py:376
  212.6 68.5 %collective-permute-start.17 = (bf16[64,32,384]{2,1,0:T(8,128)(2,1)}, bf16[64,32,384]{2,1,0:T(8,128)(2,1)}, u32[]{:S(2)}, u32[]{:S(2)}) collective-permute-start(bf16[64,32,384]{2,1,0:T(8,128)(2,1)} %wait_for.40), channel_id=1, source_target_pairs={{0,8},{4,12},{8,0},{12,4},{16,24},{20,28},{24,16},{28,20},{1,9},{5... | collective-permute-start | bytes 4718600 | tf_op jit(solution)/shard_map/ppermute | solution.py:376
  235.5 77.2 %collective-permute-start.8 = (bf16[64,32,384]{2,1,0:T(8,128)(2,1)}, bf16[64,32,384]{2,1,0:T(8,128)(2,1)S(1)}, u32[]{:S(2)}, u32[]{:S(2)}) collective-permute-start(bf16[64,32,384]{2,1,0:T(8,128)(2,1)} %wait_for.31), channel_id=1, source_target_pairs={{0,28},{4,24},{8,20},{12,16},{16,12},{20,8},{24,4},{28,0},{1,29},{... | collective-permute-start | bytes 4718600 | tf_op jit(solution)/shard_map/ppermute | solution.py:376
  246.4 100.9 %collective-permute-start.10 = (bf16[64,32,384]{2,1,0:T(8,128)(2,1)}, bf16[64,32,384]{2,1,0:T(8,128)(2,1)S(1)}, u32[]{:S(2)}, u32[]{:S(2)}) collective-permute-start(bf16[64,32,384]{2,1,0:T(8,128)(2,1)} %wait_for.33), channel_id=1, source_target_pairs={{0,24},{4,28},{8,16},{12,20},{16,8},{20,12},{24,0},{28,4},{1,25},{... | collective-permute-start | bytes 4718600 | tf_op jit(solution)/shard_map/ppermute | solution.py:376
  249.6 119.6 %collective-permute-start.12 = (bf16[64,32,384]{2,1,0:T(8,128)(2,1)}, bf16[64,32,384]{2,1,0:T(8,128)(2,1)}, u32[]{:S(2)}, u32[]{:S(2)}) collective-permute-start(bf16[64,32,384]{2,1,0:T(8,128)(2,1)} %wait_for.35), channel_id=1, source_target_pairs={{0,4},{4,0},{8,12},{12,8},{16,20},{20,16},{24,28},{28,24},{1,5},{5... | collective-permute-start | bytes 4718600 | tf_op jit(solution)/shard_map/ppermute | solution.py:376
  279.9 100.4 %collective-permute-start.15 = (bf16[64,32,384]{2,1,0:T(8,128)(2,1)}, bf16[64,32,384]{2,1,0:T(8,128)(2,1)}, u32[]{:S(2)}, u32[]{:S(2)}) collective-permute-start(bf16[64,32,384]{2,1,0:T(8,128)(2,1)} %wait_for.38), channel_id=1, source_target_pairs={{0,20},{4,16},{8,28},{12,24},{16,4},{20,0},{24,12},{28,8},{1,21},{... | collective-permute-start | bytes 4718600 | tf_op jit(solution)/shard_map/ppermute | solution.py:376
  281.1 102.4 %collective-permute-start.18 = (bf16[64,32,384]{2,1,0:T(8,128)(2,1)}, bf16[64,32,384]{2,1,0:T(8,128)(2,1)}, u32[]{:S(2)}, u32[]{:S(2)}) collective-permute-start(bf16[64,32,384]{2,1,0:T(8,128)(2,1)} %wait_for.41), channel_id=1, source_target_pairs={{0,12},{4,8},{8,4},{12,0},{16,28},{20,24},{24,20},{28,16},{1,13},{... | collective-permute-start | bytes 4718600 | tf_op jit(solution)/shard_map/ppermute | solution.py:376
  313.9 100.8 %collective-permute-start.19 = (bf16[64,32,384]{2,1,0:T(8,128)(2,1)}, bf16[64,32,384]{2,1,0:T(8,128)(2,1)}, u32[]{:S(2)}, u32[]{:S(2)}) collective-permute-start(bf16[64,32,384]{2,1,0:T(8,128)(2,1)} %wait_for.42), channel_id=1, source_target_pairs={{0,16},{4,20},{8,24},{12,28},{16,0},{20,4},{24,8},{28,12},{1,17},{... | collective-permute-start | bytes 4718600 | tf_op jit(solution)/shard_map/ppermute | solution.py:376
  348.5 1.5 copy-start.2
  348.5 67.5 %collective-permute-start.20 = (bf16[64,32,384]{2,1,0:T(8,128)(2,1)}, bf16[64,32,384]{2,1,0:T(8,128)(2,1)S(1)}, u32[]{:S(2)}, u32[]{:S(2)}) collective-permute-start(bf16[64,32,384]{2,1,0:T(8,128)(2,1)} %wait_for.43), channel_id=1, source_target_pairs={{0,8},{4,12},{8,0},{12,4},{16,24},{20,28},{24,16},{28,20},{1,9},{5... | collective-permute-start | bytes 4718600 | tf_op jit(solution)/shard_map/ppermute | solution.py:376
  369.3 99.0 %collective-permute-start.21 = (bf16[64,32,384]{2,1,0:T(8,128)(2,1)}, bf16[64,32,384]{2,1,0:T(8,128)(2,1)S(1)}, u32[]{:S(2)}, u32[]{:S(2)}) collective-permute-start(bf16[64,32,384]{2,1,0:T(8,128)(2,1)} %wait_for.45), channel_id=1, source_target_pairs={{0,28},{4,24},{8,20},{12,16},{16,12},{20,8},{24,4},{28,0},{1,29},{... | collective-permute-start | bytes 4718600 | tf_op jit(solution)/shard_map/ppermute | solution.py:376
  380.3 101.3 %collective-permute-start.22 = (bf16[64,32,384]{2,1,0:T(8,128)(2,1)}, bf16[64,32,384]{2,1,0:T(8,128)(2,1)}, u32[]{:S(2)}, u32[]{:S(2)}) collective-permute-start(bf16[64,32,384]{2,1,0:T(8,128)(2,1)} %wait_for.46), channel_id=1, source_target_pairs={{0,24},{4,28},{8,16},{12,20},{16,8},{20,12},{24,0},{28,4},{1,25},{... | collective-permute-start | bytes 4718600 | tf_op jit(solution)/shard_map/ppermute | solution.py:376
  383.5 98.1 %collective-permute-start.23 = (bf16[64,32,384]{2,1,0:T(8,128)(2,1)}, bf16[64,32,384]{2,1,0:T(8,128)(2,1)}, u32[]{:S(2)}, u32[]{:S(2)}) collective-permute-start(bf16[64,32,384]{2,1,0:T(8,128)(2,1)} %wait_for.47), channel_id=1, source_target_pairs={{0,4},{4,0},{8,12},{12,8},{16,20},{20,16},{24,28},{28,24},{1,5},{5... | collective-permute-start | bytes 4718600 | tf_op jit(solution)/shard_map/ppermute | solution.py:376
  414.8 108.8 %collective-permute-start.27 = (bf16[64,32,384]{2,1,0:T(8,128)(2,1)}, bf16[64,32,384]{2,1,0:T(8,128)(2,1)}, u32[]{:S(2)}, u32[]{:S(2)}) collective-permute-start(bf16[64,32,384]{2,1,0:T(8,128)(2,1)} %wait_for.50), channel_id=1, source_target_pairs={{0,20},{4,16},{8,28},{12,24},{16,4},{20,0},{24,12},{28,8},{1,21},{... | collective-permute-start | bytes 4718600 | tf_op jit(solution)/shard_map/ppermute | solution.py:376
  468.3 13.3 %copy-start.14 = (bf16[64,32,384]{2,1,0:T(8,128)(2,1)}, bf16[64,32,384]{2,1,0:T(8,128)(2,1)S(1)}, u32[]{:S(2)}) copy-start(bf16[64,32,384]{2,1,0:T(8,128)(2,1)S(1)} %collective-permute-done.21.refs_2_.se_ref) | copy-start | bytes 4718596
  481.5 78.1 %collective-permute-start.24 = (bf16[64,32,384]{2,1,0:T(8,128)(2,1)}, bf16[64,32,384]{2,1,0:T(8,128)(2,1)S(1)}, u32[]{:S(2)}, u32[]{:S(2)}) collective-permute-start(bf16[64,32,384]{2,1,0:T(8,128)(2,1)} %get-tuple-element.95), channel_id=1, source_target_pairs={{0,8},{4,12},{8,0},{12,4},{16,24},{20,28},{24,16},{28,20},{1,9},{5... | collective-permute-start | bytes 4718600 | tf_op jit(solution)/shard_map/ppermute | solution.py:376
  483.8 75.8 %collective-permute-start.25 = (bf16[64,32,384]{2,1,0:T(8,128)(2,1)}, bf16[64,32,384]{2,1,0:T(8,128)(2,1)S(1)}, u32[]{:S(2)}, u32[]{:S(2)}) collective-permute-start(bf16[64,32,384]{2,1,0:T(8,128)(2,1)} %get-tuple-element.96), channel_id=1, source_target_pairs={{0,16},{4,20},{8,24},{12,28},{16,0},{20,4},{24,8},{28,12},{1,17},{... | collective-permute-start | bytes 4718600 | tf_op jit(solution)/shard_map/ppermute | solution.py:376
  485.3 66.5 %collective-permute-start.26 = (bf16[64,32,384]{2,1,0:T(8,128)(2,1)}, bf16[64,32,384]{2,1,0:T(8,128)(2,1)}, u32[]{:S(2)}, u32[]{:S(2)}) collective-permute-start(bf16[64,32,384]{2,1,0:T(8,128)(2,1)} %wait_for.49), channel_id=1, source_target_pairs={{0,12},{4,8},{8,4},{12,0},{16,28},{20,24},{24,20},{28,16},{1,13},{... | collective-permute-start | bytes 4718600 | tf_op jit(solution)/shard_map/ppermute | solution.py:376
  493.0 2.4 copy-start.16
  499.3 32.1 %collective-permute-start.28 = (f32[1472,128]{1,0:T(8,128)}, f32[1472,128]{1,0:T(8,128)}, u32[]{:S(2)}, u32[]{:S(2)}) collective-permute-start(f32[1472,128]{1,0:T(8,128)} %pad_maximum_fusion), channel_id=1, source_target_pairs={{0,4},{4,0},{8,12},{12,8},{16,20},{20,16},{24,28},{28,24},{1,5},{5... | collective-permute-start | bytes 2261000 | tf_op jit(solution)/shard_map/ppermute | solution.py:376
  523.6 7.9 %copy-start.15 = (f32[4,1,320,128]{3,2,1,0:T(8,128)S(1)}, f32[4,1,320,128]{3,2,1,0:T(8,128)}, u32[]{:S(2)}) copy-start(f32[4,1,320,128]{3,2,1,0:T(8,128)} %get-tuple-element.130) | copy-start | bytes 1966084
  559.6 1.6 copy-start.13
  571.2 11.7 %collective-permute-start.31 = (f32[512,128]{1,0:T(8,128)S(1)}, f32[512,128]{1,0:T(8,128)S(1)}, u32[]{:S(2)}, u32[]{:S(2)}) collective-permute-start(f32[512,128]{1,0:T(8,128)S(1)} %get-tuple-element.142), channel_id=1, source_target_pairs={{0,24},{4,28},{8,16},{12,20},{16,8},{20,12},{24,0},{28,4},{1,25},{... | collective-permute-start | bytes 786440 | tf_op jit(solution)/shard_map/ppermute | solution.py:376
  573.7 12.8 %collective-permute-start.30 = (f32[512,128]{1,0:T(8,128)S(1)}, f32[512,128]{1,0:T(8,128)S(1)}, u32[]{:S(2)}, u32[]{:S(2)}) collective-permute-start(f32[512,128]{1,0:T(8,128)S(1)} %get-tuple-element.141), channel_id=1, source_target_pairs={{0,16},{4,20},{8,24},{12,28},{16,0},{20,4},{24,8},{28,12},{1,17},{... | collective-permute-start | bytes 786440 | tf_op jit(solution)/shard_map/ppermute | solution.py:376
  574.2 12.6 %collective-permute-start.29 = (f32[512,128]{1,0:T(8,128)S(1)}, f32[512,128]{1,0:T(8,128)S(1)}, u32[]{:S(2)}, u32[]{:S(2)}) collective-permute-start(f32[512,128]{1,0:T(8,128)S(1)} %get-tuple-element.140), channel_id=1, source_target_pairs={{0,8},{4,12},{8,0},{12,4},{16,24},{20,28},{24,16},{28,20},{1,9},{5... | collective-permute-start | bytes 786440 | tf_op jit(solution)/shard_map/ppermute | solution.py:376
  582.8 4.7 collective-permute-start.32
  589.2 15.9 %copy-start.19 = (f32[3,128,128]{2,1,0:T(8,128)S(1)}, f32[3,128,128]{2,1,0:T(8,128)}, u32[]{:S(2)}) copy-start(f32[3,128,128]{2,1,0:T(8,128)} %wait_for.55) | copy-start | bytes 589828
  590.2 6.1 collective-permute-start.33
  591.1 6.7 %collective-permute-start.38 = (f32[320,128]{1,0:T(8,128)S(1)}, f32[320,128]{1,0:T(8,128)S(1)}, u32[]{:S(2)}, u32[]{:S(2)}) collective-permute-start(f32[320,128]{1,0:T(8,128)S(1)} %slice.37), channel_id=1, source_target_pairs={{0,1},{1,0},{2,3},{3,2},{4,5},{5,4},{6,7},{7,6},{8,9},{9,8},{10,11... | collective-permute-start | bytes 491528 | tf_op jit(solution)/shard_map/ppermute | solution.py:376
  592.8 8.9 %collective-permute-start.36 = (f32[3,128,128]{2,1,0:T(8,128)}, f32[3,128,128]{2,1,0:T(8,128)S(1)}, u32[]{:S(2)}, u32[]{:S(2)}) collective-permute-start(f32[3,128,128]{2,1,0:T(8,128)} %wait_for.55), channel_id=1, source_target_pairs={{0,24},{4,28},{8,16},{12,20},{16,8},{20,12},{24,0},{28,4},{1,25},{... | collective-permute-start | bytes 589832 | tf_op jit(solution)/shard_map/ppermute | solution.py:376
  594.3 10.8 %collective-permute-start.35 = (f32[3,128,128]{2,1,0:T(8,128)}, f32[3,128,128]{2,1,0:T(8,128)S(1)}, u32[]{:S(2)}, u32[]{:S(2)}) collective-permute-start(f32[3,128,128]{2,1,0:T(8,128)} %wait_for.55), channel_id=1, source_target_pairs={{0,16},{4,20},{8,24},{12,28},{16,0},{20,4},{24,8},{28,12},{1,17},{... | collective-permute-start | bytes 589832 | tf_op jit(solution)/shard_map/ppermute | solution.py:376
  595.7 9.4 %collective-permute-start.34 = (f32[3,128,128]{2,1,0:T(8,128)}, f32[3,128,128]{2,1,0:T(8,128)S(1)}, u32[]{:S(2)}, u32[]{:S(2)}) collective-permute-start(f32[3,128,128]{2,1,0:T(8,128)} %wait_for.55), channel_id=1, source_target_pairs={{0,8},{4,12},{8,0},{12,4},{16,24},{20,28},{24,16},{28,20},{1,9},{5... | collective-permute-start | bytes 589832 | tf_op jit(solution)/shard_map/ppermute | solution.py:376
  598.7 10.3 %collective-permute-start.39 = (f32[320,128]{1,0:T(8,128)S(1)}, f32[320,128]{1,0:T(8,128)S(1)}, u32[]{:S(2)}, u32[]{:S(2)}) collective-permute-start(f32[320,128]{1,0:T(8,128)S(1)} %slice_add_fusion), channel_id=1, source_target_pairs={{0,2},{1,3},{2,0},{3,1},{4,6},{5,7},{6,4},{7,5},{8,10},{9,11},{10,... | collective-permute-start | bytes 491528 | tf_op jit(solution)/shard_map/ppermute | solution.py:376
  605.1 6.1 copy-start.1
  605.2 5.2 collective-permute-start.37
  (13 other events, 14.5 us)

commit v3 on v2

--- a/solution.py
+++ b/solution.py
@@ -284,19 +284,23 @@
     )(me, x3, kn3, w_in, factor_at, factor_a, *gts)
 
 
-def outputs_kernel(p_ref, x_ref, ct_ref, gm_ref, se_ref, wi_ref, wg_ref, wo_ref, *rest):
-    out_ref, gi_ref, gw = rest[-3:]
-    before = rest[:-3]
-    mixers = wi_ref.shape[0]
+def outputs_kernel(arrays, terms, p_ref, x_ref, ct_ref, se_ref, wg_ref, wo_ref, *rest):
+    rest = list(rest)
+    gm_ref, wi_ref = (rest.pop(0), rest.pop(0)) if arrays else (None, None)
+    gw = rest.pop() if terms else None
+    out_ref, gi_ref = rest[-2:] if arrays else (None, None)
+    before = rest[:-2] if arrays else rest
     blocks, span, chans = x_ref.shape
-    width = wi_ref.shape[1]
+    mixers, width, _ = wg_ref.shape
     rows = blocks * span
 
-    @pl.when(pl.program_id(0) == 0)
-    def _():
-        gw[...] = before[2][...] if before else jnp.zeros_like(gw)
-
-    for n in range(chans // width):
+    if terms:
+
+        @pl.when(pl.program_id(0) == 0)
+        def _():
+            gw[...] = before[-1][...] if before else jnp.zeros_like(gw)
+
+    for n in range(mixers):
         lanes = slice(n * width, (n + 1) * width)
         x = x_ref[:, :, lanes].reshape(rows, width)
         ct = ct_ref[:, :, lanes].reshape(rows, width)
@@ -304,18 +308,20 @@
         both = dot(jnp.concatenate([x, ct], axis=1), diagonal(wg_ref[n], wo_ref[n].T))
         gated = (second * both[:, :width]).astype(BF)
         grad_gate = (both[:, width:] * second).astype(BF)
-        out_ref[:, :, lanes] = dot(gated, wo_ref[n]).astype(BF).reshape(blocks, span, width)
-        grads = jnp.concatenate([gm_ref[:, :, lanes].reshape(rows, width), grad_gate], axis=1)
-        back = jnp.concatenate([wi_ref[n].T, wg_ref[n].T], axis=0)
-        gi_ref[:, :, lanes] = dot(grads, back).astype(BF).reshape(blocks, span, width)
-        terms = dot_tn(
-            jnp.concatenate([x, gated], axis=1), jnp.concatenate([grad_gate, ct], axis=1)
-        )
-        gw[n] += terms[:width, :width]
-        gw[mixers + n] += terms[width:, width:]
-
-
-def outputs_call(partner, x3, ct3, gm3, second, w_in, w_gate, w_out, before):
+        if arrays:
+            out_ref[:, :, lanes] = dot(gated, wo_ref[n]).astype(BF).reshape(blocks, span, width)
+            grads = jnp.concatenate([gm_ref[:, :, lanes].reshape(rows, width), grad_gate], axis=1)
+            back = jnp.concatenate([wi_ref[n].T, wg_ref[n].T], axis=0)
+            gi_ref[:, :, lanes] = dot(grads, back).astype(BF).reshape(blocks, span, width)
+        if terms:
+            both = dot_tn(
+                jnp.concatenate([x, gated], axis=1), jnp.concatenate([grad_gate, ct], axis=1)
+            )
+            gw[n] += both[:width, :width]
+            gw[mixers + n] += both[width:, width:]
+
+
+def outputs_call(partner, x3, ct3, gm3, second, w_in, w_gate, w_out, arrays=(), terms=()):
     blocks, inner, chans = x3.shape
     width = w_in.shape[1]
     span = second.shape[0]
@@ -326,33 +332,33 @@
     grads = pl.BlockSpec(both, lambda i, p: (0, 0, 0))
     anywhere = pl.BlockSpec(memory_space=pl.ANY)
     size = blocks * span * chans
+    operands = [x3, ct3, second, w_gate, w_out]
+    specs = [rows, rows, pl.BlockSpec((span, some, chans), lambda i, p: (0, i, 0)), weight, weight]
+    aliases, out_specs, out_shape = {}, [], []
+    if arrays is not None:
+        operands += [gm3, w_in]
+        specs += [rows, weight]
+        aliases = {len(operands) + 1 + i: i for i in range(len(arrays))}
+        operands += arrays
+        specs += [anywhere] * len(arrays)
+        out_specs += [rows, rows]
+        out_shape += [jax.ShapeDtypeStruct(x3.shape, BF)] * 2
+    if terms is not None:
+        operands += terms
+        specs += [grads] * len(terms)
+        out_specs += [grads]
+        out_shape += [jax.ShapeDtypeStruct(both, F32)]
     return pl.pallas_call(
-        outputs_kernel,
+        functools.partial(outputs_kernel, arrays is not None, terms is not None),
         grid_spec=pltpu.PrefetchScalarGridSpec(
-            num_scalar_prefetch=1,
-            grid=(blocks // some,),
-            in_specs=[
-                rows,
-                rows,
-                rows,
-                pl.BlockSpec((span, some, chans), lambda i, p: (0, i, 0)),
-                weight,
-                weight,
-                weight,
-            ]
-            + ([anywhere, anywhere, grads] if before else []),
-            out_specs=[rows, rows, grads],
+            num_scalar_prefetch=1, grid=(blocks // some,), in_specs=specs, out_specs=out_specs
         ),
-        out_shape=[
-            jax.ShapeDtypeStruct(x3.shape, BF),
-            jax.ShapeDtypeStruct(x3.shape, BF),
-            jax.ShapeDtypeStruct(both, F32),
-        ],
-        input_output_aliases={8: 0, 9: 1} if before else {},
+        out_shape=out_shape,
+        input_output_aliases=aliases,
         compiler_params=params(1),
         cost_estimate=cost(14 * size * width, 12 * size),
         name="outputs",
-    )(partner, x3, ct3, gm3, second, w_in, w_gate, w_out, *before)
+    )(partner, *operands)
 
 
 def nothing_kernel(*refs):
@@ -378,7 +384,8 @@
 
 def distances(parts):
     far = sorted(range(2, parts), key=lambda d: (-bin(d >> 1).count("1"), -(d & 1), -d))
-    return [0] + far[:2] + [1] + far[2:]
+    cut = 4 * (parts - 1) // 7
+    return [0] + far[:cut] + [1] + far[cut:]
 
 
 def send(dist, arrays, received, window, parts):
@@ -411,37 +418,50 @@
     def of_chip(c):
         return jnp.concatenate([lax.dynamic_index_in_dim(rows, c, 0, keepdims=False), half])
 
-    total = of_chip(chip)
-    for e in range(1, chips):
-        total = total + permute(of_chip(chip ^ e), 2 * e, parts)
-    (later,) = wait_for([total], [last])
-    summed, half = later[:size], later[size:]
+    summed = lax.dynamic_index_in_dim(rows, chip, 0, keepdims=False)
+    others = [permute(of_chip(chip ^ e), 2 * e, parts) for e in range(1, chips)]
+    for other in wait_for(others, []):
+        summed, half = summed + other[:size], half + other[size:]
+    total = [summed, half]
+    summed, half = wait_for(total, [last])
     d = 1
-    while d < tensors:
+    while 2 * d < tensors:
         summed = summed + permute(summed, d, tensors, "tensor")
         d *= 2
+    beside = permute(summed, d, tensors, "tensor") if d < tensors else jnp.zeros_like(summed)
     other = permute(half, 1, parts)
-    whole = jnp.where(core == 0, jnp.concatenate([half, other]), jnp.concatenate([other, half]))
+    return total, [summed, beside], [half, other]
+
+
+def unpack(pieces, rows, halves, me, parts, after):
+    summed, beside, half, other = wait_for(list(rows) + list(halves), after)
+    summed = summed + beside
     out, start = [], 0
     for p in pieces:
-        rows = p.size // parts // width
-        out.append(summed[start : start + rows].reshape(-1, p.shape[1]))
-        start += rows
-    return out, whole, total
-
-
-def sum_halves(term, me, parts):
+        size = p.size // parts // summed.shape[1]
+        out.append(summed[start : start + size].reshape(-1, p.shape[1]))
+        start += size
+    first, second = jnp.where(me % 2 == 0, half, other), jnp.where(me % 2 == 0, other, half)
+    return out, jnp.concatenate([first, second])
+
+
+def sum_halves(term, me, parts, scale):
     core = me % 2
     half = term.shape[0] // 2
     term = term + permute(term, 1, parts)
-    return lax.dynamic_slice_in_dim(term, core * half, half, 0)
-
-
-def sum_all(mine, me, parts, after):
+    return lax.dynamic_slice_in_dim(term, core * half, half, 0) * scale
+
+
+def send_halves(mine, parts, after):
     (mine,) = wait_for([mine], after)
-    total = mine
-    for e in range(1, parts // 2):
-        total = total + permute(mine, 2 * e, parts)
+    return [mine] + [permute(mine, 2 * e, parts) for e in range(1, parts // 2)]
+
+
+def sum_all(halves, me, parts, after):
+    halves = wait_for(halves, after)
+    total = halves[0]
+    for half in halves[1:]:
+        total = total + half
     other = permute(total, 1, parts)
     return jnp.where(
         me % 2 == 0, jnp.concatenate([total, other]), jnp.concatenate([other, total])
@@ -480,43 +500,60 @@
     tail = 2 * (parts - 1) // 7
     se_out[-tail - 1 :] = wait_for(se_out[-tail - 1 :], [gwi_term])
     se_in = send(dist[:-tail], se_out[:-tail], received, window, parts)
-    last = wait_for(se_out[-tail:], se_in[1 : parts // 2])
+    last = wait_for(se_out[-tail:], se_in[1 : 1 + parts // 4])
     se_in += [permute(a, d, parts) for a, d in zip(last, dist[-tail:])]
-    state = ()
-    for i, (partner, second) in enumerate(zip(partners, se_in)):
-        if i == parts - 2:
-            (second,) = wait_for([second], se_in[-1:] + list(state[2:]))
+    arrays, terms = (), ()
+    late = parts - tail
+    for i in range(late):
+        *arrays, term = outputs_call(
+            partners[i], x3, ct3, gm, se_in[i], w_in, w_gate, w_out, arrays, terms
+        )
+        terms = [term]
         if i == 1:
-            early = state[2:]
-        if i == parts - 1:
-            middle = state[2:]
-        state = outputs_call(partner, x3, ct3, gm, second, w_in, w_gate, w_out, state)
-    outputs, grad_inputs, gw_term = state
-
+            early = terms
+    middle = se_in[late:] + terms
+    for i in range(late, parts):
+        terms = outputs_call(
+            partners[i], x3, ct3, gm, se_in[i], w_in, w_gate, w_out, None, terms
+        )
+    (gw_term,) = terms
     place = jnp.asarray([dist.index(d) for d in range(parts)], jnp.int32)
     natural = place[me ^ jnp.arange(parts, dtype=jnp.int32)]
     back = (natural[:, None] * blocks + jnp.arange(blocks, dtype=jnp.int32)).reshape(-1)
     fb_term = jnp.take(jnp.take(fb_term, back, axis=0), back, axis=1)
     fa_term, fb_term, gwi_term = wait_for([fa_term, fb_term, gwi_term], early)
-    gw_half = sum_halves(gw_term, me, parts)
-    (fa_sum, fb_sum), summed_in, total = sum_terms(
-        [fa_term, fb_term], gwi_term.reshape(-1, w_in.shape[1]), me, parts, tensors, middle, gw_half
-    )
     token_scale = 1.0 / math.sqrt(N1 * N2)
-    grad_factor_a = fa_sum / math.sqrt(N1 * D)
-    grad_factor_b = fb_sum / math.sqrt(N2 * D)
+    gw_half = sum_halves(gw_term, me, parts, token_scale)
+    pieces = [fa_term / math.sqrt(N1 * D), fb_term / math.sqrt(N2 * D)]
+    total, in_rows, in_halves = sum_terms(
+        pieces,
+        gwi_term.reshape(-1, w_in.shape[1]) * token_scale,
+        me,
+        parts,
+        tensors,
+        middle,
+        gw_half,
+    )
+    halves = send_halves(gw_half, parts, [])
+    se_in[late:] = wait_for(se_in[late:], in_rows[:1])
+    for i in range(late, parts):
+        arrays = outputs_call(
+            partners[i], x3, ct3, gm, se_in[i], w_in, w_gate, w_out, arrays, None
+        )
+    outputs, grad_inputs = arrays
+    summed = sum_all(halves, me, parts, arrays)
+    (fa_sum, fb_sum), summed_in = unpack(pieces, in_rows, in_halves, me, parts, arrays)
     summed_in = summed_in.reshape(w_in.shape)
-    summed = sum_all(gw_half, me, parts, [total])
     summed_gate, summed_out = jnp.split(summed, 2)
     return (
         outputs.reshape(rows, chans),
         grad_inputs.reshape(rows, chans),
         gk.reshape(rows, chans),
-        summed_in * token_scale,
-        summed_gate * token_scale,
-        summed_out * token_scale,
-        grad_factor_a,
-        grad_factor_b,
+        summed_in,
+        summed_gate,
+        summed_out,
+        fa_sum,
+        fb_sum,
     )
 
 

time: 621 us -> 620 us (level)
  waiting for transfers between devices: 297 us -> 278 us
  other arithmetic: 10.1 us -> 17.8 us
    ppermute x40, waiting for transfers between devices: 297 us -> 278 us  [permute(): return lax.ppermute(array, axis, [(i, i ^ d) for i in range(parts)])]
    pallas_call x8 -> x10, Pallas kernels: 62.8 us -> 69.4 us  [outputs_call(): pl.pallas_call(functools.partial(outputs_kernel, arrays is not None, term...]
    unnamed x45 -> x60, local copies, waits for them, and re-layouts: 15.8 us -> 19.6 us
  transfers between devices with their start and end apart: 40 -> 40, of which waited for: 19 -> 16; matrix products, arithmetic and copies ran while one was open for 5% -> 6% of each run, Pallas kernels for 33% -> 36%
where the time goes in v3:
time: 620 us; the launch traced here: 611 us
  waiting for transfers between devices  278 us (45%)
  Pallas kernels  221 us (36%)
  starting transfers between devices  54 us (9%)
  local copies, waits for them, and re-layouts  38.4 us (6%)
  other arithmetic  17.8 us (3%)
    ppermute x40, waiting for transfers between devices, permute(): return lax.ppermute(array, axis, [(i, i ^ d) for i in range(parts)])  278 us
    pallas_call x10, Pallas kernels, outputs_call(): pl.pallas_call(functools.partial(outputs_kernel, arrays is not None, term...  69.4 us
    ppermute x40, starting transfers between devices, permute(): return lax.ppermute(array, axis, [(i, i ^ d) for i in range(parts)])  54 us
    pallas_call x1, Pallas kernels, grad_mixed_call(): pl.pallas_call(functools.partial(grad_mixed_kernel, dist), grid_spec=pltp...  51.1 us
    pallas_call x1, Pallas kernels, twisted_call(): pl.pallas_call(functools.partial(twisted_kernel, dist), grid_spec=pltpu.P...  37.2 us
    pallas_call x8, Pallas kernels, grad_second_call(): pl.pallas_call(grad_second_kernel, grid_spec=pltpu.PrefetchScalarGridSpec...  30.9 us
    unnamed x60, local copies, waits for them, and re-layouts  19.6 us
    pallas_call x1, Pallas kernels, second_call(): pl.pallas_call(second_kernel, grid=(span // some,), in_specs=[whole] + [s...  18.6 us
  transfers between devices with their start and end apart: 40, of which 16 were waited for; matrix products, arithmetic and copies ran while one was open for 6% of the time, Pallas kernels for 36%

profile of v3, /device:TPU:0, one launch (start us, length us, event | category | flops | bytes accessed | tf_op | source)
XLA Modules:
  0.0 610.9 jit_solution(5760076357005630703)
XLA Ops:
  0.7 3.9 grad_second.12
  4.5 3.3 collective-permute-start.6
  7.9 3.9 grad_second.14
  12.3 3.9 grad_second.8
  17.6 3.9 grad_second.9
  22.6 3.9 grad_second.10
  27.0 3.9 grad_second.11.refs_0_
  30.8 12.2 %collective-permute-done.6.refs_1_.refs_9_ = bf16[64,32,384]{2,1,0:T(8,128)(2,1)S(1)} collective-permute-done((bf16[64,32,384]{2,1,0:T(8,128)(2,1)}, bf16[64,32,384]{2,1,0:T(8,128)(2,1)S(1)}, u32[]{:S(2)}, u32[]{:S(2)}) %collective-permute-start.6) | collective-permute-done | bytes 1572896 | tf_op jit(solution)/shard_map/ppermute | solution.py:382
  44.1 2.4 collective-permute-start.7
  46.5 2.1 copy.87
  48.6 3.9 grad_second.13.refs_0_
  52.4 37.2 %twisted.1 = (bf16[64,32,384]{2,1,0:T(8,128)(2,1)}, bf16[64,32,384]{2,1,0:T(8,128)(2,1)}, bf16[64,32,384]{2,1,0:T(8,128)(2,1)}, bf16[64,32,384]{2,1,0:T(8,128)(2...) custom-call(s32[1]{0:T(128)} %bitcast.3.me_ref.p_ref, ...), custom_call_target="tpu_custom_call" | custom-call | flops 805306368 | bytes 3774873 | tf_op jit(solution)/shard_map/twisted/pallas_call | solution.py:126
  92.5 18.1 %collective-permute-done.refs_1_.refs_11_.refs_3_ = bf16[64,32,384]{2,1,0:T(8,128)(2,1)} collective-permute-done((bf16[64,32,384]{2,1,0:T(8,128)(2,1)}, bf16[64,32,384]{2,1,0:T(8,128)(2,1)}, u32[]{:S(2)}, u32[]{:S(2)}) %collective-permute-start) | collective-permute-done | bytes 1572896 | tf_op jit(solution)/shard_map/ppermute | solution.py:382
  110.5 2.9 collective-permute-start.1
  115.5 29.4 %collective-permute-done.7.refs_1_.refs_14_.refs_6_ = bf16[64,32,384]{2,1,0:T(8,128)(2,1)S(1)} collective-permute-done((bf16[64,32,384]{2,1,0:T(8,128)(2,1)}, bf16[64,32,384]{2,1,0:T(8,128)(2,1)S(1)}, u32[]{:S(2)}, u32[]{:S(2)}) %collective-permute-start.7) | collective-permute-done | bytes 1572896 | tf_op jit(solution)/shard_map/ppermute | solution.py:382
  149.0 28.9 %collective-permute-done.1.refs_1_ = bf16[64,32,384]{2,1,0:T(8,128)(2,1)} collective-permute-done((bf16[64,32,384]{2,1,0:T(8,128)(2,1)}, bf16[64,32,384]{2,1,0:T(8,128)(2,1)}, u32[]{:S(2)}, u32[]{:S(2)}) %collective-permute-start.1) | collective-permute-done | bytes 1572896 | tf_op jit(solution)/shard_map/ppermute | solution.py:382
  177.9 2.5 collective-permute-start.12
  183.1 3.9 grad_second.15.refs_8_.refs_0_
  187.6 14.1 %grad_twisted.1 = (bf16[64,32,384]{2,1,0:T(8,128)(2,1)}, bf16[64,32,384]{2,1,0:T(8,128)(2,1)}, bf16[64,32,384]{2,1,0:T(8,128)(2,1)}, bf16[64,32,384]{2,1,0:T(8,1...) custom-call(bf16[256,256]{1,0:T(8,128)(2,1)} %fusion.13.fb_ref, ...), custom_call_target="tpu_custom_call" | custom-call | flops 322122560 | bytes 2516582 | tf_op jit(solution)/shard_map/grad_twisted/pallas_call | solution.py:164
  201.7 43.6 %collective-permute-done.5.refs_3_.refs_1_ = bf16[64,32,384]{2,1,0:T(8,128)(2,1)} collective-permute-done((bf16[64,32,384]{2,1,0:T(8,128)(2,1)}, bf16[64,32,384]{2,1,0:T(8,128)(2,1)}, u32[]{:S(2)}, u32[]{:S(2)}) %collective-permute-start.5) | collective-permute-done | bytes 1572896 | tf_op jit(solution)/shard_map/ppermute | solution.py:382
  245.3 2.9 collective-permute-start.14
  252.3 60.5 %collective-permute-done.12.refs_6_.refs_1_ = bf16[64,32,384]{2,1,0:T(8,128)(2,1)} collective-permute-done((bf16[64,32,384]{2,1,0:T(8,128)(2,1)}, bf16[64,32,384]{2,1,0:T(8,128)(2,1)}, u32[]{:S(2)}, u32[]{:S(2)}) %collective-permute-start.12) | collective-permute-done | bytes 1572896 | tf_op jit(solution)/shard_map/ppermute | solution.py:382
  312.8 1.9 collective-permute-start.17
  319.1 32.3 %collective-permute-done.15.refs_1_.rest_2_ = bf16[64,32,384]{2,1,0:T(8,128)(2,1)S(1)} collective-permute-done((bf16[64,32,384]{2,1,0:T(8,128)(2,1)}, bf16[64,32,384]{2,1,0:T(8,128)(2,1)S(1)}, u32[]{:S(2)}, u32[]{:S(2)}) %collective-permute-start.15) | collective-permute-done | bytes 1572896 | tf_op jit(solution)/shard_map/ppermute | solution.py:382
  355.7 18.6 %second.1 = (bf16[64,32,384]{2,1,0:T(8,128)(2,1)}, bf16[64,32,384]{2,1,0:T(8,128)(2,1)}, bf16[64,32,384]{2,1,0:T(8,128)(2,1)}, bf16[64,32,384]{2,1,0:T(8,128)(2,...) custom-call(bf16[256,256]{1,0:T(8,128)(2,1)} %copy.88.fbt_ref, ...), custom_call_target="tpu_custom_call" | custom-call | flops 644245120 | bytes 3774873 | tf_op jit(solution)/shard_map/second/pallas_call | solution.py:201
  374.3 5.8 collective-permute-done.16.rest_3_.refs_1_
  380.2 3.0 collective-permute-start.21
  396.1 17.8 %collective-permute-done.19.rest_6_.refs_1_ = bf16[64,32,384]{2,1,0:T(8,128)(2,1)} collective-permute-done((bf16[64,32,384]{2,1,0:T(8,128)(2,1)}, bf16[64,32,384]{2,1,0:T(8,128)(2,1)}, u32[]{:S(2)}, u32[]{:S(2)}) %collective-permute-start.19) | collective-permute-done | bytes 1572896 | tf_op jit(solution)/shard_map/ppermute | solution.py:382
  413.9 1.9 collective-permute-start.27
  415.8 3.3 collective-permute-done.20.rest_7_.refs_1_
  420.3 51.1 %grad_mixed.1 = (bf16[32,512,384]{2,1,0:T(8,128)(2,1)}, bf16[32,512,384]{2,1,0:T(8,128)(2,1)}, f32[512,512]{1,0:T(8,128)}, f32[3,128,128]{2,1,0:T(8,128)}) custom-call(s32[1]{0:T(128)} %bitcast.3.me_ref.p_ref, bf16[32,512,384]{2,1,0:T(8,128)(2,1)} %bitcast.81, bf16[32,512,384]{2,1,0:T(8,128)(2,1)} %bitcast.113, bf16[3,128,128]{2,1,0:T(8,128)(2,1)} %rest_1_.15, ...), custom_call_target="tpu_custom_call" | custom-call | flops 2254857728 | bytes 6291456 | tf_op jit(solution)/shard_map/grad_mixed/pallas_call | solution.py:265
  471.4 14.9 %collective-permute-done.22.refs_3_.se_ref = bf16[64,32,384]{2,1,0:T(8,128)(2,1)S(1)} collective-permute-done((bf16[64,32,384]{2,1,0:T(8,128)(2,1)}, bf16[64,32,384]{2,1,0:T(8,128)(2,1)S(1)}, u32[]{:S(2)}, u32[]{:S(2)}) %collective-permute-start.22) | collective-permute-done | bytes 1572896 | tf_op jit(solution)/shard_map/ppermute | solution.py:382
  490.7 7.7 %outputs.10 = (bf16[32,512,384]{2,1,0:T(8,128)(2,1)}, bf16[32,512,384]{2,1,0:T(8,128)(2,1)}, f32[6,128,128]{2,1,0:T(8,128)}) custom-call(s32[1]{0:T(128)} %bitcast.3.me_ref.p_ref, bf16[32,512,384]{2,1,0:T(8,128)(2,1)} %bitcast.82, bf16[32,512,384]{2,1,0:T(8,128)(2,1)} %bitcast.100, bf16[64,32,384]{2,1,0:T(8,128)(2,1)} %get-tuple-element.111.se_ref, ...), custom_call_target="tpu_custom_call" | custom-call | flops 140928608 | bytes 943718 | tf_op jit(solution)/shard_map/outputs/pallas_call | solution.py:351
  498.4 7.8 %outputs.11 = (bf16[32,512,384]{2,1,0:T(8,128)(2,1)}, bf16[32,512,384]{2,1,0:T(8,128)(2,1)}, f32[6,128,128]{2,1,0:T(8,128)}) custom-call(s32[1]{0:T(128)} %bitcast.5.p_ref, bf16[32,512,384]{2,1,0:T(8,128)(2,1)} %bitcast.83, bf16[32,512,384]{2,1,0:T(8,128)(2,1)} %bitcast.101, ...), custom_call_target="tpu_custom_call", output_to_operand_aliasing={{0}: (8, {}), {1}: (9, {})} | custom-call | flops 140928608 | bytes 943718 | tf_op jit(solution)/shard_map/outputs/pallas_call | solution.py:351
  506.2 2.4 broadcast_multiply_fusion
  508.6 2.3 reshape.340
  516.3 8.0 %outputs.12 = (bf16[32,512,384]{2,1,0:T(8,128)(2,1)}, bf16[32,512,384]{2,1,0:T(8,128)(2,1)}, f32[6,128,128]{2,1,0:T(8,128)}) custom-call(s32[1]{0:T(128)} %bitcast.7.p_ref, bf16[32,512,384]{2,1,0:T(8,128)(2,1)} %bitcast.84, bf16[32,512,384]{2,1,0:T(8,128)(2,1)} %bitcast.102, ...), custom_call_target="tpu_custom_call", output_to_operand_aliasing={{0}: (8, {}), {1}: (9, {})} | custom-call | flops 140928608 | bytes 943718 | tf_op jit(solution)/shard_map/outputs/pallas_call | solution.py:351
  524.3 7.8 %outputs.13 = (bf16[32,512,384]{2,1,0:T(8,128)(2,1)}, bf16[32,512,384]{2,1,0:T(8,128)(2,1)}, f32[6,128,128]{2,1,0:T(8,128)}) custom-call(s32[1]{0:T(128)} %bitcast.9.p_ref, bf16[32,512,384]{2,1,0:T(8,128)(2,1)} %bitcast.85, bf16[32,512,384]{2,1,0:T(8,128)(2,1)} %bitcast.103, ...), custom_call_target="tpu_custom_call", output_to_operand_aliasing={{0}: (8, {}), {1}: (9, {})} | custom-call | flops 140928608 | bytes 943718 | tf_op jit(solution)/shard_map/outputs/pallas_call | solution.py:351
  532.1 7.8 %outputs.14 = (bf16[32,512,384]{2,1,0:T(8,128)(2,1)}, bf16[32,512,384]{2,1,0:T(8,128)(2,1)}, f32[6,128,128]{2,1,0:T(8,128)}) custom-call(s32[1]{0:T(128)} %bitcast.11.p_ref, bf16[32,512,384]{2,1,0:T(8,128)(2,1)} %bitcast.86, bf16[32,512,384]{2,1,0:T(8,128)(2,1)} %bitcast.104, ...), custom_call_target="tpu_custom_call", output_to_operand_aliasing={{0}: (8, {}), {1}: (9, {})} | custom-call | flops 140928608 | bytes 943718 | tf_op jit(solution)/shard_map/outputs/pallas_call | solution.py:351
  540.0 2.1 maximum_add_fusion.refs_0_
  542.1 7.8 %outputs.15 = (bf16[32,512,384]{2,1,0:T(8,128)(2,1)}, bf16[32,512,384]{2,1,0:T(8,128)(2,1)}, f32[6,128,128]{2,1,0:T(8,128)}) custom-call(s32[1]{0:T(128)} %bitcast.13.p_ref, bf16[32,512,384]{2,1,0:T(8,128)(2,1)} %bitcast.87, bf16[32,512,384]{2,1,0:T(8,128)(2,1)} %bitcast.105, ...), custom_call_target="tpu_custom_call", output_to_operand_aliasing={{0}: (8, {}), {1}: (9, {})} | custom-call | flops 140928608 | bytes 943718 | tf_op jit(solution)/shard_map/outputs/pallas_call | solution.py:351
  549.9 3.8 collective-permute-done.24.refs_2_.se_ref.refs_1_
  560.5 5.0 outputs.16.rest_0_
  565.5 5.2 outputs.17
  582.3 3.9 collective-permute-done.33
  587.2 2.7 collective-permute-start.34
  589.8 6.1 %outputs.18 = (bf16[32,512,384]{2,1,0:T(8,128)(2,1)}, bf16[32,512,384]{2,1,0:T(8,128)(2,1)}) custom-call(s32[1]{0:T(128)} %bitcast.15.p_ref, bf16[32,512,384]{2,1,0:T(8,128)(2,1)} %bitcast.90, bf16[32,512,384]{2,1,0:T(8,128)(2,1)} %bitcast.108, bf16[64,32,384]{2,1,0:T(8,128)(2,1)} %get-tuple-element.139.se_ref, ...), custom_call_target="tpu_custom_call", output_to_operand_aliasing={{0}: (8, {}), {1}: (9, {})} | custom-call | flops 140928608 | bytes 943718 | tf_op jit(solution)/shard_map/outputs/pallas_call | solution.py:351
  596.0 6.1 %outputs.19 = (bf16[32,512,384]{2,1,0:T(8,128)(2,1)}, bf16[32,512,384]{2,1,0:T(8,128)(2,1)}) custom-call(s32[1]{0:T(128)} %bitcast.p_ref, bf16[32,512,384]{2,1,0:T(8,128)(2,1)} %bitcast.91, bf16[32,512,384]{2,1,0:T(8,128)(2,1)} %bitcast.109, bf16[64,32,384]{2,1,0:T(8,128)(2,1)} %get-tuple-element.138.se_ref, ...), custom_call_target="tpu_custom_call", output_to_operand_aliasing={{0}: (8, {}), {1}: (9, {})} | custom-call | flops 140928608 | bytes 943718 | tf_op jit(solution)/shard_map/outputs/pallas_call | solution.py:351
  (210 shorter events, 81.2 us)
Async XLA Ops:
  0.6 179.7 %copy-start = (bf16[256,256]{1,0:T(8,128)(2,1)S(1)}, bf16[256,256]{1,0:T(8,128)(2,1)}, u32[]{:S(2)}) copy-start(bf16[256,256]{1,0:T(8,128)(2,1)} %param.15) | copy-start | bytes 393220
  4.5 38.5 %collective-permute-start.6 = (bf16[64,32,384]{2,1,0:T(8,128)(2,1)}, bf16[64,32,384]{2,1,0:T(8,128)(2,1)S(1)}, u32[]{:S(2)}, u32[]{:S(2)}) collective-permute-start(bf16[64,32,384]{2,1,0:T(8,128)(2,1)} %grad_second.12), channel_id=1, source_target_pairs={{0,28},{4,24},{8,20},{12,16},{16,12},{20,8},{24,4},{28,0},{1,29},{... | collective-permute-start | bytes 4718600 | tf_op jit(solution)/shard_map/ppermute | solution.py:382
  11.7 77.9 %collective-permute-start.9 = (bf16[64,32,384]{2,1,0:T(8,128)(2,1)}, bf16[64,32,384]{2,1,0:T(8,128)(2,1)S(1)}, u32[]{:S(2)}, u32[]{:S(2)}) collective-permute-start(bf16[64,32,384]{2,1,0:T(8,128)(2,1)} %grad_second.14), channel_id=1, source_target_pairs={{0,24},{4,28},{8,16},{12,20},{16,8},{20,12},{24,0},{28,4},{1,25},{... | collective-permute-start | bytes 4718600 | tf_op jit(solution)/shard_map/ppermute | solution.py:382
  16.2 94.3 %collective-permute-start = (bf16[64,32,384]{2,1,0:T(8,128)(2,1)}, bf16[64,32,384]{2,1,0:T(8,128)(2,1)}, u32[]{:S(2)}, u32[]{:S(2)}) collective-permute-start(bf16[64,32,384]{2,1,0:T(8,128)(2,1)} %grad_second.8), channel_id=1, source_target_pairs={{0,20},{4,16},{8,28},{12,24},{16,4},{20,0},{24,12},{28,8},{1,21},{... | collective-permute-start | bytes 4718600 | tf_op jit(solution)/shard_map/ppermute | solution.py:382
  21.4 92.6 %collective-permute-start.2 = (bf16[64,32,384]{2,1,0:T(8,128)(2,1)}, bf16[64,32,384]{2,1,0:T(8,128)(2,1)}, u32[]{:S(2)}, u32[]{:S(2)}) collective-permute-start(bf16[64,32,384]{2,1,0:T(8,128)(2,1)} %grad_second.9), channel_id=1, source_target_pairs={{0,12},{4,8},{8,4},{12,0},{16,28},{20,24},{24,20},{28,16},{1,13},{... | collective-permute-start | bytes 4718600 | tf_op jit(solution)/shard_map/ppermute | solution.py:382
  26.5 86.9 %collective-permute-start.4 = (bf16[64,32,384]{2,1,0:T(8,128)(2,1)}, bf16[64,32,384]{2,1,0:T(8,128)(2,1)}, u32[]{:S(2)}, u32[]{:S(2)}) collective-permute-start(bf16[64,32,384]{2,1,0:T(8,128)(2,1)} %grad_second.10), channel_id=1, source_target_pairs={{0,4},{4,0},{8,12},{12,8},{16,20},{20,16},{24,28},{28,24},{1,5},{5... | collective-permute-start | bytes 4718600 | tf_op jit(solution)/shard_map/ppermute | solution.py:382
  44.1 100.8 %collective-permute-start.7 = (bf16[64,32,384]{2,1,0:T(8,128)(2,1)}, bf16[64,32,384]{2,1,0:T(8,128)(2,1)S(1)}, u32[]{:S(2)}, u32[]{:S(2)}) collective-permute-start(bf16[64,32,384]{2,1,0:T(8,128)(2,1)} %wait_for.34), channel_id=1, source_target_pairs={{0,16},{4,20},{8,24},{12,28},{16,0},{20,4},{24,8},{28,12},{1,17},{... | collective-permute-start | bytes 4718600 | tf_op jit(solution)/shard_map/ppermute | solution.py:382
  90.9 56.4 %collective-permute-start.10 = (bf16[64,32,384]{2,1,0:T(8,128)(2,1)}, bf16[64,32,384]{2,1,0:T(8,128)(2,1)S(1)}, u32[]{:S(2)}, u32[]{:S(2)}) collective-permute-start(bf16[64,32,384]{2,1,0:T(8,128)(2,1)} %wait_for.36), channel_id=1, source_target_pairs={{0,8},{4,12},{8,0},{12,4},{16,24},{20,28},{24,16},{28,20},{1,9},{5... | collective-permute-start | bytes 4718600 | tf_op jit(solution)/shard_map/ppermute | solution.py:382
  110.5 67.4 %collective-permute-start.1 = (bf16[64,32,384]{2,1,0:T(8,128)(2,1)}, bf16[64,32,384]{2,1,0:T(8,128)(2,1)}, u32[]{:S(2)}, u32[]{:S(2)}) collective-permute-start(bf16[64,32,384]{2,1,0:T(8,128)(2,1)} %wait_for.31), channel_id=1, source_target_pairs={{0,28},{4,24},{8,20},{12,16},{16,12},{20,8},{24,4},{28,0},{1,29},{... | collective-permute-start | bytes 4718600 | tf_op jit(solution)/shard_map/ppermute | solution.py:382
  113.4 131.9 %collective-permute-start.5 = (bf16[64,32,384]{2,1,0:T(8,128)(2,1)}, bf16[64,32,384]{2,1,0:T(8,128)(2,1)}, u32[]{:S(2)}, u32[]{:S(2)}) collective-permute-start(bf16[64,32,384]{2,1,0:T(8,128)(2,1)} %wait_for.33), channel_id=1, source_target_pairs={{0,20},{4,16},{8,28},{12,24},{16,4},{20,0},{24,12},{28,8},{1,21},{... | collective-permute-start | bytes 4718600 | tf_op jit(solution)/shard_map/ppermute | solution.py:382
  114.0 134.2 %collective-permute-start.3 = (bf16[64,32,384]{2,1,0:T(8,128)(2,1)}, bf16[64,32,384]{2,1,0:T(8,128)(2,1)}, u32[]{:S(2)}, u32[]{:S(2)}) collective-permute-start(bf16[64,32,384]{2,1,0:T(8,128)(2,1)} %wait_for.32), channel_id=1, source_target_pairs={{0,24},{4,28},{8,16},{12,20},{16,8},{20,12},{24,0},{28,4},{1,25},{... | collective-permute-start | bytes 4718600 | tf_op jit(solution)/shard_map/ppermute | solution.py:382
  146.1 102.7 %collective-permute-start.8 = (bf16[64,32,384]{2,1,0:T(8,128)(2,1)}, bf16[64,32,384]{2,1,0:T(8,128)(2,1)S(1)}, u32[]{:S(2)}, u32[]{:S(2)}) collective-permute-start(bf16[64,32,384]{2,1,0:T(8,128)(2,1)} %wait_for.35), channel_id=1, source_target_pairs={{0,12},{4,8},{8,4},{12,0},{16,28},{20,24},{24,20},{28,16},{1,13},{... | collective-permute-start | bytes 4718600 | tf_op jit(solution)/shard_map/ppermute | solution.py:382
  148.5 102.9 %collective-permute-start.11 = (bf16[64,32,384]{2,1,0:T(8,128)(2,1)}, bf16[64,32,384]{2,1,0:T(8,128)(2,1)}, u32[]{:S(2)}, u32[]{:S(2)}) collective-permute-start(bf16[64,32,384]{2,1,0:T(8,128)(2,1)} %wait_for.37), channel_id=1, source_target_pairs={{0,4},{4,0},{8,12},{12,8},{16,20},{20,16},{24,28},{28,24},{1,5},{5... | collective-permute-start | bytes 4718600 | tf_op jit(solution)/shard_map/ppermute | solution.py:382
  177.9 134.9 %collective-permute-start.12 = (bf16[64,32,384]{2,1,0:T(8,128)(2,1)}, bf16[64,32,384]{2,1,0:T(8,128)(2,1)}, u32[]{:S(2)}, u32[]{:S(2)}) collective-permute-start(bf16[64,32,384]{2,1,0:T(8,128)(2,1)} %wait_for.38), channel_id=1, source_target_pairs={{0,16},{4,20},{8,24},{12,28},{16,0},{20,4},{24,8},{28,12},{1,17},{... | collective-permute-start | bytes 4718600 | tf_op jit(solution)/shard_map/ppermute | solution.py:382
  245.3 69.4 %collective-permute-start.14 = (bf16[64,32,384]{2,1,0:T(8,128)(2,1)}, bf16[64,32,384]{2,1,0:T(8,128)(2,1)S(1)}, u32[]{:S(2)}, u32[]{:S(2)}) collective-permute-start(bf16[64,32,384]{2,1,0:T(8,128)(2,1)} %wait_for.40), channel_id=1, source_target_pairs={{0,28},{4,24},{8,20},{12,16},{16,12},{20,8},{24,4},{28,0},{1,29},{... | collective-permute-start | bytes 4718600 | tf_op jit(solution)/shard_map/ppermute | solution.py:382
  248.2 69.7 %collective-permute-start.13 = (bf16[64,32,384]{2,1,0:T(8,128)(2,1)}, bf16[64,32,384]{2,1,0:T(8,128)(2,1)S(1)}, u32[]{:S(2)}, u32[]{:S(2)}) collective-permute-start(bf16[64,32,384]{2,1,0:T(8,128)(2,1)} %wait_for.39), channel_id=1, source_target_pairs={{0,8},{4,12},{8,0},{12,4},{16,24},{20,28},{24,16},{28,20},{1,9},{5... | collective-permute-start | bytes 4718600 | tf_op jit(solution)/shard_map/ppermute | solution.py:382
  249.9 101.5 %collective-permute-start.15 = (bf16[64,32,384]{2,1,0:T(8,128)(2,1)}, bf16[64,32,384]{2,1,0:T(8,128)(2,1)S(1)}, u32[]{:S(2)}, u32[]{:S(2)}) collective-permute-start(bf16[64,32,384]{2,1,0:T(8,128)(2,1)} %wait_for.41), channel_id=1, source_target_pairs={{0,24},{4,28},{8,16},{12,20},{16,8},{20,12},{24,0},{28,4},{1,25},{... | collective-permute-start | bytes 4718600 | tf_op jit(solution)/shard_map/ppermute | solution.py:382
  251.4 128.8 %collective-permute-start.16 = (bf16[64,32,384]{2,1,0:T(8,128)(2,1)}, bf16[64,32,384]{2,1,0:T(8,128)(2,1)}, u32[]{:S(2)}, u32[]{:S(2)}) collective-permute-start(bf16[64,32,384]{2,1,0:T(8,128)(2,1)} %wait_for.42), channel_id=1, source_target_pairs={{0,20},{4,16},{8,28},{12,24},{16,4},{20,0},{24,12},{28,8},{1,21},{... | collective-permute-start | bytes 4718600 | tf_op jit(solution)/shard_map/ppermute | solution.py:382
  312.8 72.2 %collective-permute-start.17 = (bf16[64,32,384]{2,1,0:T(8,128)(2,1)}, bf16[64,32,384]{2,1,0:T(8,128)(2,1)}, u32[]{:S(2)}, u32[]{:S(2)}) collective-permute-start(bf16[64,32,384]{2,1,0:T(8,128)(2,1)} %wait_for.43), channel_id=1, source_target_pairs={{0,12},{4,8},{8,4},{12,0},{16,28},{20,24},{24,20},{28,16},{1,13},{... | collective-permute-start | bytes 4718600 | tf_op jit(solution)/shard_map/ppermute | solution.py:382
  315.9 98.0 %collective-permute-start.19 = (bf16[64,32,384]{2,1,0:T(8,128)(2,1)}, bf16[64,32,384]{2,1,0:T(8,128)(2,1)}, u32[]{:S(2)}, u32[]{:S(2)}) collective-permute-start(bf16[64,32,384]{2,1,0:T(8,128)(2,1)} %wait_for.45), channel_id=1, source_target_pairs={{0,16},{4,20},{8,24},{12,28},{16,0},{20,4},{24,8},{28,12},{1,17},{... | collective-permute-start | bytes 4718600 | tf_op jit(solution)/shard_map/ppermute | solution.py:382
  319.1 75.4 %collective-permute-start.18 = (bf16[64,32,384]{2,1,0:T(8,128)(2,1)}, bf16[64,32,384]{2,1,0:T(8,128)(2,1)}, u32[]{:S(2)}, u32[]{:S(2)}) collective-permute-start(bf16[64,32,384]{2,1,0:T(8,128)(2,1)} %wait_for.44), channel_id=1, source_target_pairs={{0,4},{4,0},{8,12},{12,8},{16,20},{20,16},{24,28},{28,24},{1,5},{5... | collective-permute-start | bytes 4718600 | tf_op jit(solution)/shard_map/ppermute | solution.py:382
  352.5 2.5 copy-start.2
  352.5 66.6 %collective-permute-start.20 = (bf16[64,32,384]{2,1,0:T(8,128)(2,1)}, bf16[64,32,384]{2,1,0:T(8,128)(2,1)S(1)}, u32[]{:S(2)}, u32[]{:S(2)}) collective-permute-start(bf16[64,32,384]{2,1,0:T(8,128)(2,1)} %wait_for.46), channel_id=1, source_target_pairs={{0,8},{4,12},{8,0},{12,4},{16,24},{20,28},{24,16},{28,20},{1,9},{5... | collective-permute-start | bytes 4718600 | tf_op jit(solution)/shard_map/ppermute | solution.py:382
  380.2 91.2 %collective-permute-start.21 = (bf16[64,32,384]{2,1,0:T(8,128)(2,1)}, bf16[64,32,384]{2,1,0:T(8,128)(2,1)}, u32[]{:S(2)}, u32[]{:S(2)}) collective-permute-start(bf16[64,32,384]{2,1,0:T(8,128)(2,1)} %wait_for.48), channel_id=1, source_target_pairs={{0,28},{4,24},{8,20},{12,16},{16,12},{20,8},{24,4},{28,0},{1,29},{... | collective-permute-start | bytes 4718600 | tf_op jit(solution)/shard_map/ppermute | solution.py:382
  385.0 101.3 %collective-permute-start.22 = (bf16[64,32,384]{2,1,0:T(8,128)(2,1)}, bf16[64,32,384]{2,1,0:T(8,128)(2,1)S(1)}, u32[]{:S(2)}, u32[]{:S(2)}) collective-permute-start(bf16[64,32,384]{2,1,0:T(8,128)(2,1)} %wait_for.49), channel_id=1, source_target_pairs={{0,24},{4,28},{8,16},{12,20},{16,8},{20,12},{24,0},{28,4},{1,25},{... | collective-permute-start | bytes 4718600 | tf_op jit(solution)/shard_map/ppermute | solution.py:382
  394.6 121.3 %collective-permute-start.28 = (bf16[64,32,384]{2,1,0:T(8,128)(2,1)}, bf16[64,32,384]{2,1,0:T(8,128)(2,1)}, u32[]{:S(2)}, u32[]{:S(2)}) collective-permute-start(bf16[64,32,384]{2,1,0:T(8,128)(2,1)} %wait_for.54), channel_id=1, source_target_pairs={{0,20},{4,16},{8,28},{12,24},{16,4},{20,0},{24,12},{28,8},{1,21},{... | collective-permute-start | bytes 4718600 | tf_op jit(solution)/shard_map/ppermute | solution.py:382
  413.9 118.2 %collective-permute-start.27 = (bf16[64,32,384]{2,1,0:T(8,128)(2,1)}, bf16[64,32,384]{2,1,0:T(8,128)(2,1)}, u32[]{:S(2)}, u32[]{:S(2)}) collective-permute-start(bf16[64,32,384]{2,1,0:T(8,128)(2,1)} %wait_for.53), channel_id=1, source_target_pairs={{0,12},{4,8},{8,4},{12,0},{16,28},{20,24},{24,20},{28,16},{1,13},{... | collective-permute-start | bytes 4718600 | tf_op jit(solution)/shard_map/ppermute | solution.py:382
  487.4 62.5 %collective-permute-start.23 = (bf16[64,32,384]{2,1,0:T(8,128)(2,1)}, bf16[64,32,384]{2,1,0:T(8,128)(2,1)S(1)}, u32[]{:S(2)}, u32[]{:S(2)}) collective-permute-start(bf16[64,32,384]{2,1,0:T(8,128)(2,1)} %get-tuple-element.106), channel_id=1, source_target_pairs={{0,16},{4,20},{8,24},{12,28},{16,0},{20,4},{24,8},{28,12},{1,17},{... | collective-permute-start | bytes 4718600 | tf_op jit(solution)/shard_map/ppermute | solution.py:382
  489.2 64.5 %collective-permute-start.24 = (bf16[64,32,384]{2,1,0:T(8,128)(2,1)}, bf16[64,32,384]{2,1,0:T(8,128)(2,1)S(1)}, u32[]{:S(2)}, u32[]{:S(2)}) collective-permute-start(bf16[64,32,384]{2,1,0:T(8,128)(2,1)} %get-tuple-element.107), channel_id=1, source_target_pairs={{0,8},{4,12},{8,0},{12,4},{16,24},{20,28},{24,16},{28,20},{1,9},{5... | collective-permute-start | bytes 4718600 | tf_op jit(solution)/shard_map/ppermute | solution.py:382
  490.7 51.4 %collective-permute-start.26 = (bf16[64,32,384]{2,1,0:T(8,128)(2,1)}, bf16[64,32,384]{2,1,0:T(8,128)(2,1)}, u32[]{:S(2)}, u32[]{:S(2)}) collective-permute-start(bf16[64,32,384]{2,1,0:T(8,128)(2,1)} %wait_for.52), channel_id=1, source_target_pairs={{0,4},{4,0},{8,12},{12,8},{16,20},{20,16},{24,28},{28,24},{1,5},{5... | collective-permute-start | bytes 4718600 | tf_op jit(solution)/shard_map/ppermute | solution.py:382
  508.5 2.3 copy-start.18
  515.8 24.1 %collective-permute-start.25 = (f32[1472,128]{1,0:T(8,128)}, f32[1472,128]{1,0:T(8,128)}, u32[]{:S(2)}, u32[]{:S(2)}) collective-permute-start(f32[1472,128]{1,0:T(8,128)} %pad_maximum_fusion), channel_id=1, source_target_pairs={{0,4},{4,0},{8,12},{12,8},{16,20},{20,16},{24,28},{28,24},{1,5},{5... | collective-permute-start | bytes 2261000 | tf_op jit(solution)/shard_map/ppermute | solution.py:382
  532.1 7.9 %copy-start.17 = (f32[4,1,320,128]{3,2,1,0:T(8,128)S(1)}, f32[4,1,320,128]{3,2,1,0:T(8,128)}, u32[]{:S(2)}) copy-start(f32[4,1,320,128]{3,2,1,0:T(8,128)} %get-tuple-element.156) | copy-start | bytes 1966084
  549.9 3.8 copy-start.3
  557.0 13.9 %collective-permute-start.31 = (f32[512,128]{1,0:T(8,128)S(1)}, f32[512,128]{1,0:T(8,128)S(1)}, u32[]{:S(2)}, u32[]{:S(2)}) collective-permute-start(f32[512,128]{1,0:T(8,128)S(1)} %get-tuple-element.167), channel_id=1, source_target_pairs={{0,24},{4,28},{8,16},{12,20},{16,8},{20,12},{24,0},{28,4},{1,25},{... | collective-permute-start | bytes 786440 | tf_op jit(solution)/shard_map/ppermute | solution.py:382
  558.5 13.1 %collective-permute-start.30 = (f32[512,128]{1,0:T(8,128)S(1)}, f32[512,128]{1,0:T(8,128)S(1)}, u32[]{:S(2)}, u32[]{:S(2)}) collective-permute-start(f32[512,128]{1,0:T(8,128)S(1)} %get-tuple-element.168), channel_id=1, source_target_pairs={{0,16},{4,20},{8,24},{12,28},{16,0},{20,4},{24,8},{28,12},{1,17},{... | collective-permute-start | bytes 786440 | tf_op jit(solution)/shard_map/ppermute | solution.py:382
  560.0 11.6 %collective-permute-start.29 = (f32[512,128]{1,0:T(8,128)S(1)}, f32[512,128]{1,0:T(8,128)S(1)}, u32[]{:S(2)}, u32[]{:S(2)}) collective-permute-start(f32[512,128]{1,0:T(8,128)S(1)} %get-tuple-element.169), channel_id=1, source_target_pairs={{0,8},{4,12},{8,0},{12,4},{16,24},{20,28},{24,16},{28,20},{1,9},{5... | collective-permute-start | bytes 786440 | tf_op jit(solution)/shard_map/ppermute | solution.py:382
  570.8 5.8 copy-start.23
  570.8 5.7 collective-permute-start.32
  577.2 24.9 %collective-permute-start.38 = (f32[3,128,128]{2,1,0:T(8,128)}, f32[3,128,128]{2,1,0:T(8,128)S(1)}, u32[]{:S(2)}, u32[]{:S(2)}) collective-permute-start(f32[3,128,128]{2,1,0:T(8,128)} %wait_for.60.refs_0_), channel_id=1, source_target_pairs={{0,24},{4,28},{8,16},{12,20},{16,8},{20,12},{24,0},{28,4},{1,25},{... | collective-permute-start | bytes 589832 | tf_op jit(solution)/shard_map/ppermute | solution.py:382
  578.7 23.5 %collective-permute-start.37 = (f32[3,128,128]{2,1,0:T(8,128)}, f32[3,128,128]{2,1,0:T(8,128)S(1)}, u32[]{:S(2)}, u32[]{:S(2)}) collective-permute-start(f32[3,128,128]{2,1,0:T(8,128)} %wait_for.60.refs_0_), channel_id=1, source_target_pairs={{0,16},{4,20},{8,24},{12,28},{16,0},{20,4},{24,8},{28,12},{1,17},{... | collective-permute-start | bytes 589832 | tf_op jit(solution)/shard_map/ppermute | solution.py:382
  579.5 22.7 %collective-permute-start.36 = (f32[3,128,128]{2,1,0:T(8,128)}, f32[3,128,128]{2,1,0:T(8,128)S(1)}, u32[]{:S(2)}, u32[]{:S(2)}) collective-permute-start(f32[3,128,128]{2,1,0:T(8,128)} %wait_for.60.refs_0_), channel_id=1, source_target_pairs={{0,8},{4,12},{8,0},{12,4},{16,24},{20,28},{24,16},{28,20},{1,9},{5... | collective-permute-start | bytes 589832 | tf_op jit(solution)/shard_map/ppermute | solution.py:382
  580.7 5.5 collective-permute-start.33
  582.3 22.0 %collective-permute-start.35 = (f32[192,128]{1,0:T(8,128)}, f32[192,128]{1,0:T(8,128)S(1)}, u32[]{:S(2)}, u32[]{:S(2)}) collective-permute-start(f32[192,128]{1,0:T(8,128)} %get-tuple-element.147.refs_2_), channel_id=1, source_target_pairs={{0,4},{4,0},{8,12},{12,8},{16,20},{20,16},{24,28},{28,24},{1,5},{5... | collective-permute-start | bytes 294920 | tf_op jit(solution)/shard_map/ppermute | solution.py:382
  587.2 2.7 copy-start.16
  587.2 17.1 %collective-permute-start.34 = (f32[320,128]{1,0:T(8,128)S(1)}, f32[320,128]{1,0:T(8,128)S(1)}, u32[]{:S(2)}, u32[]{:S(2)}) collective-permute-start(f32[320,128]{1,0:T(8,128)S(1)} %add.388.refs_2_.refs_0_), channel_id=1, source_target_pairs={{0,2},{1,3},{2,0},{3,1},{4,6},{5,7},{6,4},{7,5},{8,10},{9,11},{10,... | collective-permute-start | bytes 491528 | tf_op jit(solution)/shard_map/ppermute | solution.py:382
  604.2 5.4 collective-permute-start.39
  605.6 4.8 copy-start.1
  (21 other events, 21.1 us)

commit v4 on v3

--- a/solution.py
+++ b/solution.py
@@ -398,9 +398,9 @@
     return into
 
 
-def sum_terms(pieces, whole, me, parts, tensors, after, last):
+def sum_cores(pieces, whole, me, parts):
     chips = parts // 2
-    core, chip = me % 2, me // 2
+    core = me % 2
     width = whole.shape[-1]
     packed = jnp.concatenate([p.reshape(chips, 2, -1, width) for p in pieces], axis=2)
     halves = whole.reshape(2, -1, width)
@@ -410,27 +410,31 @@
         return jnp.concatenate([rows, lax.dynamic_index_in_dim(halves, c, 0, keepdims=False)])
 
     mine = of_core(core) + permute(of_core(1 - core), 1, parts)
-    (mine,) = wait_for([mine], after)
-    size = packed.shape[2]
-    rows = mine[: chips * size].reshape(chips, size, width)
-    half = mine[chips * size :]
+    size = chips * packed.shape[2]
+    return mine[:size], mine[size:]
+
+
+def sum_chips(rows, half, me, parts, tensors, after, last):
+    chips = parts // 2
+    chip = me // 2
+    rows = rows.reshape(chips, -1, rows.shape[1])
+    rows, half = wait_for([rows, half], after)
+    size = rows.shape[1]
 
     def of_chip(c):
         return jnp.concatenate([lax.dynamic_index_in_dim(rows, c, 0, keepdims=False), half])
 
+    others = [permute(of_chip(chip ^ e), 2 * e, parts) for e in range(1, chips)]
     summed = lax.dynamic_index_in_dim(rows, chip, 0, keepdims=False)
-    others = [permute(of_chip(chip ^ e), 2 * e, parts) for e in range(1, chips)]
     for other in wait_for(others, []):
         summed, half = summed + other[:size], half + other[size:]
-    total = [summed, half]
-    summed, half = wait_for(total, [last])
+    summed, half = wait_for([summed, half], [last])
     d = 1
     while 2 * d < tensors:
         summed = summed + permute(summed, d, tensors, "tensor")
         d *= 2
     beside = permute(summed, d, tensors, "tensor") if d < tensors else jnp.zeros_like(summed)
-    other = permute(half, 1, parts)
-    return total, [summed, beside], [half, other]
+    return [summed, beside], [half, permute(half, 1, parts)]
 
 
 def unpack(pieces, rows, halves, me, parts, after):
@@ -500,8 +504,6 @@
     tail = 2 * (parts - 1) // 7
     se_out[-tail - 1 :] = wait_for(se_out[-tail - 1 :], [gwi_term])
     se_in = send(dist[:-tail], se_out[:-tail], received, window, parts)
-    last = wait_for(se_out[-tail:], se_in[1 : 1 + parts // 4])
-    se_in += [permute(a, d, parts) for a, d in zip(last, dist[-tail:])]
     arrays, terms = (), ()
     late = parts - tail
     for i in range(late):
@@ -509,31 +511,28 @@
             partners[i], x3, ct3, gm, se_in[i], w_in, w_gate, w_out, arrays, terms
         )
         terms = [term]
-        if i == 1:
+        if i == 0:
             early = terms
-    middle = se_in[late:] + terms
+            place = jnp.asarray([dist.index(d) for d in range(parts)], jnp.int32)
+            natural = place[me ^ jnp.arange(parts, dtype=jnp.int32)]
+            back = (natural[:, None] * blocks + jnp.arange(blocks, dtype=jnp.int32)).reshape(-1)
+            fb_term = jnp.take(jnp.take(fb_term, back, axis=0), back, axis=1)
+            fa_term, fb_term, gwi_term = wait_for([fa_term, fb_term, gwi_term], early)
+            token_scale = 1.0 / math.sqrt(N1 * N2)
+            pieces = [fa_term / math.sqrt(N1 * D), fb_term / math.sqrt(N2 * D)]
+            in_rows, in_half = sum_cores(
+                pieces, gwi_term.reshape(-1, w_in.shape[1]) * token_scale, me, parts
+            )
+            last = wait_for(se_out[-tail:], se_in[1 : 1 + parts // 4] )
+            se_in += [permute(a, d, parts) for a, d in zip(last, dist[-tail:])]
+    middle = terms
     for i in range(late, parts):
         terms = outputs_call(
             partners[i], x3, ct3, gm, se_in[i], w_in, w_gate, w_out, None, terms
         )
     (gw_term,) = terms
-    place = jnp.asarray([dist.index(d) for d in range(parts)], jnp.int32)
-    natural = place[me ^ jnp.arange(parts, dtype=jnp.int32)]
-    back = (natural[:, None] * blocks + jnp.arange(blocks, dtype=jnp.int32)).reshape(-1)
-    fb_term = jnp.take(jnp.take(fb_term, back, axis=0), back, axis=1)
-    fa_term, fb_term, gwi_term = wait_for([fa_term, fb_term, gwi_term], early)
-    token_scale = 1.0 / math.sqrt(N1 * N2)
     gw_half = sum_halves(gw_term, me, parts, token_scale)
-    pieces = [fa_term / math.sqrt(N1 * D), fb_term / math.sqrt(N2 * D)]
-    total, in_rows, in_halves = sum_terms(
-        pieces,
-        gwi_term.reshape(-1, w_in.shape[1]) * token_scale,
-        me,
-        parts,
-        tensors,
-        middle,
-        gw_half,
-    )
+    in_rows, in_halves = sum_chips(in_rows, in_half, me, parts, tensors, middle, gw_half)
     halves = send_halves(gw_half, parts, [])
     se_in[late:] = wait_for(se_in[late:], in_rows[:1])
     for i in range(late, parts):

time: 620 us -> 630 us (1.016)
  waiting for transfers between devices: 278 us -> 300 us
  local copies, waits for them, and re-layouts: 38.4 us -> 29.7 us
    ppermute x40, waiting for transfers between devices: 278 us -> 300 us  [permute(): return lax.ppermute(array, axis, [(i, i ^ d) for i in range(parts)])]
    unnamed x60 -> x52, local copies, waits for them, and re-layouts: 19.6 us -> 15.3 us
  transfers between devices with their start and end apart: 40 -> 40, of which waited for: 16 -> 16; matrix products, arithmetic and copies ran while one was open for 6% -> 5% of each run, Pallas kernels for 36% -> 35%
where the time goes in v4:
time: 630 us; the launch traced here: 621 us
  waiting for transfers between devices  300 us (48%)
  Pallas kernels  221 us (35%)
  starting transfers between devices  50.5 us (8%)
  local copies, waits for them, and re-layouts  29.7 us (5%)
  other arithmetic  17.1 us (3%)
    ppermute x40, waiting for transfers between devices, permute(): return lax.ppermute(array, axis, [(i, i ^ d) for i in range(parts)])  300 us
    pallas_call x10, Pallas kernels, outputs_call(): pl.pallas_call(functools.partial(outputs_kernel, arrays is not None, term...  69.4 us
    pallas_call x1, Pallas kernels, grad_mixed_call(): pl.pallas_call(functools.partial(grad_mixed_kernel, dist), grid_spec=pltp...  51.1 us
    ppermute x40, starting transfers between devices, permute(): return lax.ppermute(array, axis, [(i, i ^ d) for i in range(parts)])  50.5 us
    pallas_call x1, Pallas kernels, twisted_call(): pl.pallas_call(functools.partial(twisted_kernel, dist), grid_spec=pltpu.P...  37.2 us
    pallas_call x8, Pallas kernels, grad_second_call(): pl.pallas_call(grad_second_kernel, grid_spec=pltpu.PrefetchScalarGridSpec...  31 us
    pallas_call x1, Pallas kernels, second_call(): pl.pallas_call(second_kernel, grid=(span // some,), in_specs=[whole] + [s...  18.6 us
    unnamed x52, local copies, waits for them, and re-layouts  15.3 us
  transfers between devices with their start and end apart: 40, of which 16 were waited for; matrix products, arithmetic and copies ran while one was open for 5% of the time, Pallas kernels for 35%

profile of v4, /device:TPU:0, one launch (start us, length us, event | category | flops | bytes accessed | tf_op | source)
XLA Modules:
  0.0 620.5 jit_solution(17462917176418494228)
XLA Ops:
  0.7 3.9 grad_second.12
  4.5 3.3 collective-permute-start.6
  7.9 3.8 grad_second.8
  12.5 3.8 grad_second.9
  16.4 3.9 grad_second.10
  20.3 3.9 grad_second.14
  24.2 3.0 collective-permute-start.9
  27.2 3.9 grad_second.11.refs_0_
  31.1 12.0 %collective-permute-done.6.refs_1_.refs_9_ = bf16[64,32,384]{2,1,0:T(8,128)(2,1)S(1)} collective-permute-done((bf16[64,32,384]{2,1,0:T(8,128)(2,1)}, bf16[64,32,384]{2,1,0:T(8,128)(2,1)S(1)}, u32[]{:S(2)}, u32[]{:S(2)}) %collective-permute-start.6) | collective-permute-done | bytes 1572896 | tf_op jit(solution)/shard_map/ppermute | solution.py:382
  44.1 2.4 collective-permute-start.7
  46.5 2.1 copy.88
  48.6 3.9 grad_second.13.refs_0_
  52.5 37.2 %twisted.1 = (bf16[64,32,384]{2,1,0:T(8,128)(2,1)}, bf16[64,32,384]{2,1,0:T(8,128)(2,1)}, bf16[64,32,384]{2,1,0:T(8,128)(2,1)}, bf16[64,32,384]{2,1,0:T(8,128)(2...) custom-call(s32[1]{0:T(128)} %bitcast.3.me_ref.p_ref, ...), custom_call_target="tpu_custom_call" | custom-call | flops 805306368 | bytes 3774873 | tf_op jit(solution)/shard_map/twisted/pallas_call | solution.py:126
  93.7 17.8 %collective-permute-done.9.refs_1_.refs_10_.refs_2_ = bf16[64,32,384]{2,1,0:T(8,128)(2,1)} collective-permute-done((bf16[64,32,384]{2,1,0:T(8,128)(2,1)}, bf16[64,32,384]{2,1,0:T(8,128)(2,1)}, u32[]{:S(2)}, u32[]{:S(2)}) %collective-permute-start.9) | collective-permute-done | bytes 1572896 | tf_op jit(solution)/shard_map/ppermute | solution.py:382
  112.9 98.7 %collective-permute-done.7.refs_1_.refs_14_.refs_6_ = bf16[64,32,384]{2,1,0:T(8,128)(2,1)S(1)} collective-permute-done((bf16[64,32,384]{2,1,0:T(8,128)(2,1)}, bf16[64,32,384]{2,1,0:T(8,128)(2,1)S(1)}, u32[]{:S(2)}, u32[]{:S(2)}) %collective-permute-start.7) | collective-permute-done | bytes 1572896 | tf_op jit(solution)/shard_map/ppermute | solution.py:382
  217.4 3.9 grad_second.15.refs_8_.refs_0_
  225.7 14.0 %grad_twisted.1 = (bf16[64,32,384]{2,1,0:T(8,128)(2,1)}, bf16[64,32,384]{2,1,0:T(8,128)(2,1)}, bf16[64,32,384]{2,1,0:T(8,128)(2,1)}, bf16[64,32,384]{2,1,0:T(8,1...) custom-call(bf16[256,256]{1,0:T(8,128)(2,1)} %fusion.13.fb_ref, ...), custom_call_target="tpu_custom_call" | custom-call | flops 322122560 | bytes 2516582 | tf_op jit(solution)/shard_map/grad_twisted/pallas_call | solution.py:164
  239.8 5.5 collective-permute-done.5.refs_3_.refs_1_
  245.3 3.0 collective-permute-start.14
  249.7 2.9 collective-permute-start.15
  253.8 25.3 %collective-permute-done.12.refs_6_.refs_1_ = bf16[64,32,384]{2,1,0:T(8,128)(2,1)} collective-permute-done((bf16[64,32,384]{2,1,0:T(8,128)(2,1)}, bf16[64,32,384]{2,1,0:T(8,128)(2,1)}, u32[]{:S(2)}, u32[]{:S(2)}) %collective-permute-start.12) | collective-permute-done | bytes 1572896 | tf_op jit(solution)/shard_map/ppermute | solution.py:382
  281.0 3.3 collective-permute-done.13.refs_7_.refs_1_
  284.3 34.5 %collective-permute-done.14.refs_1_.rest_1_ = bf16[64,32,384]{2,1,0:T(8,128)(2,1)S(1)} collective-permute-done((bf16[64,32,384]{2,1,0:T(8,128)(2,1)}, bf16[64,32,384]{2,1,0:T(8,128)(2,1)S(1)}, u32[]{:S(2)}, u32[]{:S(2)}) %collective-permute-start.14) | collective-permute-done | bytes 1572896 | tf_op jit(solution)/shard_map/ppermute | solution.py:382
  319.9 32.8 %collective-permute-done.15.refs_1_.rest_2_ = bf16[64,32,384]{2,1,0:T(8,128)(2,1)S(1)} collective-permute-done((bf16[64,32,384]{2,1,0:T(8,128)(2,1)}, bf16[64,32,384]{2,1,0:T(8,128)(2,1)S(1)}, u32[]{:S(2)}, u32[]{:S(2)}) %collective-permute-start.15) | collective-permute-done | bytes 1572896 | tf_op jit(solution)/shard_map/ppermute | solution.py:382
  356.5 18.6 %second.1 = (bf16[64,32,384]{2,1,0:T(8,128)(2,1)}, bf16[64,32,384]{2,1,0:T(8,128)(2,1)}, bf16[64,32,384]{2,1,0:T(8,128)(2,1)}, bf16[64,32,384]{2,1,0:T(8,128)(2,...) custom-call(bf16[256,256]{1,0:T(8,128)(2,1)} %copy.89.fbt_ref, ...), custom_call_target="tpu_custom_call" | custom-call | flops 644245120 | bytes 3774873 | tf_op jit(solution)/shard_map/second/pallas_call | solution.py:201
  375.0 1.9 gather_fusion.3
  380.1 3.0 collective-permute-start.21
  384.6 2.9 collective-permute-start.22
  387.5 26.4 %collective-permute-done.19.rest_6_.refs_1_ = bf16[64,32,384]{2,1,0:T(8,128)(2,1)} collective-permute-done((bf16[64,32,384]{2,1,0:T(8,128)(2,1)}, bf16[64,32,384]{2,1,0:T(8,128)(2,1)}, u32[]{:S(2)}, u32[]{:S(2)}) %collective-permute-start.19) | collective-permute-done | bytes 1572896 | tf_op jit(solution)/shard_map/ppermute | solution.py:382
  413.9 1.9 collective-permute-start.27
  420.2 51.1 %grad_mixed.1 = (bf16[32,512,384]{2,1,0:T(8,128)(2,1)}, bf16[32,512,384]{2,1,0:T(8,128)(2,1)}, f32[512,512]{1,0:T(8,128)}, f32[3,128,128]{2,1,0:T(8,128)}) custom-call(s32[1]{0:T(128)} %bitcast.3.me_ref.p_ref, bf16[32,512,384]{2,1,0:T(8,128)(2,1)} %bitcast.81, bf16[32,512,384]{2,1,0:T(8,128)(2,1)} %bitcast.113, bf16[3,128,128]{2,1,0:T(8,128)(2,1)} %rest_1_.15, ...), custom_call_target="tpu_custom_call" | custom-call | flops 2254857728 | bytes 6291456 | tf_op jit(solution)/shard_map/grad_mixed/pallas_call | solution.py:265
  471.2 7.7 %outputs.10 = (bf16[32,512,384]{2,1,0:T(8,128)(2,1)}, bf16[32,512,384]{2,1,0:T(8,128)(2,1)}, f32[6,128,128]{2,1,0:T(8,128)}) custom-call(s32[1]{0:T(128)} %bitcast.3.me_ref.p_ref, bf16[32,512,384]{2,1,0:T(8,128)(2,1)} %bitcast.82, bf16[32,512,384]{2,1,0:T(8,128)(2,1)} %bitcast.100, bf16[64,32,384]{2,1,0:T(8,128)(2,1)} %get-tuple-element.112.se_ref, ...), custom_call_target="tpu_custom_call" | custom-call | flops 140928608 | bytes 943718 | tf_op jit(solution)/shard_map/outputs/pallas_call | solution.py:351
  478.9 2.3 broadcast_multiply_fusion
  485.3 2.4 collective-permute-done.22.refs_3_.se_ref
  488.0 31.6 %collective-permute-done.28.se_ref = bf16[64,32,384]{2,1,0:T(8,128)(2,1)} collective-permute-done((bf16[64,32,384]{2,1,0:T(8,128)(2,1)}, bf16[64,32,384]{2,1,0:T(8,128)(2,1)}, u32[]{:S(2)}, u32[]{:S(2)}) %collective-permute-start.28) | collective-permute-done | bytes 1572896 | tf_op jit(solution)/shard_map/ppermute | solution.py:382
  520.4 7.8 %outputs.11 = (bf16[32,512,384]{2,1,0:T(8,128)(2,1)}, bf16[32,512,384]{2,1,0:T(8,128)(2,1)}, f32[6,128,128]{2,1,0:T(8,128)}) custom-call(s32[1]{0:T(128)} %bitcast.5.p_ref, bf16[32,512,384]{2,1,0:T(8,128)(2,1)} %bitcast.83, bf16[32,512,384]{2,1,0:T(8,128)(2,1)} %bitcast.101, ...), custom_call_target="tpu_custom_call", output_to_operand_aliasing={{0}: (8, {}), {1}: (9, {})} | custom-call | flops 140928608 | bytes 943718 | tf_op jit(solution)/shard_map/outputs/pallas_call | solution.py:351
  528.2 8.0 %outputs.12 = (bf16[32,512,384]{2,1,0:T(8,128)(2,1)}, bf16[32,512,384]{2,1,0:T(8,128)(2,1)}, f32[6,128,128]{2,1,0:T(8,128)}) custom-call(s32[1]{0:T(128)} %bitcast.7.p_ref, bf16[32,512,384]{2,1,0:T(8,128)(2,1)} %bitcast.84, bf16[32,512,384]{2,1,0:T(8,128)(2,1)} %bitcast.102, ...), custom_call_target="tpu_custom_call", output_to_operand_aliasing={{0}: (8, {}), {1}: (9, {})} | custom-call | flops 140928608 | bytes 943718 | tf_op jit(solution)/shard_map/outputs/pallas_call | solution.py:351
  536.2 7.8 %outputs.13 = (bf16[32,512,384]{2,1,0:T(8,128)(2,1)}, bf16[32,512,384]{2,1,0:T(8,128)(2,1)}, f32[6,128,128]{2,1,0:T(8,128)}) custom-call(s32[1]{0:T(128)} %bitcast.9.p_ref, bf16[32,512,384]{2,1,0:T(8,128)(2,1)} %bitcast.85, bf16[32,512,384]{2,1,0:T(8,128)(2,1)} %bitcast.103, ...), custom_call_target="tpu_custom_call", output_to_operand_aliasing={{0}: (8, {}), {1}: (9, {})} | custom-call | flops 140928608 | bytes 943718 | tf_op jit(solution)/shard_map/outputs/pallas_call | solution.py:351
  544.1 7.8 %outputs.14 = (bf16[32,512,384]{2,1,0:T(8,128)(2,1)}, bf16[32,512,384]{2,1,0:T(8,128)(2,1)}, f32[6,128,128]{2,1,0:T(8,128)}) custom-call(s32[1]{0:T(128)} %bitcast.11.p_ref, bf16[32,512,384]{2,1,0:T(8,128)(2,1)} %bitcast.86, bf16[32,512,384]{2,1,0:T(8,128)(2,1)} %bitcast.104, ...), custom_call_target="tpu_custom_call", output_to_operand_aliasing={{0}: (8, {}), {1}: (9, {})} | custom-call | flops 140928608 | bytes 943718 | tf_op jit(solution)/shard_map/outputs/pallas_call | solution.py:351
  554.7 7.8 %outputs.15 = (bf16[32,512,384]{2,1,0:T(8,128)(2,1)}, bf16[32,512,384]{2,1,0:T(8,128)(2,1)}, f32[6,128,128]{2,1,0:T(8,128)}) custom-call(s32[1]{0:T(128)} %bitcast.13.p_ref, bf16[32,512,384]{2,1,0:T(8,128)(2,1)} %bitcast.87, bf16[32,512,384]{2,1,0:T(8,128)(2,1)} %bitcast.105, ...), custom_call_target="tpu_custom_call", output_to_operand_aliasing={{0}: (8, {}), {1}: (9, {})} | custom-call | flops 140928608 | bytes 943718 | tf_op jit(solution)/shard_map/outputs/pallas_call | solution.py:351
  563.6 1.8 pad_maximum_fusion.1
  570.1 5.0 outputs.16.rest_0_
  576.2 5.2 outputs.17
  583.9 1.8 fusion.2.refs_0_
  591.5 4.4 collective-permute-done.33
  596.8 2.6 collective-permute-start.34
  599.5 6.1 outputs.18
  605.6 6.1 outputs.19
  (202 shorter events, 68.0 us)
Async XLA Ops:
  0.6 214.1 %copy-start = (bf16[256,256]{1,0:T(8,128)(2,1)S(1)}, bf16[256,256]{1,0:T(8,128)(2,1)}, u32[]{:S(2)}) copy-start(bf16[256,256]{1,0:T(8,128)(2,1)} %param.15) | copy-start | bytes 393220
  4.5 38.5 %collective-permute-start.6 = (bf16[64,32,384]{2,1,0:T(8,128)(2,1)}, bf16[64,32,384]{2,1,0:T(8,128)(2,1)S(1)}, u32[]{:S(2)}, u32[]{:S(2)}) collective-permute-start(bf16[64,32,384]{2,1,0:T(8,128)(2,1)} %grad_second.12), channel_id=1, source_target_pairs={{0,28},{4,24},{8,20},{12,16},{16,12},{20,8},{24,4},{28,0},{1,29},{... | collective-permute-start | bytes 4718600 | tf_op jit(solution)/shard_map/ppermute | solution.py:382
  11.7 78.0 %collective-permute-start = (bf16[64,32,384]{2,1,0:T(8,128)(2,1)}, bf16[64,32,384]{2,1,0:T(8,128)(2,1)S(1)}, u32[]{:S(2)}, u32[]{:S(2)}) collective-permute-start(bf16[64,32,384]{2,1,0:T(8,128)(2,1)} %grad_second.8), channel_id=1, source_target_pairs={{0,20},{4,16},{8,28},{12,24},{16,4},{20,0},{24,12},{28,8},{1,21},{... | collective-permute-start | bytes 4718600 | tf_op jit(solution)/shard_map/ppermute | solution.py:382
  16.3 75.4 %collective-permute-start.2 = (bf16[64,32,384]{2,1,0:T(8,128)(2,1)}, bf16[64,32,384]{2,1,0:T(8,128)(2,1)}, u32[]{:S(2)}, u32[]{:S(2)}) collective-permute-start(bf16[64,32,384]{2,1,0:T(8,128)(2,1)} %grad_second.9), channel_id=1, source_target_pairs={{0,12},{4,8},{8,4},{12,0},{16,28},{20,24},{24,20},{28,16},{1,13},{... | collective-permute-start | bytes 4718600 | tf_op jit(solution)/shard_map/ppermute | solution.py:382
  20.3 72.9 %collective-permute-start.4 = (bf16[64,32,384]{2,1,0:T(8,128)(2,1)}, bf16[64,32,384]{2,1,0:T(8,128)(2,1)}, u32[]{:S(2)}, u32[]{:S(2)}) collective-permute-start(bf16[64,32,384]{2,1,0:T(8,128)(2,1)} %grad_second.10), channel_id=1, source_target_pairs={{0,4},{4,0},{8,12},{12,8},{16,20},{20,16},{24,28},{28,24},{1,5},{5... | collective-permute-start | bytes 4718600 | tf_op jit(solution)/shard_map/ppermute | solution.py:382
  24.2 87.3 %collective-permute-start.9 = (bf16[64,32,384]{2,1,0:T(8,128)(2,1)}, bf16[64,32,384]{2,1,0:T(8,128)(2,1)}, u32[]{:S(2)}, u32[]{:S(2)}) collective-permute-start(bf16[64,32,384]{2,1,0:T(8,128)(2,1)} %grad_second.14), channel_id=1, source_target_pairs={{0,24},{4,28},{8,16},{12,20},{16,8},{20,12},{24,0},{28,4},{1,25},{... | collective-permute-start | bytes 4718600 | tf_op jit(solution)/shard_map/ppermute | solution.py:382
  44.1 167.5 %collective-permute-start.7 = (bf16[64,32,384]{2,1,0:T(8,128)(2,1)}, bf16[64,32,384]{2,1,0:T(8,128)(2,1)S(1)}, u32[]{:S(2)}, u32[]{:S(2)}) collective-permute-start(bf16[64,32,384]{2,1,0:T(8,128)(2,1)} %wait_for.34), channel_id=1, source_target_pairs={{0,16},{4,20},{8,24},{12,28},{16,0},{20,4},{24,8},{28,12},{1,17},{... | collective-permute-start | bytes 4718600 | tf_op jit(solution)/shard_map/ppermute | solution.py:382
  90.9 132.7 %collective-permute-start.1 = (bf16[64,32,384]{2,1,0:T(8,128)(2,1)}, bf16[64,32,384]{2,1,0:T(8,128)(2,1)}, u32[]{:S(2)}, u32[]{:S(2)}) collective-permute-start(bf16[64,32,384]{2,1,0:T(8,128)(2,1)} %wait_for.31), channel_id=1, source_target_pairs={{0,28},{4,24},{8,20},{12,16},{16,12},{20,8},{24,4},{28,0},{1,29},{... | collective-permute-start | bytes 4718600 | tf_op jit(solution)/shard_map/ppermute | solution.py:382
  91.8 133.3 %collective-permute-start.3 = (bf16[64,32,384]{2,1,0:T(8,128)(2,1)}, bf16[64,32,384]{2,1,0:T(8,128)(2,1)}, u32[]{:S(2)}, u32[]{:S(2)}) collective-permute-start(bf16[64,32,384]{2,1,0:T(8,128)(2,1)} %wait_for.32), channel_id=1, source_target_pairs={{0,24},{4,28},{8,16},{12,20},{16,8},{20,12},{24,0},{28,4},{1,25},{... | collective-permute-start | bytes 4718600 | tf_op jit(solution)/shard_map/ppermute | solution.py:382
  93.3 152.0 %collective-permute-start.5 = (bf16[64,32,384]{2,1,0:T(8,128)(2,1)}, bf16[64,32,384]{2,1,0:T(8,128)(2,1)}, u32[]{:S(2)}, u32[]{:S(2)}) collective-permute-start(bf16[64,32,384]{2,1,0:T(8,128)(2,1)} %wait_for.33), channel_id=1, source_target_pairs={{0,20},{4,16},{8,28},{12,24},{16,4},{20,0},{24,12},{28,8},{1,21},{... | collective-permute-start | bytes 4718600 | tf_op jit(solution)/shard_map/ppermute | solution.py:382
  111.5 110.4 %collective-permute-start.10 = (bf16[64,32,384]{2,1,0:T(8,128)(2,1)}, bf16[64,32,384]{2,1,0:T(8,128)(2,1)S(1)}, u32[]{:S(2)}, u32[]{:S(2)}) collective-permute-start(bf16[64,32,384]{2,1,0:T(8,128)(2,1)} %wait_for.36), channel_id=1, source_target_pairs={{0,8},{4,12},{8,0},{12,4},{16,24},{20,28},{24,16},{28,20},{1,9},{5... | collective-permute-start | bytes 4718600 | tf_op jit(solution)/shard_map/ppermute | solution.py:382
  212.8 36.9 %collective-permute-start.8 = (bf16[64,32,384]{2,1,0:T(8,128)(2,1)}, bf16[64,32,384]{2,1,0:T(8,128)(2,1)}, u32[]{:S(2)}, u32[]{:S(2)}) collective-permute-start(bf16[64,32,384]{2,1,0:T(8,128)(2,1)} %wait_for.35), channel_id=1, source_target_pairs={{0,12},{4,8},{8,4},{12,0},{16,28},{20,24},{24,20},{28,16},{1,13},{... | collective-permute-start | bytes 4718600 | tf_op jit(solution)/shard_map/ppermute | solution.py:382
  223.1 30.2 %collective-permute-start.11 = (bf16[64,32,384]{2,1,0:T(8,128)(2,1)}, bf16[64,32,384]{2,1,0:T(8,128)(2,1)}, u32[]{:S(2)}, u32[]{:S(2)}) collective-permute-start(bf16[64,32,384]{2,1,0:T(8,128)(2,1)} %wait_for.37), channel_id=1, source_target_pairs={{0,4},{4,0},{8,12},{12,8},{16,20},{20,16},{24,28},{28,24},{1,5},{5... | collective-permute-start | bytes 4718600 | tf_op jit(solution)/shard_map/ppermute | solution.py:382
  223.7 55.5 %collective-permute-start.12 = (bf16[64,32,384]{2,1,0:T(8,128)(2,1)}, bf16[64,32,384]{2,1,0:T(8,128)(2,1)}, u32[]{:S(2)}, u32[]{:S(2)}) collective-permute-start(bf16[64,32,384]{2,1,0:T(8,128)(2,1)} %wait_for.38), channel_id=1, source_target_pairs={{0,16},{4,20},{8,24},{12,28},{16,0},{20,4},{24,8},{28,12},{1,17},{... | collective-permute-start | bytes 4718600 | tf_op jit(solution)/shard_map/ppermute | solution.py:382
  225.1 59.1 %collective-permute-start.13 = (bf16[64,32,384]{2,1,0:T(8,128)(2,1)}, bf16[64,32,384]{2,1,0:T(8,128)(2,1)}, u32[]{:S(2)}, u32[]{:S(2)}) collective-permute-start(bf16[64,32,384]{2,1,0:T(8,128)(2,1)} %wait_for.39), channel_id=1, source_target_pairs={{0,8},{4,12},{8,0},{12,4},{16,24},{20,28},{24,16},{28,20},{1,9},{5... | collective-permute-start | bytes 4718600 | tf_op jit(solution)/shard_map/ppermute | solution.py:382
  245.3 73.5 %collective-permute-start.14 = (bf16[64,32,384]{2,1,0:T(8,128)(2,1)}, bf16[64,32,384]{2,1,0:T(8,128)(2,1)S(1)}, u32[]{:S(2)}, u32[]{:S(2)}) collective-permute-start(bf16[64,32,384]{2,1,0:T(8,128)(2,1)} %wait_for.40), channel_id=1, source_target_pairs={{0,28},{4,24},{8,20},{12,16},{16,12},{20,8},{24,4},{28,0},{1,29},{... | collective-permute-start | bytes 4718600 | tf_op jit(solution)/shard_map/ppermute | solution.py:382
  249.7 2.9 copy-start.2
  249.7 103.0 %collective-permute-start.15 = (bf16[64,32,384]{2,1,0:T(8,128)(2,1)}, bf16[64,32,384]{2,1,0:T(8,128)(2,1)S(1)}, u32[]{:S(2)}, u32[]{:S(2)}) collective-permute-start(bf16[64,32,384]{2,1,0:T(8,128)(2,1)} %wait_for.41), channel_id=1, source_target_pairs={{0,24},{4,28},{8,16},{12,20},{16,8},{20,12},{24,0},{28,4},{1,25},{... | collective-permute-start | bytes 4718600 | tf_op jit(solution)/shard_map/ppermute | solution.py:382
  253.3 126.8 %collective-permute-start.16 = (bf16[64,32,384]{2,1,0:T(8,128)(2,1)}, bf16[64,32,384]{2,1,0:T(8,128)(2,1)}, u32[]{:S(2)}, u32[]{:S(2)}) collective-permute-start(bf16[64,32,384]{2,1,0:T(8,128)(2,1)} %wait_for.42), channel_id=1, source_target_pairs={{0,20},{4,16},{8,28},{12,24},{16,4},{20,0},{24,12},{28,8},{1,21},{... | collective-permute-start | bytes 4718600 | tf_op jit(solution)/shard_map/ppermute | solution.py:382
  279.1 105.4 %collective-permute-start.17 = (bf16[64,32,384]{2,1,0:T(8,128)(2,1)}, bf16[64,32,384]{2,1,0:T(8,128)(2,1)}, u32[]{:S(2)}, u32[]{:S(2)}) collective-permute-start(bf16[64,32,384]{2,1,0:T(8,128)(2,1)} %wait_for.43), channel_id=1, source_target_pairs={{0,12},{4,8},{8,4},{12,0},{16,28},{20,24},{24,20},{28,16},{1,13},{... | collective-permute-start | bytes 4718600 | tf_op jit(solution)/shard_map/ppermute | solution.py:382
  284.3 131.5 %collective-permute-start.18 = (bf16[64,32,384]{2,1,0:T(8,128)(2,1)}, bf16[64,32,384]{2,1,0:T(8,128)(2,1)}, u32[]{:S(2)}, u32[]{:S(2)}) collective-permute-start(bf16[64,32,384]{2,1,0:T(8,128)(2,1)} %wait_for.44), channel_id=1, source_target_pairs={{0,4},{4,0},{8,12},{12,8},{16,20},{20,16},{24,28},{28,24},{1,5},{5... | collective-permute-start | bytes 4718600 | tf_op jit(solution)/shard_map/ppermute | solution.py:382
  319.9 94.0 %collective-permute-start.19 = (bf16[64,32,384]{2,1,0:T(8,128)(2,1)}, bf16[64,32,384]{2,1,0:T(8,128)(2,1)}, u32[]{:S(2)}, u32[]{:S(2)}) collective-permute-start(bf16[64,32,384]{2,1,0:T(8,128)(2,1)} %wait_for.45), channel_id=1, source_target_pairs={{0,16},{4,20},{8,24},{12,28},{16,0},{20,4},{24,8},{28,12},{1,17},{... | collective-permute-start | bytes 4718600 | tf_op jit(solution)/shard_map/ppermute | solution.py:382
  353.9 65.2 %collective-permute-start.20 = (bf16[64,32,384]{2,1,0:T(8,128)(2,1)}, bf16[64,32,384]{2,1,0:T(8,128)(2,1)S(1)}, u32[]{:S(2)}, u32[]{:S(2)}) collective-permute-start(bf16[64,32,384]{2,1,0:T(8,128)(2,1)} %wait_for.46), channel_id=1, source_target_pairs={{0,8},{4,12},{8,0},{12,4},{16,24},{20,28},{24,16},{28,20},{1,9},{5... | collective-permute-start | bytes 4718600 | tf_op jit(solution)/shard_map/ppermute | solution.py:382
  380.1 104.7 %collective-permute-start.21 = (bf16[64,32,384]{2,1,0:T(8,128)(2,1)}, bf16[64,32,384]{2,1,0:T(8,128)(2,1)S(1)}, u32[]{:S(2)}, u32[]{:S(2)}) collective-permute-start(bf16[64,32,384]{2,1,0:T(8,128)(2,1)} %wait_for.48), channel_id=1, source_target_pairs={{0,28},{4,24},{8,20},{12,16},{16,12},{20,8},{24,4},{28,0},{1,29},{... | collective-permute-start | bytes 4718600 | tf_op jit(solution)/shard_map/ppermute | solution.py:382
  384.6 103.1 %collective-permute-start.22 = (bf16[64,32,384]{2,1,0:T(8,128)(2,1)}, bf16[64,32,384]{2,1,0:T(8,128)(2,1)}, u32[]{:S(2)}, u32[]{:S(2)}) collective-permute-start(bf16[64,32,384]{2,1,0:T(8,128)(2,1)} %wait_for.49), channel_id=1, source_target_pairs={{0,24},{4,28},{8,16},{12,20},{16,8},{20,12},{24,0},{28,4},{1,25},{... | collective-permute-start | bytes 4718600 | tf_op jit(solution)/shard_map/ppermute | solution.py:382
  413.9 130.2 %collective-permute-start.27 = (bf16[64,32,384]{2,1,0:T(8,128)(2,1)}, bf16[64,32,384]{2,1,0:T(8,128)(2,1)}, u32[]{:S(2)}, u32[]{:S(2)}) collective-permute-start(bf16[64,32,384]{2,1,0:T(8,128)(2,1)} %wait_for.53), channel_id=1, source_target_pairs={{0,12},{4,8},{8,4},{12,0},{16,28},{20,24},{24,20},{28,16},{1,13},{... | collective-permute-start | bytes 4718600 | tf_op jit(solution)/shard_map/ppermute | solution.py:382
  415.8 103.8 %collective-permute-start.28 = (bf16[64,32,384]{2,1,0:T(8,128)(2,1)}, bf16[64,32,384]{2,1,0:T(8,128)(2,1)}, u32[]{:S(2)}, u32[]{:S(2)}) collective-permute-start(bf16[64,32,384]{2,1,0:T(8,128)(2,1)} %wait_for.54), channel_id=1, source_target_pairs={{0,20},{4,16},{8,28},{12,24},{16,4},{20,0},{24,12},{28,8},{1,21},{... | collective-permute-start | bytes 4718600 | tf_op jit(solution)/shard_map/ppermute | solution.py:382
  482.7 72.0 %collective-permute-start.26 = (bf16[64,32,384]{2,1,0:T(8,128)(2,1)}, bf16[64,32,384]{2,1,0:T(8,128)(2,1)}, u32[]{:S(2)}, u32[]{:S(2)}) collective-permute-start(bf16[64,32,384]{2,1,0:T(8,128)(2,1)} %wait_for.52), channel_id=1, source_target_pairs={{0,4},{4,0},{8,12},{12,8},{16,20},{20,16},{24,28},{28,24},{1,5},{5... | collective-permute-start | bytes 4718600 | tf_op jit(solution)/shard_map/ppermute | solution.py:382
  484.8 2.9 copy-start.12
  484.8 67.1 %collective-permute-start.25 = (f32[1472,128]{1,0:T(8,128)}, f32[1472,128]{1,0:T(8,128)}, u32[]{:S(2)}, u32[]{:S(2)}) collective-permute-start(f32[1472,128]{1,0:T(8,128)} %pad_maximum_fusion), channel_id=1, source_target_pairs={{0,4},{4,0},{8,12},{12,8},{16,20},{20,16},{24,28},{28,24},{1,5},{5... | collective-permute-start | bytes 2261000 | tf_op jit(solution)/shard_map/ppermute | solution.py:382
  487.7 81.3 %collective-permute-start.23 = (bf16[64,32,384]{2,1,0:T(8,128)(2,1)}, bf16[64,32,384]{2,1,0:T(8,128)(2,1)S(1)}, u32[]{:S(2)}, u32[]{:S(2)}) collective-permute-start(bf16[64,32,384]{2,1,0:T(8,128)(2,1)} %get-tuple-element.108), channel_id=1, source_target_pairs={{0,16},{4,20},{8,24},{12,28},{16,0},{20,4},{24,8},{28,12},{1,17},{... | collective-permute-start | bytes 4718600 | tf_op jit(solution)/shard_map/ppermute | solution.py:382
  519.6 55.5 %collective-permute-start.24 = (bf16[64,32,384]{2,1,0:T(8,128)(2,1)}, bf16[64,32,384]{2,1,0:T(8,128)(2,1)S(1)}, u32[]{:S(2)}, u32[]{:S(2)}) collective-permute-start(bf16[64,32,384]{2,1,0:T(8,128)(2,1)} %get-tuple-element.109), channel_id=1, source_target_pairs={{0,8},{4,12},{8,0},{12,4},{16,24},{20,28},{24,16},{28,20},{1,9},{5... | collective-permute-start | bytes 4718600 | tf_op jit(solution)/shard_map/ppermute | solution.py:382
  544.1 7.9 %copy-start.14 = (f32[4,1,320,128]{3,2,1,0:T(8,128)S(1)}, f32[4,1,320,128]{3,2,1,0:T(8,128)}, u32[]{:S(2)}) copy-start(f32[4,1,320,128]{3,2,1,0:T(8,128)} %get-tuple-element.160) | copy-start | bytes 1966084
  565.5 16.1 %collective-permute-start.29 = (f32[512,128]{1,0:T(8,128)}, f32[512,128]{1,0:T(8,128)S(1)}, u32[]{:S(2)}, u32[]{:S(2)}) collective-permute-start(f32[512,128]{1,0:T(8,128)} %get-tuple-element.173), channel_id=1, source_target_pairs={{0,8},{4,12},{8,0},{12,4},{16,24},{20,28},{24,16},{28,20},{1,9},{5... | collective-permute-start | bytes 786440 | tf_op jit(solution)/shard_map/ppermute | solution.py:382
  566.7 14.9 %collective-permute-start.30 = (f32[512,128]{1,0:T(8,128)}, f32[512,128]{1,0:T(8,128)}, u32[]{:S(2)}, u32[]{:S(2)}) collective-permute-start(f32[512,128]{1,0:T(8,128)} %get-tuple-element.172), channel_id=1, source_target_pairs={{0,16},{4,20},{8,24},{12,28},{16,0},{20,4},{24,8},{28,12},{1,17},{... | collective-permute-start | bytes 786440 | tf_op jit(solution)/shard_map/ppermute | solution.py:382
  568.0 13.5 %collective-permute-start.31 = (f32[512,128]{1,0:T(8,128)}, f32[512,128]{1,0:T(8,128)}, u32[]{:S(2)}, u32[]{:S(2)}) collective-permute-start(f32[512,128]{1,0:T(8,128)} %get-tuple-element.171), channel_id=1, source_target_pairs={{0,24},{4,28},{8,16},{12,20},{16,8},{20,12},{24,0},{28,4},{1,25},{... | collective-permute-start | bytes 786440 | tf_op jit(solution)/shard_map/ppermute | solution.py:382
  575.1 7.2 %copy-start.17 = (f32[192,128]{1,0:T(8,128)S(1)}, f32[192,128]{1,0:T(8,128)}, u32[]{:S(2)}) copy-start(f32[192,128]{1,0:T(8,128)} %get-tuple-element.137) | copy-start | bytes 294916
  581.4 4.3 copy-start.19
  581.4 4.3 collective-permute-start.32
  586.4 25.3 %collective-permute-start.36 = (f32[3,128,128]{2,1,0:T(8,128)}, f32[3,128,128]{2,1,0:T(8,128)S(1)}, u32[]{:S(2)}, u32[]{:S(2)}) collective-permute-start(f32[3,128,128]{2,1,0:T(8,128)} %wait_for.60.refs_0_), channel_id=1, source_target_pairs={{0,8},{4,12},{8,0},{12,4},{16,24},{20,28},{24,16},{28,20},{1,9},{5... | collective-permute-start | bytes 589832 | tf_op jit(solution)/shard_map/ppermute | solution.py:382
  587.6 24.1 %collective-permute-start.37 = (f32[3,128,128]{2,1,0:T(8,128)}, f32[3,128,128]{2,1,0:T(8,128)S(1)}, u32[]{:S(2)}, u32[]{:S(2)}) collective-permute-start(f32[3,128,128]{2,1,0:T(8,128)} %wait_for.60.refs_0_), channel_id=1, source_target_pairs={{0,16},{4,20},{8,24},{12,28},{16,0},{20,4},{24,8},{28,12},{1,17},{... | collective-permute-start | bytes 589832 | tf_op jit(solution)/shard_map/ppermute | solution.py:382
  589.0 22.8 %collective-permute-start.38 = (f32[3,128,128]{2,1,0:T(8,128)}, f32[3,128,128]{2,1,0:T(8,128)S(1)}, u32[]{:S(2)}, u32[]{:S(2)}) collective-permute-start(f32[3,128,128]{2,1,0:T(8,128)} %wait_for.60.refs_0_), channel_id=1, source_target_pairs={{0,24},{4,28},{8,16},{12,20},{16,8},{20,12},{24,0},{28,4},{1,25},{... | collective-permute-start | bytes 589832 | tf_op jit(solution)/shard_map/ppermute | solution.py:382
  589.9 6.0 collective-permute-start.33
  591.5 22.4 %collective-permute-start.35 = (f32[192,128]{1,0:T(8,128)}, f32[192,128]{1,0:T(8,128)S(1)}, u32[]{:S(2)}, u32[]{:S(2)}) collective-permute-start(f32[192,128]{1,0:T(8,128)} %get-tuple-element.151.refs_2_), channel_id=1, source_target_pairs={{0,4},{4,0},{8,12},{12,8},{16,20},{20,16},{24,28},{28,24},{1,5},{5... | collective-permute-start | bytes 294920 | tf_op jit(solution)/shard_map/ppermute | solution.py:382
  596.8 2.6 copy-start.13
  596.8 17.1 %collective-permute-start.34 = (f32[320,128]{1,0:T(8,128)S(1)}, f32[320,128]{1,0:T(8,128)S(1)}, u32[]{:S(2)}, u32[]{:S(2)}) collective-permute-start(f32[320,128]{1,0:T(8,128)S(1)} %add.388.refs_2_.refs_0_), channel_id=1, source_target_pairs={{0,2},{1,3},{2,0},{3,1},{4,6},{5,7},{6,4},{7,5},{8,10},{9,11},{10,... | collective-permute-start | bytes 491528 | tf_op jit(solution)/shard_map/ppermute | solution.py:382
  613.8 5.4 collective-permute-start.39
  615.2 4.8 copy-start.1
  (17 other events, 16.9 us)
